TPU v7x, 32 devices: a whole 2x2x4 slice. The times are simulated.
32 devices in a mesh: scen: 2 (over y), orig: 4 (over x, core), dest: 4 (over z).
Axes of the slice: x: 2, y: 2, z: 4, core: 2. Of those that a mesh axis runs over, the one named last changes fastest.
Arguments:
- tile_values: bfloat16 [8, 4, 12, 24, 128, 128], P(('scen', 'orig'), 'dest'), parts along dimension 0, may hold values from -48 to 48
- tile_hours: int32 [8, 4, 12, 24], P(('scen', 'orig'), 'dest'), parts along dimension 0, may hold values from 0 to 167, as said below
- tile_anchor: int32 [8, 4, 12], P(('scen', 'orig'), 'dest'), parts along dimension 0, may hold values from 0 to 7, as said below
- tile_dest: int32 [8, 4, 12], P(('scen', 'orig'), 'dest'), parts along dimension 0, may hold values from 0 to 15, as said below
- tile_live: int32 [8, 4, 12], P(('scen', 'orig'), 'dest'), parts along dimension 0, may hold values from 0 to 24, as said below
- dest_factor_in: float32 [64, 16384], P(None, ('scen', 'dest')), parts along dimension 1, may hold values from -10 to 10
- hour_factor: float32 [64, 336], P(None, 'scen'), parts along dimension 1, may hold values from -10 to 10
Outputs:
- anchor_factor: float32 [64, 8192], P(None, ('scen', 'orig')), parts along dimension 1
- dest_factor: float32 [64, 16384], P(None, ('scen', 'dest')), parts along dimension 1
There are 2 independent parts, one for each index of `scen`. A program takes and returns all parts, laid end to end along the dimension named above; each array names one. Nothing has to cross between parts.
Inputs may be any that keep to these rules, and one draw needn't show every extreme that they name: `tile_hours`: within a tile the hours of its slots are distinct. On each device the pairs (tile_anchor, tile_dest) of its 12 tile slots are distinct. `tile_dest`: see tile_anchor. `tile_live`: live hour slots of a tile come first, and tile slots with live hours come first on each device; loads differ from device to device, and on one device of each scenario all 12 tile slots hold 24 live hour slots.
All inputs are finite; a program needn't handle non-finite values.
Results may differ from a plain program's by a relative error of at most 0.0038.
Values sent between devices are 32-bit elements; how exact they have to be, the bound alone decides.
No kernel may reach another device: no remote copies, remote signals or barrier semaphores. Data moves between devices by JAX's collectives and lax.ppermute only.
A program may use at most 64 MiB of HBM per device.

v0:
```python
import jax
import jax.numpy as jnp
from jax import lax
from jax.sharding import PartitionSpec as P

OB = 8


def gram_of(factor):
    return jnp.dot(
        factor, factor.T, precision=lax.Precision.HIGHEST, preferred_element_type=jnp.float32
    )


def solve_gram(gram, right_side):
    lower_factor = jnp.linalg.cholesky(gram)
    return jax.scipy.linalg.cho_solve((lower_factor, True), right_side)


def hour_scales(live_hours, hour_ids, hour_factor):
    rank_count = hour_factor.shape[0]
    tile_count, slot_count = hour_ids.shape
    chosen = jnp.take(hour_factor, hour_ids.reshape(-1), axis=1).reshape(
        rank_count, tile_count, slot_count
    )
    alive_mask = (
        lax.broadcasted_iota(jnp.int32, (tile_count, slot_count), 1) < live_hours[:, None]
    ).astype(jnp.float32)
    return chosen * alive_mask[None, :, :]


def tile_weights(factor, tile_index, scales, tile_size):
    rank_count = factor.shape[0]
    blocks = factor.reshape(rank_count, factor.shape[1] // tile_size, tile_size)
    picked = jnp.take(blocks, tile_index, axis=1)
    return (picked[:, :, None, :] * scales[:, :, :, None]).astype(jnp.bfloat16)


def place_tiles(tile_terms, tile_index, block_count):
    onehot = (
        tile_index[:, None]
        == lax.broadcasted_iota(jnp.int32, (tile_index.shape[0], block_count), 1)
    ).astype(jnp.float32)
    placed = jnp.einsum("rtc,tb->rbc", tile_terms, onehot, precision=lax.Precision.HIGHEST)
    return placed.reshape(tile_terms.shape[0], block_count * tile_terms.shape[2])


def shards(tile_values, tile_hours, tile_anchor, tile_dest, tile_live, dest_factor_in, hour_factor):
    values = tile_values[0, 0]
    hour_ids = tile_hours[0, 0]
    anchor_ids = tile_anchor[0, 0]
    dest_ids = tile_dest[0, 0]
    live_hours = tile_live[0, 0]
    tile_size = values.shape[-1]
    scales = hour_scales(live_hours, hour_ids, hour_factor)
    hour_gram = gram_of(hour_factor)
    dest_gram = lax.psum(gram_of(dest_factor_in), "dest") * hour_gram
    dest_weights = tile_weights(dest_factor_in, dest_ids, scales, tile_size)
    anchor_terms = jnp.einsum(
        "rtsd,tsod->rto", dest_weights, values, preferred_element_type=jnp.float32
    )
    anchor_part = place_tiles(anchor_terms, anchor_ids, OB)
    anchor_factor = solve_gram(dest_gram, lax.psum(anchor_part, "dest"))
    col_sq = lax.psum(jnp.sum(anchor_factor * anchor_factor, axis=1), "orig")
    col_norm = jnp.sqrt(col_sq + 1e-06)
    anchor_unit = anchor_factor / col_norm[:, None]
    unit_gram = lax.psum(gram_of(anchor_unit), "orig")
    anchor_gram = unit_gram * hour_gram
    anchor_weights = tile_weights(anchor_unit, anchor_ids, scales, tile_size)
    dest_terms = jnp.einsum(
        "rtso,tsod->rtd", anchor_weights, values, preferred_element_type=jnp.float32
    )
    dest_part = place_tiles(dest_terms, dest_ids, dest_factor_in.shape[1] // tile_size)
    dest_factor = solve_gram(anchor_gram, lax.psum(dest_part, "orig"))
    return (anchor_factor, dest_factor)


def solution(mesh):
    placed = (
        P(("scen", "orig"), "dest", None, None, None, None),
        P(("scen", "orig"), "dest", None, None),
        P(("scen", "orig"), "dest", None),
        P(("scen", "orig"), "dest", None),
        P(("scen", "orig"), "dest", None),
        P(None, ("scen", "dest")),
        P(None, "scen"),
    )
    return jax.shard_map(
        shards,
        mesh=mesh,
        in_specs=placed,
        out_specs=(P(None, ("scen", "orig")), P(None, ("scen", "dest"))),
        check_vma=False,
    )
```

profile of v0, /device:TPU:0, one launch (start us, length us, event | category | flops | bytes accessed | tf_op | source)
XLA Modules:
  0.0 136.8 jit_solution(17492109452854740770)
XLA Ops:
  7.2 0.0 copy-start
  7.2 0.0 all-reduce.3.cloned.1.call-start
  7.2 0.7 compare_and_fusion.2
  7.9 0.7 fusion.40
  8.6 0.7 reduce.4
  9.3 0.1 reshape_squeeze.6
  9.4 0.8 fusion.32
  10.2 0.9 copy.32
  11.2 0.0 copy-start.4
  11.2 1.1 gather_fusion.1
  12.3 0.6 gather_fusion
  12.9 0.0 copy-start.2
  12.9 0.1 select_bitcast_fusion.1
  13.0 0.1 select_multiply_fusion
  13.1 6.9 %fusion.8 = f32[64,12,128]{2,0,1:T(8,128)S(1)} fusion(bf16[1,1,12,24,128,128]{5,4,3,2,1,0:T(8,128)(2,1)} %param.8, f32[64,12,24]{0,2,1:T(8,128)S(1)} %select_multiply_fusion, f32[64,12,128]{2,0,1:T(8,128)S(1)} %select_bitcast_fusion.1), kind=kOutput, calls=%fused_computation.13 | convolution fusion | flops 608698368 | bytes 10297344 | tf_op jit(solution)/shard_map/rtsd,tsod->rto/dot_general | solution.py:59
  20.0 0.5 fusion.16
  20.6 0.8 copy.61
  21.3 0.0 all-reduce.3.cloned.1.call-update
  21.3 0.0 all-reduce.5.cloned.1.call-start
  21.4 0.6 fusion.43
  22.0 21.2 %psum.35 = f32[64,64]{0,1:T(8,128)S(1)} all-reduce(f32[64,64]{0,1:T(8,128)S(1)} %fusion.43), channel_id=1, replica_groups=mesh['scen'=2,'orig'=4,'dest'=4] {'dest'}, use_global_device_ids=true, to_apply=%region_0.1 | all-reduce | flops 4096 | bytes 32768 | tf_op jit(solution)/shard_map/psum | solution.py:57
  43.2 0.2 fusion.42
  43.4 0.1 copy.30
  43.5 5.8 %cholesky.44 = f32[64,64]{1,0:T(8,128)S(1)} custom-call(f32[64,64]{1,0:T(8,128)S(1)} %fusion.31), custom_call_target="Cholesky" | custom-call | tf_op jit(solution)/shard_map/jit(cholesky)/cholesky | solution.py:16
  49.4 0.6 compare_reduce_fusion.1
  50.0 0.7 fusion.20
  50.7 4.9 %custom-call.16 = f32[1,64,64]{1,2,0:T(8,128)S(1)} custom-call(f32[1,64,64]{2,1,0:T(8,128)S(1)} %fusion.20), custom_call_target="InvertDiagBlocksLowerTriangular" | custom-call | tf_op jit(solution)/shard_map/jit(_cho_solve)/triangular_solve | solution.py:17
  55.6 4.3 %all-reduce.3.cloned.1.call-done = f32[64,1024]{1,0:T(8,128)} async-done(((f32[64,1024]{1,0:T(8,128)}), f32[64,1024]{1,0:T(8,128)}) %all-reduce.3.cloned.1.call-update) | async-done | bytes 262160 | tf_op jit(solution)/shard_map/psum | solution.py:63
  60.0 1.4 fusion.29
  61.3 0.5 multiply_reduce_fusion
  61.8 5.7 %psum.37 = f32[64]{0:T(128)S(1)} all-reduce(f32[64]{0:T(128)S(1)} %get-tuple-element.5), channel_id=1, replica_groups=mesh['scen'=2,'orig'=4,'dest'=4] {'orig'}, use_global_device_ids=true, to_apply=%region_5.7 | all-reduce | flops 64 | bytes 512 | tf_op jit(solution)/shard_map/psum | solution.py:64
  67.5 0.5 fusion.19
  67.9 0.1 copy_bitcast_fusion.3
  68.0 11.1 %psum.38 = f32[64,64]{0,1:T(8,128)S(1)} all-reduce(f32[64,64]{0,1:T(8,128)S(1)} %fusion.19), channel_id=1, replica_groups=mesh['scen'=2,'orig'=4,'dest'=4] {'orig'}, use_global_device_ids=true, to_apply=%region_6.8 | all-reduce | flops 4096 | bytes 32768 | tf_op jit(solution)/shard_map/psum | solution.py:67
  79.2 0.1 copy.36
  79.3 5.8 %cholesky.55 = f32[64,64]{1,0:T(8,128)S(1)} custom-call(f32[64,64]{1,0:T(8,128)S(1)} %fusion.26), custom_call_target="Cholesky" | custom-call | tf_op jit(solution)/shard_map/jit(cholesky)/cholesky | solution.py:16
  85.2 0.6 gather_fusion.2
  85.8 0.1 select_bitcast_fusion
  85.9 6.9 %fusion.11 = f32[64,12,128]{2,0,1:T(8,128)S(1)} fusion(bf16[1,1,12,24,128,128]{5,4,3,2,1,0:T(8,128)(2,1)} %param.8, f32[64,12,128]{2,0,1:T(8,128)S(1)} %select_bitcast_fusion, f32[64,12,24]{0,2,1:T(8,128)S(1)} %select_multiply_fusion), kind=kOutput, calls=%fused_computation.14 | convolution fusion | flops 608698368 | bytes 10297344 | tf_op jit(solution)/shard_map/rtso,tsod->rtd/dot_general | solution.py:70
  92.8 0.6 fusion.14
  93.4 1.0 copy.60
  94.3 0.0 all-reduce.5.cloned.1.call-update
  94.4 0.7 compare_reduce_fusion
  95.1 0.7 fusion.21
  95.8 4.9 %custom-call.17 = f32[1,64,64]{1,2,0:T(8,128)S(1)} custom-call(f32[1,64,64]{2,1,0:T(8,128)S(1)} %fusion.21), custom_call_target="InvertDiagBlocksLowerTriangular" | custom-call | tf_op jit(solution)/shard_map/jit(_cho_solve)/triangular_solve | solution.py:17
  100.7 26.2 %all-reduce.5.cloned.1.call-done = f32[64,2048]{1,0:T(8,128)} async-done(((f32[64,2048]{1,0:T(8,128)}), f32[64,2048]{1,0:T(8,128)}) %all-reduce.5.cloned.1.call-update) | async-done | bytes 524304 | tf_op jit(solution)/shard_map/psum | solution.py:74
  126.9 1.7 %fusion.24 = f32[64,2048]{1,0:T(8,128)S(1)} fusion(f32[64,2048]{1,0:T(8,128)} %all-reduce.5.cloned.1.call-done, f32[1,64,64]{1,2,0:T(8,128)S(1)} %custom-call.17), kind=kOutput, calls=%fused_computation.36 | convolution fusion | flops 100663296 | bytes 1064960 | tf_op jit(solution)/shard_map/jit(_cho_solve)/triangular_solve | solution.py:17
  128.6 1.4 fusion.22
  (20 shorter events, 0.2 us)
Async XLA Ops:
  7.2 4.0 %copy-start = (f32[64,2048]{1,0:T(8,128)S(1)}, f32[64,2048]{1,0:T(8,128)}, u32[]{:S(2)}) copy-start(f32[64,2048]{1,0:T(8,128)} %param.13) | copy-start | bytes 1572868
  7.2 52.8 %all-reduce.3.cloned.1.call-start = ((), (), s32[]{:S(2)}) async-start(), calls=%async_computation | async-start | bytes 524288 | tf_op jit(solution)/shard_map/psum | solution.py:63
  11.2 8.8 %copy-start.4 = (s32[1,1,12]{2,1,0:T(1,128)S(1)}, s32[1,1,12]{2,1,0:T(1,128)}, u32[]{:S(2)}) copy-start(s32[1,1,12]{2,1,0:T(1,128)} %param.10) | copy-start | bytes 148
  12.9 30.3 %copy-start.2 = (f32[64,168]{1,0:T(8,128)S(1)}, f32[64,168]{1,0:T(8,128)}, u32[]{:S(2)}) copy-start(f32[64,168]{1,0:T(8,128)} %param.14) | copy-start | bytes 129028
  21.3 71.5 %copy-start.3 = (s32[1,1,12]{2,1,0:T(1,128)S(1)}, s32[1,1,12]{2,1,0:T(1,128)}, u32[]{:S(2)}) copy-start(s32[1,1,12]{2,1,0:T(1,128)} %param.11) | copy-start | bytes 148
  21.3 105.6 %all-reduce.5.cloned.1.call-start = ((), (), s32[]{:S(2)}) async-start(), calls=%async_computation.1 | async-start | bytes 1048576 | tf_op jit(solution)/shard_map/psum | solution.py:74
  61.8 66.8 %copy-start.1 = (f32[64,1024]{1,0:T(8,128)}, f32[64,1024]{1,0:T(8,128)S(1)}, u32[]{:S(2)}) copy-start(f32[64,1024]{1,0:T(8,128)S(1)} %get-tuple-element.6) | copy-start | bytes 786436
Sparse Core Ops, SparseCore 0:
  21.5 38.4 all-reduce.2
  94.5 32.3 all-reduce.4
where the time goes:
time: 137 us
  blocking collectives  38 us (28%)
  waiting for transfers between devices  30.6 us (22%)
  other arithmetic  27.6 us (20%)
  matrix products  21 us (15%)
  between operations  14.3 us (10%)
  local copies, waits for them, and re-layouts  5.16 us (4%)
    psum x1, waiting for transfers between devices, shards(): dest_factor = solve_gram(anchor_gram, lax.psum(dest_part, 'orig'))  26.2 us
    psum x1, blocking collectives, shards(): dest_gram = lax.psum(gram_of(dest_factor_in), 'dest') * hour_gram  21.2 us
    another operation x6, other arithmetic, solve_gram(): lower_factor = jnp.linalg.cholesky(gram)  13.1 us
    another operation x4, other arithmetic, solve_gram(): return jax.scipy.linalg.cho_solve((lower_factor, True), right_side)  11.1 us
    psum x1, blocking collectives, shards(): unit_gram = lax.psum(gram_of(anchor_unit), 'orig')  11.1 us
    dot_general x1, matrix products, shards(): jnp.einsum('rtso,tsod->rtd', anchor_weights, values, preferred_element_ty...  6.92 us
    dot_general x1, matrix products, shards(): jnp.einsum('rtsd,tsod->rto', dest_weights, values, preferred_element_type...  6.87 us
    psum x1, blocking collectives, shards(): col_sq = lax.psum(jnp.sum(anchor_factor * anchor_factor, axis=1), 'orig')  5.67 us
  transfers between devices with their start and end apart: 2, of which 2 were waited for; matrix products, arithmetic and copies ran while one was open for 14% of the time, Pallas kernels for 0%

commit v1 on v0

v1 whole, which is shorter than its diff:
```python
import functools

import jax
import jax.numpy as jnp
from jax import lax
from jax.experimental import pallas as pl
from jax.experimental.pallas import tpu as pltpu
from jax.sharding import PartitionSpec as P

OB = 8
F32 = jnp.float32
BF16 = jnp.bfloat16
HIGHEST = lax.Precision.HIGHEST
VMEM = pl.BlockSpec(memory_space=pltpu.VMEM)
HBM = pl.BlockSpec(memory_space=pltpu.HBM)
VMEM_BYTES = 48 << 20


def gram_of(factor):
    return lax.dot_general(
        factor, factor, (((1,), (1,)), ((), ())), precision=HIGHEST, preferred_element_type=F32
    )


def spd_inverse(matrix, panel=8):
    size = matrix.shape[0]
    rows = lax.broadcasted_iota(jnp.int32, matrix.shape, 0)
    cols = lax.broadcasted_iota(jnp.int32, matrix.shape, 1)
    for start in range(0, size, panel):
        columns = [
            jnp.broadcast_to(matrix[:, start + j : start + j + 1], matrix.shape) for j in range(panel)
        ]
        for j in range(panel):
            k = start + j
            column = columns[j]
            inverse_pivot = 1.0 / column[k : k + 1, :]
            row = jnp.where(cols[k : k + 1] == k, 1.0, matrix[k : k + 1, :]) * inverse_pivot
            for later in range(j + 1, panel):
                ahead = columns[later][k : k + 1, :] * inverse_pivot
                columns[later] = jnp.where(rows == k, ahead, columns[later] - column * ahead)
            matrix = jnp.where(rows == k, row, jnp.where(cols == k, 0.0, matrix) - column * row)
    return matrix


def anchor_pass(
    hours, live, anchors, dests, dest_factor, hour_factor, values, message, hour_gram,
    values_buf, dest_buf, hour_buf, hour_rows, hours_s, live_s, anchors_s, dests_s, sems, small_sems,
):
    tiles, slots, tile_size, _ = values_buf.shape
    parts, part_rows, _ = message.shape
    rank = dest_buf.shape[0]
    width = OB * tile_size
    small = [
        (hour_factor, hour_buf), (hours, hours_s), (live, live_s), (anchors, anchors_s),
        (dests, dests_s), (dest_factor, dest_buf),
    ]
    small_copies = [pltpu.make_async_copy(s, d, small_sems.at[i]) for i, (s, d) in enumerate(small)]
    copies = [pltpu.make_async_copy(values.at[t], values_buf.at[t], sems.at[t]) for t in range(tiles)]
    for copy in small_copies + copies:
        copy.start()
    message[:, :, :width] = jnp.zeros((parts, part_rows, width), F32)
    for copy in small_copies:
        copy.wait()
    hour_rows[...] = hour_buf[...].T
    hour_gram[...] = gram_of(hour_buf[...])
    gram = gram_of(dest_buf[...])
    packed = jnp.concatenate([gram[c * part_rows : (c + 1) * part_rows] for c in range(parts)], axis=1)
    message[:, :, width:] = jnp.broadcast_to(packed[None], (parts,) + packed.shape)
    for t in range(tiles):
        dest_at = pl.multiple_of(dests_s[0, 0, t] * tile_size, tile_size)
        anchor_at = pl.multiple_of(anchors_s[0, 0, t] * tile_size, tile_size)
        dest_rows = dest_buf[:, pl.ds(dest_at, tile_size)].T
        weights = []
        for s in range(slots):
            scale = hour_rows[pl.ds(hours_s[0, 0, t, s], 1), :]
            scale = jnp.where(s < live_s[0, 0, t], scale, 0.0)
            weights.append((dest_rows * scale).astype(BF16))
        copies[t].wait()
        tile = jnp.concatenate([values_buf[t, s] for s in range(slots)], axis=1)
        term = jnp.dot(tile, jnp.concatenate(weights, axis=0), preferred_element_type=F32).T
        message[:, :, pl.ds(anchor_at, tile_size)] += term.reshape(parts, part_rows, tile_size)


def dest_gram_inverse(packed, hour_gram, inverse):
    part_rows, width = packed.shape
    rank = hour_gram.shape[0]
    gram = jnp.concatenate([packed[:, c * rank : (c + 1) * rank] for c in range(width // rank)], axis=0)
    inverse[...] = spd_inverse(gram * hour_gram[...])


def dest_pass(
    axis, hours, live, anchors, dests, hour_factor, values, gram_inverse, *refs,
):
    pieces, refs = refs[:-13], refs[-13:]
    (anchor_factor, message, sums, values_buf, hour_buf, hour_rows, hours_s, live_s, anchors_s, dests_s, factor,
     sems, small_sems) = refs
    tiles, slots, tile_size, _ = values_buf.shape
    rank, width = sums.shape
    half = message.shape[2] - rank
    half_tiles = half // tile_size
    small = [
        (hour_factor, hour_buf), (hours, hours_s), (live, live_s), (anchors, anchors_s), (dests, dests_s),
    ]
    small_copies = [pltpu.make_async_copy(s, d, small_sems.at[i]) for i, (s, d) in enumerate(small)]
    copies = [pltpu.make_async_copy(values.at[t], values_buf.at[t], sems.at[t]) for t in range(tiles)]
    for copy in small_copies + copies:
        copy.start()
    me = lax.axis_index(axis)
    part_rows = pieces[0].shape[0]
    for k, piece in enumerate(pieces):
        at = pl.multiple_of(jnp.bitwise_xor(me, k) * part_rows, part_rows)
        sums[pl.ds(at, part_rows), :] = piece[...]
    solved = jnp.dot(gram_inverse[...], sums[...], precision=HIGHEST, preferred_element_type=F32)
    factor[...] = solved
    anchor_factor[...] = solved
    gram = gram_of(solved)
    message[:, :, :half] = jnp.zeros((2, rank, half), F32)
    message[:, :, half:] = jnp.broadcast_to(gram[None], (2, rank, rank))
    for copy in small_copies:
        copy.wait()
    hour_rows[...] = hour_buf[...].T
    for t in range(tiles):
        anchor_at = pl.multiple_of(anchors_s[0, 0, t] * tile_size, tile_size)
        dest = dests_s[0, 0, t]
        tile_factor = factor[:, pl.ds(anchor_at, tile_size)]
        scales = jnp.concatenate(
            [
                jnp.where(s < live_s[0, 0, t], hour_rows[pl.ds(hours_s[0, 0, t, s], 1), :], 0.0)
                for s in range(slots)
            ],
            axis=0,
        ).T
        weights = jnp.concatenate(
            [(tile_factor * scales[:, s : s + 1]).astype(BF16) for s in range(slots)], axis=1
        )
        copies[t].wait()
        tile = values_buf[t].reshape(slots * tile_size, tile_size)
        term = jnp.dot(weights, tile, preferred_element_type=F32)
        dest_at = pl.multiple_of(lax.rem(dest, half_tiles) * tile_size, tile_size)
        message[dest // half_tiles, :, pl.ds(dest_at, tile_size)] += term


def anchor_gram_inverse(gram, hour_gram, inverse):
    total = gram[...]
    rows = lax.broadcasted_iota(jnp.int32, total.shape, 0)
    cols = lax.broadcasted_iota(jnp.int32, total.shape, 1)
    diagonal = jnp.where(rows == cols, total, 0.0)
    row_scale = 1.0 / jnp.sqrt(jnp.sum(diagonal, axis=1, keepdims=True) + 1e-06)
    col_scale = 1.0 / jnp.sqrt(jnp.sum(diagonal, axis=0, keepdims=True) + 1e-06)
    inverse[...] = spd_inverse((total * row_scale * col_scale) * hour_gram[...]) * col_scale


def dest_solve(axis, gram_inverse, mine, other, dest_factor):
    half = mine.shape[1]
    core = lax.rem(lax.axis_index(axis), 2)
    for at, piece in ((core, mine), (1 - core, other)):
        dest_factor[:, pl.ds(pl.multiple_of(at * half, half), half)] = jnp.dot(
            gram_inverse[...], piece[...], precision=HIGHEST, preferred_element_type=F32
        )


def swap(array, axis, count, distance):
    return lax.ppermute(array, axis, [(i, i ^ distance) for i in range(count)])


def tree_sum(terms):
    while len(terms) > 1:
        terms = [terms[i] + terms[i + 1] for i in range(0, len(terms), 2)]
    return terms[0]


def call(body, out_shape, in_specs, scratch_shapes=()):
    return pl.pallas_call(
        body,
        out_shape=out_shape,
        in_specs=in_specs,
        out_specs=jax.tree.map(lambda _: VMEM, out_shape),
        scratch_shapes=list(scratch_shapes),
        compiler_params=pltpu.CompilerParams(vmem_limit_bytes=VMEM_BYTES),
    )


def solution(mesh):
    dest_count = mesh.shape["dest"]
    orig_count = mesh.shape["orig"]

    def shards(hours_of_values, tile_hours, tile_anchor, tile_dest, tile_live, dest_factor_in, hour_factor):
        values = hours_of_values[0, 0]
        tiles, slots, tile_size, _ = values.shape
        rank, dest_width = dest_factor_in.shape
        hour_count = hour_factor.shape[1]
        width = OB * tile_size
        part_rows = rank // dest_count
        half = dest_width // 2
        square = jax.ShapeDtypeStruct((rank, rank), F32)
        index_scratch = [
            pltpu.SMEM((1, 1, tiles, slots), jnp.int32),
            pltpu.SMEM((1, 1, tiles), jnp.int32),
            pltpu.SMEM((1, 1, tiles), jnp.int32),
            pltpu.SMEM((1, 1, tiles), jnp.int32),
        ]
        sent, hour_gram = call(
            anchor_pass,
            (jax.ShapeDtypeStruct((dest_count, part_rows, width + dest_count * rank), F32), square),
            [HBM] * 7,
            [
                pltpu.VMEM(values.shape, BF16),
                pltpu.VMEM((rank, dest_width), F32),
                pltpu.VMEM((rank, hour_count), F32),
                pltpu.VMEM((hour_count, rank), F32),
                *index_scratch,
                pltpu.SemaphoreType.DMA((tiles,)),
                pltpu.SemaphoreType.DMA((6,)),
            ],
        )(tile_hours, tile_live, tile_anchor, tile_dest, dest_factor_in, hour_factor, values)

        me = lax.axis_index("dest")
        parts = [lax.dynamic_index_in_dim(sent, me, 0, keepdims=False)]
        for k in range(1, dest_count):
            part = lax.dynamic_index_in_dim(sent, me ^ k, 0, keepdims=False)
            parts.append(swap(part, "dest", dest_count, k))
        part = tree_sum(parts)
        mine = part[:, :width]
        pieces = [mine] + [swap(mine, "dest", dest_count, k) for k in range(1, dest_count)]
        dest_inverse = call(dest_gram_inverse, square, [VMEM] * 2)(part[:, width:], hour_gram)

        anchor_factor, sent = call(
            functools.partial(dest_pass, "dest"),
            (
                jax.ShapeDtypeStruct((rank, width), F32),
                jax.ShapeDtypeStruct((2, rank, half + rank), F32),
            ),
            [HBM] * 6 + [VMEM] * (1 + dest_count),
            [
                pltpu.VMEM((rank, width), F32),
                pltpu.VMEM(values.shape, BF16),
                pltpu.VMEM((rank, hour_count), F32),
                pltpu.VMEM((hour_count, rank), F32),
                *index_scratch,
                pltpu.VMEM((rank, width), F32),
                pltpu.SemaphoreType.DMA((tiles,)),
                pltpu.SemaphoreType.DMA((5,)),
            ],
        )(tile_hours, tile_live, tile_anchor, tile_dest, hour_factor, values, dest_inverse, *pieces)

        core = lax.axis_index("orig") % 2
        mine = lax.dynamic_index_in_dim(sent, core, 0, keepdims=False)
        theirs = lax.dynamic_index_in_dim(sent, 1 - core, 0, keepdims=False)
        mine = mine + swap(theirs, "orig", orig_count, 1)
        sums, gram = mine[:, :half], mine[:, half:]
        distance = 2
        while distance < orig_count:
            gram = gram + swap(gram, "orig", orig_count, distance)
            sums = sums + swap(sums, "orig", orig_count, distance)
            distance *= 2
        anchor_inverse = call(anchor_gram_inverse, square, [VMEM] * 2)(gram, hour_gram)
        other = swap(sums, "orig", orig_count, 1)
        dest_factor = call(
            functools.partial(dest_solve, "orig"),
            jax.ShapeDtypeStruct((rank, dest_width), F32),
            [VMEM] * 3,
        )(anchor_inverse, sums, other)
        return anchor_factor, dest_factor

    placed = (
        P(("scen", "orig"), "dest", None, None, None, None),
        P(("scen", "orig"), "dest", None, None),
        P(("scen", "orig"), "dest", None),
        P(("scen", "orig"), "dest", None),
        P(("scen", "orig"), "dest", None),
        P(None, ("scen", "dest")),
        P(None, "scen"),
    )
    return jax.shard_map(
        shards,
        mesh=mesh,
        in_specs=placed,
        out_specs=(P(None, ("scen", "orig")), P(None, ("scen", "dest"))),
        check_vma=False,
    )
```

time: 137 us -> 58.6 us (0.43)
  blocking collectives: 38 us -> 0 us
  other arithmetic: 27.6 us -> 0.09 us
  matrix products: 21 us -> 0 us
  Pallas kernels: 0 us -> 19.5 us
  starting transfers between devices: 0.08 us -> 13.7 us
  between operations: 14.3 us -> 0.81 us
  waiting for transfers between devices: 30.6 us -> 19.5 us
    psum x3 -> x0, blocking collectives: 38 us -> none  [the longest x1 21.2 us: shards(): dest_gram = lax.psum(gram_of(dest_factor_in), 'dest') * hour_gram]
    psum x2 -> x0, waiting for transfers between devices: 30.6 us -> none  [the longest x1 26.2 us: shards(): dest_factor = solve_gram(anchor_gram, lax.psum(dest_part, 'orig'))]
    another operation x10 -> x0, other arithmetic: 24.3 us -> none  [the longest x6 13.1 us: solve_gram(): lower_factor = jnp.linalg.cholesky(gram)]
    pallas_call x0 -> x5, Pallas kernels: none -> 19.5 us  [the longest x1 7.69 us: shards(): call(functools.partial(dest_pass, 'dest'), (jax.ShapeDtypeStruct((rank, w...]
    ppermute x0 -> x10, waiting for transfers between devices: none -> 19.5 us  [swap(): return lax.ppermute(array, axis, [(i, i ^ distance) for i in range(count)])]
    dot_general x7 -> x0, matrix products: 16.1 us -> none  [the longest x1 6.92 us: shards(): jnp.einsum('rtso,tsod->rtd', anchor_weights, values, preferred_element_ty...]
    ppermute x0 -> x10, starting transfers between devices: none -> 13.7 us  [swap(): return lax.ppermute(array, axis, [(i, i ^ distance) for i in range(count)])]
    another operation x4 -> x0, matrix products: 4.83 us -> none  [solve_gram(): return jax.scipy.linalg.cho_solve((lower_factor, True), right_side)]
  transfers between devices with their start and end apart: 2 -> 10, of which waited for: 2 -> 7; matrix products, arithmetic and copies ran while one was open for 14% -> 0% of each run, Pallas kernels for 0% -> 5%
where the time goes in v1:
time: 58.6 us; the launch traced here: 58.3 us
  Pallas kernels  19.5 us (33%)
  waiting for transfers between devices  19.5 us (33%)
  starting transfers between devices  13.7 us (23%)
  local copies, waits for them, and re-layouts  4.65 us (8%)
  between operations  0.81 us (1%)
    ppermute x10, waiting for transfers between devices, swap(): return lax.ppermute(array, axis, [(i, i ^ distance) for i in range(count)])  19.5 us
    ppermute x10, starting transfers between devices, swap(): return lax.ppermute(array, axis, [(i, i ^ distance) for i in range(count)])  13.7 us
    pallas_call x1, Pallas kernels, shards(): call(functools.partial(dest_pass, 'dest'), (jax.ShapeDtypeStruct((rank, w...  7.69 us
    pallas_call x1, Pallas kernels, shards(): call(anchor_pass, (jax.ShapeDtypeStruct((dest_count, part_rows, width + d...  7.33 us
    unnamed x19, local copies, waits for them, and re-layouts  4.56 us
    pallas_call x1, Pallas kernels, shards(): call(anchor_gram_inverse, square, [VMEM] * 2)(gram, hour_gram)  1.62 us
    pallas_call x1, Pallas kernels, shards(): call(dest_gram_inverse, square, [VMEM] * 2)(part[:, width:], hour_gram)  1.5 us
    pallas_call x1, Pallas kernels, shards(): call(functools.partial(dest_solve, 'orig'), jax.ShapeDtypeStruct((rank, d...  1.37 us
  transfers between devices with their start and end apart: 10, of which 7 were waited for; matrix products, arithmetic and copies ran while one was open for 0% of the time, Pallas kernels for 5%

profile of v1, /device:TPU:0, one launch (start us, length us, event | category | flops | bytes accessed | tf_op | source)
XLA Modules:
  0.0 58.3 jit_solution(1819256647096666602)
XLA Ops:
  0.6 0.0 copy-start.4
  0.6 0.0 copy-start.8
  0.7 0.0 copy-start.6
  0.7 0.7 %copy.10.hours = s32[1,1,12,24]{3,2,1,0:T(8,128)S(1)} copy(s32[1,1,12,24]{3,1,2,0:T(1,128)} %param.8) | data formatting | bytes 2304 | tf_op args[1]
  1.4 0.0 copy-start
  1.4 1.0 %copy-done = f32[64,2048]{1,0:T(8,128)S(1)} copy-done((f32[64,2048]{1,0:T(8,128)S(1)}, f32[64,2048]{1,0:T(8,128)}, u32[]{:S(2)}) %copy-start) | copy-done | bytes 524312
  2.4 0.0 copy-start.1
  2.4 0.8 %copy-done.1 = f32[64,168]{1,0:T(8,128)S(1)} copy-done((f32[64,168]{1,0:T(8,128)S(1)}, f32[64,168]{1,0:T(8,128)}, u32[]{:S(2)}) %copy-start.1) | copy-done | bytes 43032
  3.3 0.0 copy-start.3
  3.3 0.7 %copy-done.3 = s32[1,1,12]{2,1,0:T(1,128)S(1)} copy-done((s32[1,1,12]{2,1,0:T(1,128)S(1)}, s32[1,1,12]{2,1,0:T(1,128)}, u32[]{:S(2)}) %copy-start.3) | copy-done | bytes 72
  3.9 0.0 copy-start.5
  3.9 0.7 %copy-done.5 = s32[1,1,12]{2,1,0:T(1,128)S(1)} copy-done((s32[1,1,12]{2,1,0:T(1,128)S(1)}, s32[1,1,12]{2,1,0:T(1,128)}, u32[]{:S(2)}) %copy-start.5) | copy-done | bytes 72
  4.6 0.0 copy-start.7
  4.6 0.7 %copy-done.7 = s32[1,1,12]{2,1,0:T(1,128)S(1)} copy-done((s32[1,1,12]{2,1,0:T(1,128)S(1)}, s32[1,1,12]{2,1,0:T(1,128)}, u32[]{:S(2)}) %copy-start.7) | copy-done | bytes 72
  5.2 0.0 copy-start.2
  5.2 7.3 %shard_map.86 = (f32[4,16,1280]{2,1,0:T(8,128)S(1)}, f32[64,64]{1,0:T(8,128)S(1)}) custom-call(s32[1,1,12,24]{3,2,1,0:T(8,128)S(1)} %copy.10.hours, s32[1,1,12]{2,1,0:T(1,128)S(1)} %copy-done.3, s32[1,1,12]{2,1,0:T(1,128)S(1)} %copy-done.5, s32[1,1,12]{2,1,0:T(1,128)S(1)} %copy-done.7, f32[64,2048]{1,0:T(8,128)S(1)} %copy-done, f32[64,168]{1,0:T(8,128)S(1)} %copy-done.1, ...), custom_call_target="tpu_custom_call" | custom-call | tf_op jit(solution)/shard_map/pallas_call | solution.py:202
  12.6 5.1 %collective-permute-start.2 = (f32[16,1280]{1,0:T(8,128)S(1)}, f32[16,1280]{1,0:T(8,128)S(1)}, u32[]{:S(2)}, u32[]{:S(2)}) collective-permute-start(f32[16,1280]{1,0:T(8,128)S(1)} %get-tuple-element.10), channel_id=1, source_target_pairs={{0,3},{1,2},{2,1},{3,0},{4,7},{5,6},{6,5},{7,4},{8,11},{9,10},{10,... | collective-permute-start | bytes 245768 | tf_op jit(solution)/shard_map/ppermute | solution.py:163
  17.7 0.0 collective-permute-start.1
  17.7 0.6 %collective-permute-start = (f32[16,1280]{1,0:T(8,128)S(1)}, f32[16,1280]{1,0:T(8,128)S(1)}, u32[]{:S(2)}, u32[]{:S(2)}) collective-permute-start(f32[16,1280]{1,0:T(8,128)S(1)} %get-tuple-element.12), channel_id=1, source_target_pairs={{0,1},{1,0},{2,3},{3,2},{4,5},{5,4},{6,7},{7,6},{8,9},{9,8},{10,11... | collective-permute-start | bytes 245768 | tf_op jit(solution)/shard_map/ppermute | solution.py:163
  18.4 2.4 %collective-permute-done.2 = f32[16,1280]{1,0:T(8,128)S(1)} collective-permute-done((f32[16,1280]{1,0:T(8,128)S(1)}, f32[16,1280]{1,0:T(8,128)S(1)}, u32[]{:S(2)}, u32[]{:S(2)}) %collective-permute-start.2) | collective-permute-done | bytes 81952 | tf_op jit(solution)/shard_map/ppermute | solution.py:163
  20.7 3.8 %collective-permute-done.1 = f32[16,1280]{1,0:T(8,128)S(1)} collective-permute-done((f32[16,1280]{1,0:T(8,128)S(1)}, f32[16,1280]{1,0:T(8,128)S(1)}, u32[]{:S(2)}, u32[]{:S(2)}) %collective-permute-start.1) | collective-permute-done | bytes 81952 | tf_op jit(solution)/shard_map/ppermute | solution.py:163
  24.6 0.0 collective-permute-done
  24.6 2.7 %collective-permute-start.5 = (f32[16,1024]{1,0:T(8,128)S(1)}, f32[16,1024]{1,0:T(8,128)S(1)}, u32[]{:S(2)}, u32[]{:S(2)}) collective-permute-start(f32[16,1024]{1,0:T(8,128)S(1)} %slice.17.refs_0_), channel_id=1, source_target_pairs={{0,3},{1,2},{2,1},{3,0},{4,7},{5,6},{6,5},{7,4},{8,11},{9,10},{10,... | collective-permute-start | bytes 196616 | tf_op jit(solution)/shard_map/ppermute | solution.py:163
  27.4 0.0 collective-permute-start.4
  27.4 1.7 %collective-permute-start.3 = (f32[16,1024]{1,0:T(8,128)S(1)}, f32[16,1024]{1,0:T(8,128)S(1)}, u32[]{:S(2)}, u32[]{:S(2)}) collective-permute-start(f32[16,1024]{1,0:T(8,128)S(1)} %slice.17.refs_0_), channel_id=1, source_target_pairs={{0,1},{1,0},{2,3},{3,2},{4,5},{5,4},{6,7},{7,6},{8,9},{9,8},{10,11... | collective-permute-start | bytes 196616 | tf_op jit(solution)/shard_map/ppermute | solution.py:163
  29.1 1.5 %shard_map.87.gram_inverse = f32[64,64]{1,0:T(8,128)S(1)} custom-call(f32[16,256]{1,0:T(8,128)S(1)} %slice.16.packed, f32[64,64]{1,0:T(8,128)S(1)} %get-tuple-element.7.hour_gram), custom_call_target="tpu_custom_call" | custom-call | tf_op jit(solution)/shard_map/pallas_call | solution.py:225
  30.6 0.5 collective-permute-done.5.refs_3_
  31.1 2.2 %collective-permute-done.4.refs_2_ = f32[16,1024]{1,0:T(8,128)S(1)} collective-permute-done((f32[16,1024]{1,0:T(8,128)S(1)}, f32[16,1024]{1,0:T(8,128)S(1)}, u32[]{:S(2)}, u32[]{:S(2)}) %collective-permute-start.4) | collective-permute-done | bytes 65568 | tf_op jit(solution)/shard_map/ppermute | solution.py:163
  33.3 0.0 collective-permute-done.3.refs_1_
  33.3 0.0 copy-done.4
  33.3 0.0 copy-done.8
  33.3 0.0 copy-done.6
  33.3 0.0 copy-done.2
  33.3 7.7 %shard_map.88 = (f32[64,1024]{1,0:T(8,128)}, f32[2,64,1088]{2,1,0:T(8,128)S(1)}) custom-call(s32[1,1,12,24]{3,2,1,0:T(8,128)S(1)} %copy.10.hours, s32[1,1,12]{2,1,0:T(1,128)S(1)} %copy-done.4, s32[1,1,12]{2,1,0:T(1,128)S(1)} %copy-done.6, s32[1,1,12]{2,1,0:T(1,128)S(1)} %copy-done.8, f32[64,168]{1,0:T(8,128)S(1)} %copy-done.2, ...), custom_call_target="tpu_custom_call" | custom-call | tf_op jit(solution)/shard_map/pallas_call | solution.py:227
  41.1 0.1 collective-permute-start.6
  41.1 1.6 %collective-permute-done.6 = f32[64,1088]{1,0:T(8,128)S(1)} collective-permute-done((f32[64,1088]{1,0:T(8,128)S(1)}, f32[64,1088]{1,0:T(8,128)S(1)}, u32[]{:S(2)}, u32[]{:S(2)}) %collective-permute-start.6) | collective-permute-done | bytes 278560 | tf_op jit(solution)/shard_map/ppermute | solution.py:163
  42.8 1.7 %collective-permute-start.8 = (f32[64,1024]{1,0:T(8,128)S(1)}, f32[64,1024]{1,0:T(8,128)S(1)}, u32[]{:S(2)}, u32[]{:S(2)}) collective-permute-start(f32[64,1024]{1,0:T(8,128)S(1)} %slice.19), channel_id=1, source_target_pairs={{0,8},{4,12},{8,0},{12,4},{1,9},{5,13},{9,1},{13,5},{2,10},{6,14},... | collective-permute-start | bytes 786440 | tf_op jit(solution)/shard_map/ppermute | solution.py:163
  44.5 6.7 %collective-permute-done.8 = f32[64,1024]{1,0:T(8,128)S(1)} collective-permute-done((f32[64,1024]{1,0:T(8,128)S(1)}, f32[64,1024]{1,0:T(8,128)S(1)}, u32[]{:S(2)}, u32[]{:S(2)}) %collective-permute-start.8) | collective-permute-done | bytes 262176 | tf_op jit(solution)/shard_map/ppermute | solution.py:163
  51.2 0.1 collective-permute-start.9
  51.3 1.7 %collective-permute-start.7 = (f32[64,64]{1,0:T(8,128)S(1)}, f32[64,64]{1,0:T(8,128)S(1)}, u32[]{:S(2)}, u32[]{:S(2)}) collective-permute-start(f32[64,64]{1,0:T(8,128)S(1)} %slice.18), channel_id=1, source_target_pairs={{0,8},{4,12},{8,0},{12,4},{1,9},{5,13},{9,1},{13,5},{2,10},{6,14},... | collective-permute-start | bytes 49160 | tf_op jit(solution)/shard_map/ppermute | solution.py:163
  53.0 2.3 %collective-permute-done.7 = f32[64,64]{1,0:T(8,128)S(1)} collective-permute-done((f32[64,64]{1,0:T(8,128)S(1)}, f32[64,64]{1,0:T(8,128)S(1)}, u32[]{:S(2)}, u32[]{:S(2)}) %collective-permute-start.7) | collective-permute-done | bytes 16416 | tf_op jit(solution)/shard_map/ppermute | solution.py:163
  55.3 1.6 %shard_map.89.gram_inverse = f32[64,64]{1,0:T(8,128)S(1)} custom-call(f32[64,64]{1,0:T(8,128)S(1)} %slice_add_fusion.gram, f32[64,64]{1,0:T(8,128)S(1)} %get-tuple-element.7.hour_gram), custom_call_target="tpu_custom_call" | custom-call | tf_op jit(solution)/shard_map/pallas_call | solution.py:256
  56.9 0.0 collective-permute-done.9.other
  56.9 1.4 %shard_map.90 = f32[64,2048]{1,0:T(8,128)} custom-call(f32[64,64]{1,0:T(8,128)S(1)} %shard_map.89.gram_inverse, f32[64,1024]{1,0:T(8,128)S(1)} %slice_add_fusion.1.mine, f32[64,1024]{1,0:T(8,128)S(1)} %collective-permute-done.9.other), custom_call_target="tpu_custom_call" | custom-call | tf_op jit(solution)/shard_map/pallas_call | solution.py:258
  (10 shorter events, 0.2 us)
Async XLA Ops:
  0.6 32.7 %copy-start.4 = (s32[1,1,12]{2,1,0:T(1,128)S(1)}, s32[1,1,12]{2,1,0:T(1,128)}, u32[]{:S(2)}) copy-start(s32[1,1,12]{2,1,0:T(1,128)} %live.3) | copy-start | bytes 148
  0.6 32.7 %copy-start.8 = (s32[1,1,12]{2,1,0:T(1,128)S(1)}, s32[1,1,12]{2,1,0:T(1,128)}, u32[]{:S(2)}) copy-start(s32[1,1,12]{2,1,0:T(1,128)} %dests.3) | copy-start | bytes 148
  0.7 32.7 %copy-start.6 = (s32[1,1,12]{2,1,0:T(1,128)S(1)}, s32[1,1,12]{2,1,0:T(1,128)}, u32[]{:S(2)}) copy-start(s32[1,1,12]{2,1,0:T(1,128)} %anchors.3) | copy-start | bytes 148
  1.4 1.0 %copy-start = (f32[64,2048]{1,0:T(8,128)S(1)}, f32[64,2048]{1,0:T(8,128)}, u32[]{:S(2)}) copy-start(f32[64,2048]{1,0:T(8,128)} %dest_factor.1) | copy-start | bytes 1572868
  2.4 0.8 %copy-start.1 = (f32[64,168]{1,0:T(8,128)S(1)}, f32[64,168]{1,0:T(8,128)}, u32[]{:S(2)}) copy-start(f32[64,168]{1,0:T(8,128)} %hour_factor.3) | copy-start | bytes 129028
  3.3 0.7 %copy-start.3 = (s32[1,1,12]{2,1,0:T(1,128)S(1)}, s32[1,1,12]{2,1,0:T(1,128)}, u32[]{:S(2)}) copy-start(s32[1,1,12]{2,1,0:T(1,128)} %live.3) | copy-start | bytes 148
  3.9 0.7 %copy-start.5 = (s32[1,1,12]{2,1,0:T(1,128)S(1)}, s32[1,1,12]{2,1,0:T(1,128)}, u32[]{:S(2)}) copy-start(s32[1,1,12]{2,1,0:T(1,128)} %anchors.3) | copy-start | bytes 148
  4.6 0.7 %copy-start.7 = (s32[1,1,12]{2,1,0:T(1,128)S(1)}, s32[1,1,12]{2,1,0:T(1,128)}, u32[]{:S(2)}) copy-start(s32[1,1,12]{2,1,0:T(1,128)} %dests.3) | copy-start | bytes 148
  5.2 28.1 %copy-start.2 = (f32[64,168]{1,0:T(8,128)S(1)}, f32[64,168]{1,0:T(8,128)}, u32[]{:S(2)}) copy-start(f32[64,168]{1,0:T(8,128)} %hour_factor.3) | copy-start | bytes 129028
  12.6 8.1 %collective-permute-start.2 = (f32[16,1280]{1,0:T(8,128)S(1)}, f32[16,1280]{1,0:T(8,128)S(1)}, u32[]{:S(2)}, u32[]{:S(2)}) collective-permute-start(f32[16,1280]{1,0:T(8,128)S(1)} %get-tuple-element.10), channel_id=1, source_target_pairs={{0,3},{1,2},{2,1},{3,0},{4,7},{5,6},{6,5},{7,4},{8,11},{9,10},{10,... | collective-permute-start | bytes 245768 | tf_op jit(solution)/shard_map/ppermute | solution.py:163
  17.7 6.9 %collective-permute-start.1 = (f32[16,1280]{1,0:T(8,128)S(1)}, f32[16,1280]{1,0:T(8,128)S(1)}, u32[]{:S(2)}, u32[]{:S(2)}) collective-permute-start(f32[16,1280]{1,0:T(8,128)S(1)} %get-tuple-element.11), channel_id=1, source_target_pairs={{0,2},{1,3},{2,0},{3,1},{4,6},{5,7},{6,4},{7,5},{8,10},{9,11},{10,... | collective-permute-start | bytes 245768 | tf_op jit(solution)/shard_map/ppermute | solution.py:163
  17.7 6.9 %collective-permute-start = (f32[16,1280]{1,0:T(8,128)S(1)}, f32[16,1280]{1,0:T(8,128)S(1)}, u32[]{:S(2)}, u32[]{:S(2)}) collective-permute-start(f32[16,1280]{1,0:T(8,128)S(1)} %get-tuple-element.12), channel_id=1, source_target_pairs={{0,1},{1,0},{2,3},{3,2},{4,5},{5,4},{6,7},{7,6},{8,9},{9,8},{10,11... | collective-permute-start | bytes 245768 | tf_op jit(solution)/shard_map/ppermute | solution.py:163
  24.6 6.5 %collective-permute-start.5 = (f32[16,1024]{1,0:T(8,128)S(1)}, f32[16,1024]{1,0:T(8,128)S(1)}, u32[]{:S(2)}, u32[]{:S(2)}) collective-permute-start(f32[16,1024]{1,0:T(8,128)S(1)} %slice.17.refs_0_), channel_id=1, source_target_pairs={{0,3},{1,2},{2,1},{3,0},{4,7},{5,6},{6,5},{7,4},{8,11},{9,10},{10,... | collective-permute-start | bytes 196616 | tf_op jit(solution)/shard_map/ppermute | solution.py:163
  27.4 5.9 %collective-permute-start.4 = (f32[16,1024]{1,0:T(8,128)S(1)}, f32[16,1024]{1,0:T(8,128)S(1)}, u32[]{:S(2)}, u32[]{:S(2)}) collective-permute-start(f32[16,1024]{1,0:T(8,128)S(1)} %slice.17.refs_0_), channel_id=1, source_target_pairs={{0,2},{1,3},{2,0},{3,1},{4,6},{5,7},{6,4},{7,5},{8,10},{9,11},{10,... | collective-permute-start | bytes 196616 | tf_op jit(solution)/shard_map/ppermute | solution.py:163
  27.4 5.9 %collective-permute-start.3 = (f32[16,1024]{1,0:T(8,128)S(1)}, f32[16,1024]{1,0:T(8,128)S(1)}, u32[]{:S(2)}, u32[]{:S(2)}) collective-permute-start(f32[16,1024]{1,0:T(8,128)S(1)} %slice.17.refs_0_), channel_id=1, source_target_pairs={{0,1},{1,0},{2,3},{3,2},{4,5},{5,4},{6,7},{7,6},{8,9},{9,8},{10,11... | collective-permute-start | bytes 196616 | tf_op jit(solution)/shard_map/ppermute | solution.py:163
  41.1 1.6 %collective-permute-start.6 = (f32[64,1088]{1,0:T(8,128)S(1)}, f32[64,1088]{1,0:T(8,128)S(1)}, u32[]{:S(2)}, u32[]{:S(2)}) collective-permute-start(f32[64,1088]{1,0:T(8,128)S(1)} %dynamic-slice_bitcast_fusion), channel_id=1, source_target_pairs={{0,4},{4,0},{8,12},{12,8},{1,5},{5,1},{9,13},{13,9},{2,6},{6,2},{1... | collective-permute-start | bytes 835592 | tf_op jit(solution)/shard_map/ppermute | solution.py:163
  42.8 8.4 %collective-permute-start.8 = (f32[64,1024]{1,0:T(8,128)S(1)}, f32[64,1024]{1,0:T(8,128)S(1)}, u32[]{:S(2)}, u32[]{:S(2)}) collective-permute-start(f32[64,1024]{1,0:T(8,128)S(1)} %slice.19), channel_id=1, source_target_pairs={{0,8},{4,12},{8,0},{12,4},{1,9},{5,13},{9,1},{13,5},{2,10},{6,14},... | collective-permute-start | bytes 786440 | tf_op jit(solution)/shard_map/ppermute | solution.py:163
  51.2 5.7 %collective-permute-start.9 = (f32[64,1024]{1,0:T(8,128)S(1)}, f32[64,1024]{1,0:T(8,128)S(1)}, u32[]{:S(2)}, u32[]{:S(2)}) collective-permute-start(f32[64,1024]{1,0:T(8,128)S(1)} %slice_add_fusion.1.mine), channel_id=1, source_target_pairs={{0,4},{4,0},{8,12},{12,8},{1,5},{5,1},{9,13},{13,9},{2,6},{6,2},{1... | collective-permute-start | bytes 786440 | tf_op jit(solution)/shard_map/ppermute | solution.py:163
  51.3 4.0 %collective-permute-start.7 = (f32[64,64]{1,0:T(8,128)S(1)}, f32[64,64]{1,0:T(8,128)S(1)}, u32[]{:S(2)}, u32[]{:S(2)}) collective-permute-start(f32[64,64]{1,0:T(8,128)S(1)} %slice.18), channel_id=1, source_target_pairs={{0,8},{4,12},{8,0},{12,4},{1,9},{5,13},{9,1},{13,5},{2,10},{6,14},... | collective-permute-start | bytes 49160 | tf_op jit(solution)/shard_map/ppermute | solution.py:163

commit v2 on v1

--- a/solution.py
+++ b/solution.py
@@ -72,7 +72,7 @@
         dest_rows = dest_buf[:, pl.ds(dest_at, tile_size)].T
         weights = []
         for s in range(slots):
-            scale = hour_rows[pl.ds(hours_s[0, 0, t, s], 1), :]
+            scale = hour_rows[pl.ds(hours_s[t, 0, s], 1), :]
             scale = jnp.where(s < live_s[0, 0, t], scale, 0.0)
             weights.append((dest_rows * scale).astype(BF16))
         copies[t].wait()
@@ -125,7 +125,7 @@
         tile_factor = factor[:, pl.ds(anchor_at, tile_size)]
         scales = jnp.concatenate(
             [
-                jnp.where(s < live_s[0, 0, t], hour_rows[pl.ds(hours_s[0, 0, t, s], 1), :], 0.0)
+                jnp.where(s < live_s[0, 0, t], hour_rows[pl.ds(hours_s[t, 0, s], 1), :], 0.0)
                 for s in range(slots)
             ],
             axis=0,
@@ -169,6 +169,10 @@
     return terms[0]
 
 
+def in_hbm(array):
+    return pltpu.with_memory_space_constraint(array, pltpu.HBM)
+
+
 def call(body, out_shape, in_specs, scratch_shapes=()):
     return pl.pallas_call(
         body,
@@ -194,11 +198,14 @@
         half = dest_width // 2
         square = jax.ShapeDtypeStruct((rank, rank), F32)
         index_scratch = [
-            pltpu.SMEM((1, 1, tiles, slots), jnp.int32),
+            pltpu.SMEM((tiles, 1, slots), jnp.int32),
             pltpu.SMEM((1, 1, tiles), jnp.int32),
             pltpu.SMEM((1, 1, tiles), jnp.int32),
             pltpu.SMEM((1, 1, tiles), jnp.int32),
         ]
+        indices = [in_hbm(tile_hours.reshape(tiles, 1, slots))]
+        indices += [in_hbm(index) for index in (tile_live, tile_anchor, tile_dest)]
+        values, hour_factor = in_hbm(values), in_hbm(hour_factor)
         sent, hour_gram = call(
             anchor_pass,
             (jax.ShapeDtypeStruct((dest_count, part_rows, width + dest_count * rank), F32), square),
@@ -212,7 +219,7 @@
                 pltpu.SemaphoreType.DMA((tiles,)),
                 pltpu.SemaphoreType.DMA((6,)),
             ],
-        )(tile_hours, tile_live, tile_anchor, tile_dest, dest_factor_in, hour_factor, values)
+        )(*indices, in_hbm(dest_factor_in), hour_factor, values)
 
         me = lax.axis_index("dest")
         parts = [lax.dynamic_index_in_dim(sent, me, 0, keepdims=False)]
@@ -241,18 +248,17 @@
                 pltpu.SemaphoreType.DMA((tiles,)),
                 pltpu.SemaphoreType.DMA((5,)),
             ],
-        )(tile_hours, tile_live, tile_anchor, tile_dest, hour_factor, values, dest_inverse, *pieces)
+        )(*indices, hour_factor, values, dest_inverse, *pieces)
 
         core = lax.axis_index("orig") % 2
         mine = lax.dynamic_index_in_dim(sent, core, 0, keepdims=False)
         theirs = lax.dynamic_index_in_dim(sent, 1 - core, 0, keepdims=False)
         mine = mine + swap(theirs, "orig", orig_count, 1)
-        sums, gram = mine[:, :half], mine[:, half:]
         distance = 2
         while distance < orig_count:
-            gram = gram + swap(gram, "orig", orig_count, distance)
-            sums = sums + swap(sums, "orig", orig_count, distance)
+            mine = mine + swap(mine, "orig", orig_count, distance)
             distance *= 2
+        sums, gram = mine[:, :half], mine[:, half:]
         anchor_inverse = call(anchor_gram_inverse, square, [VMEM] * 2)(gram, hour_gram)
         other = swap(sums, "orig", orig_count, 1)
         dest_factor = call(

time: 58.6 us -> 55.1 us (0.940)
  local copies, waits for them, and re-layouts: 4.65 us -> 0.09 us
  Pallas kernels: 19.5 us -> 24 us
  waiting for transfers between devices: 19.5 us -> 17.9 us
  starting transfers between devices: 13.7 us -> 12.1 us
    unnamed x19 -> x0, local copies, waits for them, and re-layouts: 4.56 us -> none
    pallas_call x1, Pallas kernels: 7.33 us -> 10.2 us  [shards(): call(anchor_pass, (jax.ShapeDtypeStruct((dest_count, part_rows, width + d...]
    ppermute x10 -> x9, starting transfers between devices: 13.7 us -> 12.1 us  [swap(): return lax.ppermute(array, axis, [(i, i ^ distance) for i in range(count)])]
    pallas_call x1, Pallas kernels: 7.69 us -> 9.31 us  [shards(): call(functools.partial(dest_pass, 'dest'), (jax.ShapeDtypeStruct((rank, w...]
    ppermute x10 -> x9, waiting for transfers between devices: 19.5 us -> 17.9 us  [swap(): return lax.ppermute(array, axis, [(i, i ^ distance) for i in range(count)])]
  transfers between devices with their start and end apart: 10 -> 9, of which waited for: 7 -> 6; matrix products, arithmetic and copies ran while one was open for 0% -> 0% of each run, Pallas kernels for 5% -> 6%
where the time goes in v2:
time: 55.1 us; the launch traced here: 54.9 us
  Pallas kernels  24 us (44%)
  waiting for transfers between devices  17.9 us (32%)
  starting transfers between devices  12.1 us (22%)
  between operations  0.77 us (1%)
    ppermute x9, waiting for transfers between devices, swap(): return lax.ppermute(array, axis, [(i, i ^ distance) for i in range(count)])  17.9 us
    ppermute x9, starting transfers between devices, swap(): return lax.ppermute(array, axis, [(i, i ^ distance) for i in range(count)])  12.1 us
    pallas_call x1, Pallas kernels, shards(): call(anchor_pass, (jax.ShapeDtypeStruct((dest_count, part_rows, width + d...  10.2 us
    pallas_call x1, Pallas kernels, shards(): call(functools.partial(dest_pass, 'dest'), (jax.ShapeDtypeStruct((rank, w...  9.31 us
    pallas_call x1, Pallas kernels, shards(): call(anchor_gram_inverse, square, [VMEM] * 2)(gram, hour_gram)  1.62 us
    pallas_call x1, Pallas kernels, shards(): call(dest_gram_inverse, square, [VMEM] * 2)(part[:, width:], hour_gram)  1.5 us
    pallas_call x1, Pallas kernels, shards(): call(functools.partial(dest_solve, 'orig'), jax.ShapeDtypeStruct((rank, d...  1.36 us
  transfers between devices with their start and end apart: 9, of which 6 were waited for; matrix products, arithmetic and copies ran while one was open for 0% of the time, Pallas kernels for 6%

profile of v2, /device:TPU:0, one launch (start us, length us, event | category | flops | bytes accessed | tf_op | source)
XLA Modules:
  0.0 54.9 jit_solution(12351396923130666091)
XLA Ops:
  0.7 10.2 %shard_map.86 = (f32[4,16,1280]{2,1,0:T(8,128)S(1)}, f32[64,64]{1,0:T(8,128)S(1)}) custom-call(s32[12,1,24]{2,1,0:T(1,128)} %bitcast.18, s32[1,1,12]{2,1,0:T(1,128)} %live.3, s32[1,1,12]{2,1,0:T(1,128)} %anchors.3, s32[1,1,12]{2,1,0:T(1,128)} %dests.3, f32[64,2048]{1,0:T(8,128)} %dest_factor.1, f32[64,168]{1,0:T(8,128)} %hour_factor.3, ...), custom_call_target="tpu_custom_call" | custom-call | tf_op jit(solution)/shard_map/pallas_call | solution.py:209
  10.9 5.1 %collective-permute-start.2 = (f32[16,1280]{1,0:T(8,128)S(1)}, f32[16,1280]{1,0:T(8,128)S(1)}, u32[]{:S(2)}, u32[]{:S(2)}) collective-permute-start(f32[16,1280]{1,0:T(8,128)S(1)} %get-tuple-element.10), channel_id=1, source_target_pairs={{0,3},{1,2},{2,1},{3,0},{4,7},{5,6},{6,5},{7,4},{8,11},{9,10},{10,... | collective-permute-start | bytes 245768 | tf_op jit(solution)/shard_map/ppermute | solution.py:163
  16.0 0.0 collective-permute-start.1
  16.0 0.6 %collective-permute-start = (f32[16,1280]{1,0:T(8,128)S(1)}, f32[16,1280]{1,0:T(8,128)S(1)}, u32[]{:S(2)}, u32[]{:S(2)}) collective-permute-start(f32[16,1280]{1,0:T(8,128)S(1)} %get-tuple-element.12), channel_id=1, source_target_pairs={{0,1},{1,0},{2,3},{3,2},{4,5},{5,4},{6,7},{7,6},{8,9},{9,8},{10,11... | collective-permute-start | bytes 245768 | tf_op jit(solution)/shard_map/ppermute | solution.py:163
  16.7 2.4 %collective-permute-done.2 = f32[16,1280]{1,0:T(8,128)S(1)} collective-permute-done((f32[16,1280]{1,0:T(8,128)S(1)}, f32[16,1280]{1,0:T(8,128)S(1)}, u32[]{:S(2)}, u32[]{:S(2)}) %collective-permute-start.2) | collective-permute-done | bytes 81952 | tf_op jit(solution)/shard_map/ppermute | solution.py:163
  19.1 3.8 %collective-permute-done.1 = f32[16,1280]{1,0:T(8,128)S(1)} collective-permute-done((f32[16,1280]{1,0:T(8,128)S(1)}, f32[16,1280]{1,0:T(8,128)S(1)}, u32[]{:S(2)}, u32[]{:S(2)}) %collective-permute-start.1) | collective-permute-done | bytes 81952 | tf_op jit(solution)/shard_map/ppermute | solution.py:163
  22.9 0.0 collective-permute-done
  22.9 2.8 %collective-permute-start.5 = (f32[16,1024]{1,0:T(8,128)S(1)}, f32[16,1024]{1,0:T(8,128)S(1)}, u32[]{:S(2)}, u32[]{:S(2)}) collective-permute-start(f32[16,1024]{1,0:T(8,128)S(1)} %slice.17.refs_0_), channel_id=1, source_target_pairs={{0,3},{1,2},{2,1},{3,0},{4,7},{5,6},{6,5},{7,4},{8,11},{9,10},{10,... | collective-permute-start | bytes 196616 | tf_op jit(solution)/shard_map/ppermute | solution.py:163
  25.7 0.0 collective-permute-start.4
  25.7 1.7 %collective-permute-start.3 = (f32[16,1024]{1,0:T(8,128)S(1)}, f32[16,1024]{1,0:T(8,128)S(1)}, u32[]{:S(2)}, u32[]{:S(2)}) collective-permute-start(f32[16,1024]{1,0:T(8,128)S(1)} %slice.17.refs_0_), channel_id=1, source_target_pairs={{0,1},{1,0},{2,3},{3,2},{4,5},{5,4},{6,7},{7,6},{8,9},{9,8},{10,11... | collective-permute-start | bytes 196616 | tf_op jit(solution)/shard_map/ppermute | solution.py:163
  27.4 1.5 %shard_map.87.gram_inverse = f32[64,64]{1,0:T(8,128)S(1)} custom-call(f32[16,256]{1,0:T(8,128)S(1)} %slice.16.packed, f32[64,64]{1,0:T(8,128)S(1)} %get-tuple-element.7.hour_gram), custom_call_target="tpu_custom_call" | custom-call | tf_op jit(solution)/shard_map/pallas_call | solution.py:232
  28.9 0.5 collective-permute-done.5.refs_3_
  29.4 2.2 %collective-permute-done.4.refs_2_ = f32[16,1024]{1,0:T(8,128)S(1)} collective-permute-done((f32[16,1024]{1,0:T(8,128)S(1)}, f32[16,1024]{1,0:T(8,128)S(1)}, u32[]{:S(2)}, u32[]{:S(2)}) %collective-permute-start.4) | collective-permute-done | bytes 65568 | tf_op jit(solution)/shard_map/ppermute | solution.py:163
  31.6 0.0 collective-permute-done.3.refs_1_
  31.6 9.3 %shard_map.88 = (f32[64,1024]{1,0:T(8,128)}, f32[2,64,1088]{2,1,0:T(8,128)S(1)}) custom-call(s32[12,1,24]{2,1,0:T(1,128)} %bitcast.19, s32[1,1,12]{2,1,0:T(1,128)} %live.3, s32[1,1,12]{2,1,0:T(1,128)} %anchors.3, s32[1,1,12]{2,1,0:T(1,128)} %dests.3, f32[64,168]{1,0:T(8,128)} %hour_factor.3, bf16[12,24,128,128]{3,2,1,0:T(8,128)(2,1)} %bitcast.17, ...), custom_call_target="tpu_custom_call" | custom-call | tf_op jit(solution)/shard_map/pallas_call | solution.py:234
  41.0 0.1 collective-permute-start.6
  41.1 1.6 %collective-permute-done.6 = f32[64,1088]{1,0:T(8,128)S(1)} collective-permute-done((f32[64,1088]{1,0:T(8,128)S(1)}, f32[64,1088]{1,0:T(8,128)S(1)}, u32[]{:S(2)}, u32[]{:S(2)}) %collective-permute-start.6) | collective-permute-done | bytes 278560 | tf_op jit(solution)/shard_map/ppermute | solution.py:163
  42.7 1.7 %collective-permute-start.7 = (f32[64,1088]{1,0:T(8,128)S(1)}, f32[64,1088]{1,0:T(8,128)S(1)}, u32[]{:S(2)}, u32[]{:S(2)}) collective-permute-start(f32[64,1088]{1,0:T(8,128)S(1)} %bitcast_add_fusion), channel_id=1, source_target_pairs={{0,8},{4,12},{8,0},{12,4},{1,9},{5,13},{9,1},{13,5},{2,10},{6,14},... | collective-permute-start | bytes 835592 | tf_op jit(solution)/shard_map/ppermute | solution.py:163
  44.4 7.4 %collective-permute-done.7 = f32[64,1088]{1,0:T(8,128)S(1)} collective-permute-done((f32[64,1088]{1,0:T(8,128)S(1)}, f32[64,1088]{1,0:T(8,128)S(1)}, u32[]{:S(2)}, u32[]{:S(2)}) %collective-permute-start.7) | collective-permute-done | bytes 278560 | tf_op jit(solution)/shard_map/ppermute | solution.py:163
  51.8 0.1 collective-permute-start.8
  51.9 1.6 %shard_map.89.gram_inverse = f32[64,64]{1,0:T(8,128)S(1)} custom-call(f32[64,64]{1,0:T(8,128)S(1)} %slice.18.gram, f32[64,64]{1,0:T(8,128)S(1)} %get-tuple-element.7.hour_gram), custom_call_target="tpu_custom_call" | custom-call | tf_op jit(solution)/shard_map/pallas_call | solution.py:262
  53.5 0.0 collective-permute-done.8.other
  53.6 1.4 %shard_map.90 = f32[64,2048]{1,0:T(8,128)} custom-call(f32[64,64]{1,0:T(8,128)S(1)} %shard_map.89.gram_inverse, f32[64,1024]{1,0:T(8,128)S(1)} %slice.19.mine, f32[64,1024]{1,0:T(8,128)S(1)} %collective-permute-done.8.other), custom_call_target="tpu_custom_call" | custom-call | tf_op jit(solution)/shard_map/pallas_call | solution.py:264
  (9 shorter events, 0.2 us)
Async XLA Ops:
  10.9 8.1 %collective-permute-start.2 = (f32[16,1280]{1,0:T(8,128)S(1)}, f32[16,1280]{1,0:T(8,128)S(1)}, u32[]{:S(2)}, u32[]{:S(2)}) collective-permute-start(f32[16,1280]{1,0:T(8,128)S(1)} %get-tuple-element.10), channel_id=1, source_target_pairs={{0,3},{1,2},{2,1},{3,0},{4,7},{5,6},{6,5},{7,4},{8,11},{9,10},{10,... | collective-permute-start | bytes 245768 | tf_op jit(solution)/shard_map/ppermute | solution.py:163
  16.0 6.9 %collective-permute-start.1 = (f32[16,1280]{1,0:T(8,128)S(1)}, f32[16,1280]{1,0:T(8,128)S(1)}, u32[]{:S(2)}, u32[]{:S(2)}) collective-permute-start(f32[16,1280]{1,0:T(8,128)S(1)} %get-tuple-element.11), channel_id=1, source_target_pairs={{0,2},{1,3},{2,0},{3,1},{4,6},{5,7},{6,4},{7,5},{8,10},{9,11},{10,... | collective-permute-start | bytes 245768 | tf_op jit(solution)/shard_map/ppermute | solution.py:163
  16.0 6.9 %collective-permute-start = (f32[16,1280]{1,0:T(8,128)S(1)}, f32[16,1280]{1,0:T(8,128)S(1)}, u32[]{:S(2)}, u32[]{:S(2)}) collective-permute-start(f32[16,1280]{1,0:T(8,128)S(1)} %get-tuple-element.12), channel_id=1, source_target_pairs={{0,1},{1,0},{2,3},{3,2},{4,5},{5,4},{6,7},{7,6},{8,9},{9,8},{10,11... | collective-permute-start | bytes 245768 | tf_op jit(solution)/shard_map/ppermute | solution.py:163
  22.9 6.5 %collective-permute-start.5 = (f32[16,1024]{1,0:T(8,128)S(1)}, f32[16,1024]{1,0:T(8,128)S(1)}, u32[]{:S(2)}, u32[]{:S(2)}) collective-permute-start(f32[16,1024]{1,0:T(8,128)S(1)} %slice.17.refs_0_), channel_id=1, source_target_pairs={{0,3},{1,2},{2,1},{3,0},{4,7},{5,6},{6,5},{7,4},{8,11},{9,10},{10,... | collective-permute-start | bytes 196616 | tf_op jit(solution)/shard_map/ppermute | solution.py:163
  25.7 5.9 %collective-permute-start.4 = (f32[16,1024]{1,0:T(8,128)S(1)}, f32[16,1024]{1,0:T(8,128)S(1)}, u32[]{:S(2)}, u32[]{:S(2)}) collective-permute-start(f32[16,1024]{1,0:T(8,128)S(1)} %slice.17.refs_0_), channel_id=1, source_target_pairs={{0,2},{1,3},{2,0},{3,1},{4,6},{5,7},{6,4},{7,5},{8,10},{9,11},{10,... | collective-permute-start | bytes 196616 | tf_op jit(solution)/shard_map/ppermute | solution.py:163
  25.7 5.9 %collective-permute-start.3 = (f32[16,1024]{1,0:T(8,128)S(1)}, f32[16,1024]{1,0:T(8,128)S(1)}, u32[]{:S(2)}, u32[]{:S(2)}) collective-permute-start(f32[16,1024]{1,0:T(8,128)S(1)} %slice.17.refs_0_), channel_id=1, source_target_pairs={{0,1},{1,0},{2,3},{3,2},{4,5},{5,4},{6,7},{7,6},{8,9},{9,8},{10,11... | collective-permute-start | bytes 196616 | tf_op jit(solution)/shard_map/ppermute | solution.py:163
  41.0 1.6 %collective-permute-start.6 = (f32[64,1088]{1,0:T(8,128)S(1)}, f32[64,1088]{1,0:T(8,128)S(1)}, u32[]{:S(2)}, u32[]{:S(2)}) collective-permute-start(f32[64,1088]{1,0:T(8,128)S(1)} %dynamic-slice_bitcast_fusion), channel_id=1, source_target_pairs={{0,4},{4,0},{8,12},{12,8},{1,5},{5,1},{9,13},{13,9},{2,6},{6,2},{1... | collective-permute-start | bytes 835592 | tf_op jit(solution)/shard_map/ppermute | solution.py:163
  42.7 9.1 %collective-permute-start.7 = (f32[64,1088]{1,0:T(8,128)S(1)}, f32[64,1088]{1,0:T(8,128)S(1)}, u32[]{:S(2)}, u32[]{:S(2)}) collective-permute-start(f32[64,1088]{1,0:T(8,128)S(1)} %bitcast_add_fusion), channel_id=1, source_target_pairs={{0,8},{4,12},{8,0},{12,4},{1,9},{5,13},{9,1},{13,5},{2,10},{6,14},... | collective-permute-start | bytes 835592 | tf_op jit(solution)/shard_map/ppermute | solution.py:163
  51.8 1.7 %collective-permute-start.8 = (f32[64,1024]{1,0:T(8,128)S(1)}, f32[64,1024]{1,0:T(8,128)S(1)}, u32[]{:S(2)}, u32[]{:S(2)}) collective-permute-start(f32[64,1024]{1,0:T(8,128)S(1)} %slice.19.mine), channel_id=1, source_target_pairs={{0,4},{4,0},{8,12},{12,8},{1,5},{5,1},{9,13},{13,9},{2,6},{6,2},{1... | collective-permute-start | bytes 786440 | tf_op jit(solution)/shard_map/ppermute | solution.py:163

commit v3 on v2

v3 whole, which is shorter than its diff:
```python
import functools

import jax
import jax.numpy as jnp
from jax import lax
from jax.experimental import pallas as pl
from jax.experimental.pallas import tpu as pltpu
from jax.sharding import PartitionSpec as P

OB = 8
F32 = jnp.float32
BF16 = jnp.bfloat16
HIGHEST = lax.Precision.HIGHEST
VMEM = pl.BlockSpec(memory_space=pltpu.VMEM)
HBM = pl.BlockSpec(memory_space=pltpu.HBM)
VMEM_BYTES = 16 << 20


def gram_of(factor):
    return lax.dot_general(
        factor, factor, (((1,), (1,)), ((), ())), precision=HIGHEST, preferred_element_type=F32
    )


def spd_inverse(matrix, panel=8):
    size = matrix.shape[0]
    rows = lax.broadcasted_iota(jnp.int32, matrix.shape, 0)
    cols = lax.broadcasted_iota(jnp.int32, matrix.shape, 1)
    for start in range(0, size, panel):
        columns = [
            jnp.broadcast_to(matrix[:, start + j : start + j + 1], matrix.shape) for j in range(panel)
        ]
        for j in range(panel):
            k = start + j
            column = columns[j]
            inverse_pivot = 1.0 / column[k : k + 1, :]
            row = jnp.where(cols[k : k + 1] == k, 1.0, matrix[k : k + 1, :]) * inverse_pivot
            for later in range(j + 1, panel):
                ahead = columns[later][k : k + 1, :] * inverse_pivot
                columns[later] = jnp.where(rows == k, ahead, columns[later] - column * ahead)
            matrix = jnp.where(rows == k, row, jnp.where(cols == k, 0.0, matrix) - column * row)
    return matrix


def anchor_pass(
    axis, hours, live, anchors, dests, dest_factor, hour_factor, values, hour_gram, values_buf, scale_rows, *refs,
):
    parts, refs = refs[:-10], refs[-10:]
    (sums, dest_buf, hour_buf, hour_rows, hours_s, live_s, anchors_s, dests_s, sems, small_sems) = refs
    tiles, slots, tile_size, _ = values_buf.shape
    part_rows = parts[0].shape[0]
    rank, width = sums.shape
    small = [
        (hours, hours_s), (live, live_s), (anchors, anchors_s), (dests, dests_s), (hour_factor, hour_buf),
        (dest_factor, dest_buf),
    ]
    small_copies = [pltpu.make_async_copy(s, d, small_sems.at[i]) for i, (s, d) in enumerate(small)]
    copies = [pltpu.make_async_copy(values.at[t], values_buf.at[t], sems.at[t]) for t in range(tiles)]
    for copy in small_copies:
        copy.start()
    for copy in copies:
        copy.start(priority=1)
    sums[...] = jnp.zeros_like(sums)
    for copy in small_copies:
        copy.wait()
    hour_rows[...] = hour_buf[...].T
    hour_gram[...] = gram_of(hour_buf[...])
    gram = gram_of(dest_buf[...])
    packed = jnp.concatenate(
        [gram[c * part_rows : (c + 1) * part_rows] for c in range(rank // part_rows)], axis=1
    )
    for part in parts:
        part[:, width:] = packed
    for t in range(tiles):
        dest_at = pl.multiple_of(dests_s[0, 0, t] * tile_size, tile_size)
        anchor_at = pl.multiple_of(anchors_s[0, 0, t] * tile_size, tile_size)
        dest_rows = dest_buf[:, pl.ds(dest_at, tile_size)].T
        weights = []
        for s in range(slots):
            scale = hour_rows[pl.ds(hours_s[t, 0, s], 1), :]
            scale = jnp.where(s < live_s[0, 0, t], scale, 0.0)
            scale_rows[t, s : s + 1, :] = scale
            weights.append((dest_rows * scale).astype(BF16))
        copies[t].wait()
        tile = jnp.concatenate([values_buf[t, s] for s in range(slots)], axis=1)
        term = jnp.dot(tile, jnp.concatenate(weights, axis=0), preferred_element_type=F32)
        sums[:, pl.ds(anchor_at, tile_size)] += term.T
    me = lax.axis_index(axis)
    for k, part in enumerate(parts):
        at = pl.multiple_of(jnp.bitwise_xor(me, k) * part_rows, part_rows)
        part[:, :width] = sums[pl.ds(at, part_rows), :]


def add_parts(*refs):
    parts, (piece, packed) = refs[:-2], refs[-2:]
    width = piece.shape[1]
    total = tree_sum([part[...] for part in parts])
    piece[...] = total[:, :width]
    packed[...] = total[:, width:]


def spread_scales(scale_rows, spread):
    tiles, slots, rank, tile_size = spread.shape
    for t in range(tiles):
        columns = scale_rows[t].T
        for s in range(slots):
            spread[t, s] = jnp.broadcast_to(columns[:, s : s + 1], (rank, tile_size))


def dest_gram_inverse(packed, hour_gram, inverse):
    part_rows, width = packed.shape
    rank = hour_gram.shape[0]
    gram = jnp.concatenate([packed[:, c * rank : (c + 1) * rank] for c in range(width // rank)], axis=0)
    inverse[...] = spd_inverse(gram * hour_gram[...])


def dest_pass(dest_axis, orig_axis, anchors, dests, values, spread, gram_inverse, *refs):
    pieces, refs = refs[:-8], refs[-8:]
    anchor_factor, kept, sent, sums, halves, anchors_s, dests_s, small_sems = refs
    tiles, slots, tile_size, _ = values.shape
    rank, width = sums.shape
    half = halves.shape[2]
    half_tiles = half // tile_size
    small_copies = [
        pltpu.make_async_copy(anchors, anchors_s, small_sems.at[0]),
        pltpu.make_async_copy(dests, dests_s, small_sems.at[1]),
    ]
    for copy in small_copies:
        copy.start()
    me = lax.axis_index(dest_axis)
    core = lax.rem(lax.axis_index(orig_axis), 2)
    part_rows = pieces[0].shape[0]
    for k, piece in enumerate(pieces):
        at = pl.multiple_of(jnp.bitwise_xor(me, k) * part_rows, part_rows)
        sums[pl.ds(at, part_rows), :] = piece[...]
    solved = jnp.dot(gram_inverse[...], sums[...], precision=HIGHEST, preferred_element_type=F32)
    anchor_factor[...] = solved
    gram = gram_of(solved)
    kept[:, half:] = gram
    sent[:, half:] = gram
    halves[...] = jnp.zeros_like(halves)
    for copy in small_copies:
        copy.wait()
    for t in range(tiles):
        anchor_at = pl.multiple_of(anchors_s[0, 0, t] * tile_size, tile_size)
        dest = dests_s[0, 0, t]
        tile_factor = anchor_factor[:, pl.ds(anchor_at, tile_size)]
        weights = jnp.concatenate([(tile_factor * spread[t, s]).astype(BF16) for s in range(slots)], axis=1)
        tile = values[t].reshape(slots * tile_size, tile_size)
        term = jnp.dot(weights, tile, preferred_element_type=F32)
        dest_at = pl.multiple_of(lax.rem(dest, half_tiles) * tile_size, tile_size)
        halves[dest // half_tiles, :, pl.ds(dest_at, tile_size)] += term
    kept[:, :half] = halves[core]
    sent[:, :half] = halves[1 - core]


def anchor_gram_inverse(gram, hour_gram, inverse):
    total = gram[...]
    rows = lax.broadcasted_iota(jnp.int32, total.shape, 0)
    cols = lax.broadcasted_iota(jnp.int32, total.shape, 1)
    diagonal = jnp.where(rows == cols, total, 0.0)
    row_scale = 1.0 / jnp.sqrt(jnp.sum(diagonal, axis=1, keepdims=True) + 1e-06)
    col_scale = 1.0 / jnp.sqrt(jnp.sum(diagonal, axis=0, keepdims=True) + 1e-06)
    inverse[...] = spd_inverse((total * row_scale * col_scale) * hour_gram[...]) * col_scale


def dest_solve(axis, gram_inverse, mine, other, dest_factor):
    half = mine.shape[1]
    core = lax.rem(lax.axis_index(axis), 2)
    for at, piece in ((core, mine), (1 - core, other)):
        dest_factor[:, pl.ds(pl.multiple_of(at * half, half), half)] = jnp.dot(
            gram_inverse[...], piece[...], precision=HIGHEST, preferred_element_type=F32
        )


def swap(array, axis, count, distance):
    return lax.ppermute(array, axis, [(i, i ^ distance) for i in range(count)])


def tree_sum(terms):
    while len(terms) > 1:
        terms = [terms[i] + terms[i + 1] for i in range(0, len(terms), 2)]
    return terms[0]


def in_hbm(array):
    return pltpu.with_memory_space_constraint(array, pltpu.HBM)


def in_vmem(array):
    return pltpu.with_memory_space_constraint(array, pltpu.VMEM)


def call(body, out_shape, in_specs, scratch_shapes=()):
    return pl.pallas_call(
        body,
        out_shape=out_shape,
        in_specs=in_specs,
        out_specs=jax.tree.map(lambda _: VMEM, out_shape),
        scratch_shapes=list(scratch_shapes),
        compiler_params=pltpu.CompilerParams(vmem_limit_bytes=VMEM_BYTES),
    )


def solution(mesh):
    dest_count = mesh.shape["dest"]
    orig_count = mesh.shape["orig"]

    def shards(hours_of_values, tile_hours, tile_anchor, tile_dest, tile_live, dest_factor_in, hour_factor):
        values = hours_of_values[0, 0]
        tiles, slots, tile_size, _ = values.shape
        rank, dest_width = dest_factor_in.shape
        hour_count = hour_factor.shape[1]
        width = OB * tile_size
        part_rows = rank // dest_count
        half = dest_width // 2
        square = jax.ShapeDtypeStruct((rank, rank), F32)
        index_scratch = [pltpu.SMEM((1, 1, tiles), jnp.int32)] * 2
        hours = in_hbm(tile_hours.reshape(tiles, 1, slots))
        live, anchors, dests = (in_hbm(index) for index in (tile_live, tile_anchor, tile_dest))
        hour_gram, values, scale_rows, *parts = call(
            functools.partial(anchor_pass, "dest"),
            (
                square,
                pltpu.VMEM(values.shape, BF16),
                jax.ShapeDtypeStruct((tiles, slots, rank), F32),
                *[jax.ShapeDtypeStruct((part_rows, width + dest_count * rank), F32)] * dest_count,
            ),
            [HBM] * 7,
            [
                pltpu.VMEM((rank, width), F32),
                pltpu.VMEM((rank, dest_width), F32),
                pltpu.VMEM((rank, hour_count), F32),
                pltpu.VMEM((hour_count, rank), F32),
                pltpu.SMEM((tiles, 1, slots), jnp.int32),
                *index_scratch,
                *index_scratch[:1],
                pltpu.SemaphoreType.DMA((tiles,)),
                pltpu.SemaphoreType.DMA((6,)),
            ],
        )(hours, live, anchors, dests, in_hbm(dest_factor_in), in_hbm(hour_factor), in_hbm(values))
        spread = call(spread_scales, pltpu.VMEM((tiles, slots, rank, tile_size), F32), [VMEM])(scale_rows)
        parts = parts[:1] + [swap(parts[k], "dest", dest_count, k) for k in range(1, dest_count)]
        parts, spread = lax.optimization_barrier((parts, spread))
        piece, packed = call(
            add_parts,
            (
                jax.ShapeDtypeStruct((part_rows, width), F32),
                jax.ShapeDtypeStruct((part_rows, dest_count * rank), F32),
            ),
            [VMEM] * dest_count,
        )(*parts)
        pieces = [piece] + [swap(piece, "dest", dest_count, k) for k in range(1, dest_count)]
        dest_inverse = call(dest_gram_inverse, square, [VMEM] * 2)(packed, hour_gram)

        anchor_factor, kept, sent = call(
            functools.partial(dest_pass, "dest", "orig"),
            (
                jax.ShapeDtypeStruct((rank, width), F32),
                *[jax.ShapeDtypeStruct((rank, half + rank), F32)] * 2,
            ),
            [HBM] * 2 + [VMEM] * (3 + dest_count),
            [
                pltpu.VMEM((rank, width), F32),
                pltpu.VMEM((2, rank, half), F32),
                *index_scratch,
                pltpu.SemaphoreType.DMA((2,)),
            ],
        )(anchors, dests, in_vmem(values), in_vmem(spread), dest_inverse, *pieces)

        mine = kept + swap(sent, "orig", orig_count, 1)
        distance = 2
        while distance < orig_count:
            mine = mine + swap(mine, "orig", orig_count, distance)
            distance *= 2
        sums, gram = mine[:, :half], mine[:, half:]
        anchor_inverse = call(anchor_gram_inverse, square, [VMEM] * 2)(gram, hour_gram)
        other = swap(sums, "orig", orig_count, 1)
        dest_factor = call(
            functools.partial(dest_solve, "orig"),
            jax.ShapeDtypeStruct((rank, dest_width), F32),
            [VMEM] * 3,
        )(anchor_inverse, sums, other)
        return anchor_factor, dest_factor

    placed = (
        P(("scen", "orig"), "dest", None, None, None, None),
        P(("scen", "orig"), "dest", None, None),
        P(("scen", "orig"), "dest", None),
        P(("scen", "orig"), "dest", None),
        P(("scen", "orig"), "dest", None),
        P(None, ("scen", "dest")),
        P(None, "scen"),
    )
    return jax.shard_map(
        shards,
        mesh=mesh,
        in_specs=placed,
        out_specs=(P(None, ("scen", "orig")), P(None, ("scen", "dest"))),
        check_vma=False,
    )
```

time: 55.1 us -> 46.8 us (0.85)
  Pallas kernels: 24 us -> 18.9 us
  waiting for transfers between devices: 17.9 us -> 15.1 us
    pallas_call x3 -> x5, Pallas kernels: 21 us -> 15.9 us  [the longest x1 7.86 us: shards(): call(functools.partial(anchor_pass, 'dest'), (square, pltpu.VMEM(values.s...]
    ppermute x9, waiting for transfers between devices: 17.9 us -> 15.1 us  [swap(): return lax.ppermute(array, axis, [(i, i ^ distance) for i in range(count)])]
  transfers between devices with their start and end apart: 9 -> 9, of which waited for: 6 -> 5; matrix products, arithmetic and copies ran while one was open for 0% -> 0% of each run, Pallas kernels for 6% -> 13%
where the time goes in v3:
time: 46.8 us; the launch traced here: 46.7 us
  Pallas kernels  18.9 us (40%)
  waiting for transfers between devices  15.1 us (32%)
  starting transfers between devices  11.8 us (25%)
  between operations  0.73 us (2%)
    ppermute x9, waiting for transfers between devices, swap(): return lax.ppermute(array, axis, [(i, i ^ distance) for i in range(count)])  15.1 us
    ppermute x9, starting transfers between devices, swap(): return lax.ppermute(array, axis, [(i, i ^ distance) for i in range(count)])  11.8 us
    pallas_call x1, Pallas kernels, shards(): call(functools.partial(anchor_pass, 'dest'), (square, pltpu.VMEM(values.s...  7.86 us
    pallas_call x1, Pallas kernels, shards(): call(functools.partial(dest_pass, 'dest', 'orig'), (jax.ShapeDtypeStruct(...  3.49 us
    pallas_call x1, Pallas kernels, shards(): call(spread_scales, pltpu.VMEM((tiles, slots, rank, tile_size), F32), [VM...  3.07 us
    pallas_call x1, Pallas kernels, shards(): call(anchor_gram_inverse, square, [VMEM] * 2)(gram, hour_gram)  1.62 us
    pallas_call x1, Pallas kernels, shards(): call(dest_gram_inverse, square, [VMEM] * 2)(packed, hour_gram)  1.5 us
    pallas_call x1, Pallas kernels, shards(): call(functools.partial(dest_solve, 'orig'), jax.ShapeDtypeStruct((rank, d...  1.37 us
  transfers between devices with their start and end apart: 9, of which 5 were waited for; matrix products, arithmetic and copies ran while one was open for 0% of the time, Pallas kernels for 13%

profile of v3, /device:TPU:0, one launch (start us, length us, event | category | flops | bytes accessed | tf_op | source)
XLA Modules:
  0.0 46.7 jit_solution(7788223433963850680)
XLA Ops:
  0.6 7.9 %shard_map.86 = (f32[64,64]{1,0:T(8,128)S(1)}, bf16[12,24,128,128]{3,2,1,0:T(8,128)(2,1)S(1)}, f32[12,24,64]{2,1,0:T(8,128)S(1)}, f32[16,1280]{1,0:T(8,128)S(1)}...) custom-call(s32[12,1,24]{2,1,0:T(1,128)} %bitcast.3, s32[1,1,12]{2,1,0:T(1,128)} %live.1, ...), custom_call_target="tpu_custom_call" | custom-call | tf_op jit(solution)/shard_map/pallas_call | solution.py:221
  8.5 3.1 %collective-permute-start = (f32[16,1280]{1,0:T(8,128)S(1)}, f32[16,1280]{1,0:T(8,128)S(1)}, u32[]{:S(2)}, u32[]{:S(2)}) collective-permute-start(f32[16,1280]{1,0:T(8,128)S(1)} %get-tuple-element.21), channel_id=1, source_target_pairs={{0,1},{1,0},{2,3},{3,2},{4,5},{5,4},{6,7},{7,6},{8,9},{9,8},{10,11... | collective-permute-start | bytes 245768 | tf_op jit(solution)/shard_map/ppermute | solution.py:177
  11.6 2.6 %collective-permute-start.1 = (f32[16,1280]{1,0:T(8,128)S(1)}, f32[16,1280]{1,0:T(8,128)S(1)}, u32[]{:S(2)}, u32[]{:S(2)}) collective-permute-start(f32[16,1280]{1,0:T(8,128)S(1)} %get-tuple-element.22), channel_id=1, source_target_pairs={{0,2},{1,3},{2,0},{3,1},{4,6},{5,7},{6,4},{7,5},{8,10},{9,11},{10,... | collective-permute-start | bytes 245768 | tf_op jit(solution)/shard_map/ppermute | solution.py:177
  14.2 0.0 collective-permute-start.2
  14.2 3.1 %shard_map.87.spread = f32[12,24,64,128]{3,2,1,0:T(8,128)S(1)} custom-call(f32[12,24,64]{2,1,0:T(8,128)S(1)} %get-tuple-element.24.scale_rows), custom_call_target="tpu_custom_call" | custom-call | tf_op jit(solution)/shard_map/pallas_call | solution.py:242
  17.3 0.0 collective-permute-done.refs_1_
  17.3 3.5 %collective-permute-done.1.refs_2_ = f32[16,1280]{1,0:T(8,128)S(1)} collective-permute-done((f32[16,1280]{1,0:T(8,128)S(1)}, f32[16,1280]{1,0:T(8,128)S(1)}, u32[]{:S(2)}, u32[]{:S(2)}) %collective-permute-start.1) | collective-permute-done | bytes 81952 | tf_op jit(solution)/shard_map/ppermute | solution.py:177
  20.8 0.0 collective-permute-done.2.refs_3_
  20.8 2.5 %collective-permute-start.5 = (f32[16,1024]{1,0:T(8,128)S(1)}, f32[16,1024]{1,0:T(8,128)S(1)}, u32[]{:S(2)}, u32[]{:S(2)}) collective-permute-start(f32[16,1024]{1,0:T(8,128)S(1)} %get-tuple-element.32.refs_0_), channel_id=1, source_target_pairs={{0,3},{1,2},{2,1},{3,0},{4,7},{5,6},{6,5},{7,4},{8,11},{9,10},{10,... | collective-permute-start | bytes 196616 | tf_op jit(solution)/shard_map/ppermute | solution.py:177
  23.4 0.4 collective-permute-start.4
  23.8 1.5 %collective-permute-start.3 = (f32[16,1024]{1,0:T(8,128)S(1)}, f32[16,1024]{1,0:T(8,128)S(1)}, u32[]{:S(2)}, u32[]{:S(2)}) collective-permute-start(f32[16,1024]{1,0:T(8,128)S(1)} %get-tuple-element.32.refs_0_), channel_id=1, source_target_pairs={{0,1},{1,0},{2,3},{3,2},{4,5},{5,4},{6,7},{7,6},{8,9},{9,8},{10,11... | collective-permute-start | bytes 196616 | tf_op jit(solution)/shard_map/ppermute | solution.py:177
  25.3 1.5 %shard_map.89.gram_inverse = f32[64,64]{1,0:T(8,128)S(1)} custom-call(f32[16,256]{1,0:T(8,128)S(1)} %get-tuple-element.30.packed, f32[64,64]{1,0:T(8,128)S(1)} %get-tuple-element.31.hour_gram), custom_call_target="tpu_custom_call" | custom-call | tf_op jit(solution)/shard_map/pallas_call | solution.py:254
  26.8 0.6 %collective-permute-done.5.refs_3_ = f32[16,1024]{1,0:T(8,128)S(1)} collective-permute-done((f32[16,1024]{1,0:T(8,128)S(1)}, f32[16,1024]{1,0:T(8,128)S(1)}, u32[]{:S(2)}, u32[]{:S(2)}) %collective-permute-start.5) | collective-permute-done | bytes 65568 | tf_op jit(solution)/shard_map/ppermute | solution.py:177
  27.3 1.9 %collective-permute-done.4.refs_2_ = f32[16,1024]{1,0:T(8,128)S(1)} collective-permute-done((f32[16,1024]{1,0:T(8,128)S(1)}, f32[16,1024]{1,0:T(8,128)S(1)}, u32[]{:S(2)}, u32[]{:S(2)}) %collective-permute-start.4) | collective-permute-done | bytes 65568 | tf_op jit(solution)/shard_map/ppermute | solution.py:177
  29.2 0.0 collective-permute-done.3.refs_1_
  29.2 3.5 %shard_map.90 = (f32[64,1024]{1,0:T(8,128)}, f32[64,1088]{1,0:T(8,128)S(1)}, f32[64,1088]{1,0:T(8,128)S(1)}) custom-call(s32[1,1,12]{2,1,0:T(1,128)} %anchors.3, s32[1,1,12]{2,1,0:T(1,128)} %dests.3, bf16[12,24,128,128]{3,2,1,0:T(8,128)(2,1)S(1)} %get-tuple-element.19.values, f32[12,24,64,128]{3,2,1,0:T(8,128)S(1)} %shard_map.87.spread, ...), custom_call_target="tpu_custom_call" | custom-call | tf_op jit(solution)/shard_map/pallas_call | solution.py:256
  32.7 0.1 collective-permute-start.6
  32.8 1.6 %collective-permute-done.6 = f32[64,1088]{1,0:T(8,128)S(1)} collective-permute-done((f32[64,1088]{1,0:T(8,128)S(1)}, f32[64,1088]{1,0:T(8,128)S(1)}, u32[]{:S(2)}, u32[]{:S(2)}) %collective-permute-start.6) | collective-permute-done | bytes 278560 | tf_op jit(solution)/shard_map/ppermute | solution.py:177
  34.4 1.5 %collective-permute-start.7 = (f32[64,1088]{1,0:T(8,128)S(1)}, f32[64,1088]{1,0:T(8,128)S(1)}, u32[]{:S(2)}, u32[]{:S(2)}) collective-permute-start(f32[64,1088]{1,0:T(8,128)S(1)} %add.6), channel_id=1, source_target_pairs={{0,8},{4,12},{8,0},{12,4},{1,9},{5,13},{9,1},{13,5},{2,10},{6,14},... | collective-permute-start | bytes 835592 | tf_op jit(solution)/shard_map/ppermute | solution.py:177
  35.9 7.6 %collective-permute-done.7 = f32[64,1088]{1,0:T(8,128)S(1)} collective-permute-done((f32[64,1088]{1,0:T(8,128)S(1)}, f32[64,1088]{1,0:T(8,128)S(1)}, u32[]{:S(2)}, u32[]{:S(2)}) %collective-permute-start.7) | collective-permute-done | bytes 278560 | tf_op jit(solution)/shard_map/ppermute | solution.py:177
  43.6 0.1 collective-permute-start.8
  43.7 1.6 %shard_map.91.gram_inverse = f32[64,64]{1,0:T(8,128)S(1)} custom-call(f32[64,64]{1,0:T(8,128)S(1)} %slice.8.gram, f32[64,64]{1,0:T(8,128)S(1)} %get-tuple-element.31.hour_gram), custom_call_target="tpu_custom_call" | custom-call | tf_op jit(solution)/shard_map/pallas_call | solution.py:277
  45.3 0.0 collective-permute-done.8.other
  45.3 1.4 %shard_map.92 = f32[64,2048]{1,0:T(8,128)} custom-call(f32[64,64]{1,0:T(8,128)S(1)} %shard_map.91.gram_inverse, f32[64,1024]{1,0:T(8,128)S(1)} %slice.9.mine, f32[64,1024]{1,0:T(8,128)S(1)} %collective-permute-done.8.other), custom_call_target="tpu_custom_call" | custom-call | tf_op jit(solution)/shard_map/pallas_call | solution.py:279
  (5 shorter events, 0.1 us)
Async XLA Ops:
  8.5 8.8 %collective-permute-start = (f32[16,1280]{1,0:T(8,128)S(1)}, f32[16,1280]{1,0:T(8,128)S(1)}, u32[]{:S(2)}, u32[]{:S(2)}) collective-permute-start(f32[16,1280]{1,0:T(8,128)S(1)} %get-tuple-element.21), channel_id=1, source_target_pairs={{0,1},{1,0},{2,3},{3,2},{4,5},{5,4},{6,7},{7,6},{8,9},{9,8},{10,11... | collective-permute-start | bytes 245768 | tf_op jit(solution)/shard_map/ppermute | solution.py:177
  11.6 9.2 %collective-permute-start.1 = (f32[16,1280]{1,0:T(8,128)S(1)}, f32[16,1280]{1,0:T(8,128)S(1)}, u32[]{:S(2)}, u32[]{:S(2)}) collective-permute-start(f32[16,1280]{1,0:T(8,128)S(1)} %get-tuple-element.22), channel_id=1, source_target_pairs={{0,2},{1,3},{2,0},{3,1},{4,6},{5,7},{6,4},{7,5},{8,10},{9,11},{10,... | collective-permute-start | bytes 245768 | tf_op jit(solution)/shard_map/ppermute | solution.py:177
  14.2 6.6 %collective-permute-start.2 = (f32[16,1280]{1,0:T(8,128)S(1)}, f32[16,1280]{1,0:T(8,128)S(1)}, u32[]{:S(2)}, u32[]{:S(2)}) collective-permute-start(f32[16,1280]{1,0:T(8,128)S(1)} %get-tuple-element.23), channel_id=1, source_target_pairs={{0,3},{1,2},{2,1},{3,0},{4,7},{5,6},{6,5},{7,4},{8,11},{9,10},{10,... | collective-permute-start | bytes 245768 | tf_op jit(solution)/shard_map/ppermute | solution.py:177
  20.8 6.5 %collective-permute-start.5 = (f32[16,1024]{1,0:T(8,128)S(1)}, f32[16,1024]{1,0:T(8,128)S(1)}, u32[]{:S(2)}, u32[]{:S(2)}) collective-permute-start(f32[16,1024]{1,0:T(8,128)S(1)} %get-tuple-element.32.refs_0_), channel_id=1, source_target_pairs={{0,3},{1,2},{2,1},{3,0},{4,7},{5,6},{6,5},{7,4},{8,11},{9,10},{10,... | collective-permute-start | bytes 196616 | tf_op jit(solution)/shard_map/ppermute | solution.py:177
  23.4 5.8 %collective-permute-start.4 = (f32[16,1024]{1,0:T(8,128)S(1)}, f32[16,1024]{1,0:T(8,128)S(1)}, u32[]{:S(2)}, u32[]{:S(2)}) collective-permute-start(f32[16,1024]{1,0:T(8,128)S(1)} %get-tuple-element.32.refs_0_), channel_id=1, source_target_pairs={{0,2},{1,3},{2,0},{3,1},{4,6},{5,7},{6,4},{7,5},{8,10},{9,11},{10,... | collective-permute-start | bytes 196616 | tf_op jit(solution)/shard_map/ppermute | solution.py:177
  23.8 5.4 %collective-permute-start.3 = (f32[16,1024]{1,0:T(8,128)S(1)}, f32[16,1024]{1,0:T(8,128)S(1)}, u32[]{:S(2)}, u32[]{:S(2)}) collective-permute-start(f32[16,1024]{1,0:T(8,128)S(1)} %get-tuple-element.32.refs_0_), channel_id=1, source_target_pairs={{0,1},{1,0},{2,3},{3,2},{4,5},{5,4},{6,7},{7,6},{8,9},{9,8},{10,11... | collective-permute-start | bytes 196616 | tf_op jit(solution)/shard_map/ppermute | solution.py:177
  32.7 1.6 %collective-permute-start.6 = (f32[64,1088]{1,0:T(8,128)S(1)}, f32[64,1088]{1,0:T(8,128)S(1)}, u32[]{:S(2)}, u32[]{:S(2)}) collective-permute-start(f32[64,1088]{1,0:T(8,128)S(1)} %get-tuple-element.35), channel_id=1, source_target_pairs={{0,4},{4,0},{8,12},{12,8},{1,5},{5,1},{9,13},{13,9},{2,6},{6,2},{1... | collective-permute-start | bytes 835592 | tf_op jit(solution)/shard_map/ppermute | solution.py:177
  34.4 9.1 %collective-permute-start.7 = (f32[64,1088]{1,0:T(8,128)S(1)}, f32[64,1088]{1,0:T(8,128)S(1)}, u32[]{:S(2)}, u32[]{:S(2)}) collective-permute-start(f32[64,1088]{1,0:T(8,128)S(1)} %add.6), channel_id=1, source_target_pairs={{0,8},{4,12},{8,0},{12,4},{1,9},{5,13},{9,1},{13,5},{2,10},{6,14},... | collective-permute-start | bytes 835592 | tf_op jit(solution)/shard_map/ppermute | solution.py:177
  43.6 1.7 %collective-permute-start.8 = (f32[64,1024]{1,0:T(8,128)S(1)}, f32[64,1024]{1,0:T(8,128)S(1)}, u32[]{:S(2)}, u32[]{:S(2)}) collective-permute-start(f32[64,1024]{1,0:T(8,128)S(1)} %slice.9.mine), channel_id=1, source_target_pairs={{0,4},{4,0},{8,12},{12,8},{1,5},{5,1},{9,13},{13,9},{2,6},{6,2},{1... | collective-permute-start | bytes 786440 | tf_op jit(solution)/shard_map/ppermute | solution.py:177

commit v4 on v3

--- a/solution.py
+++ b/solution.py
@@ -10,15 +10,32 @@
 OB = 8
 F32 = jnp.float32
 BF16 = jnp.bfloat16
-HIGHEST = lax.Precision.HIGHEST
 VMEM = pl.BlockSpec(memory_space=pltpu.VMEM)
 HBM = pl.BlockSpec(memory_space=pltpu.HBM)
 VMEM_BYTES = 16 << 20
 
 
+def head_and_tail(array):
+    head = array.astype(BF16)
+    return head, (array - head.astype(F32)).astype(BF16)
+
+
 def gram_of(factor):
-    return lax.dot_general(
-        factor, factor, (((1,), (1,)), ((), ())), precision=HIGHEST, preferred_element_type=F32
+    rank = factor.shape[0]
+    head, tail = head_and_tail(factor)
+    both = lax.dot_general(
+        jnp.concatenate([head, tail], axis=0), head, (((1,), (1,)), ((), ())), preferred_element_type=F32
+    )
+    return both[:rank] + (both[rank:] + both[rank:].T)
+
+
+def solve_with(inverse, right_side):
+    inverse_head, inverse_tail = head_and_tail(inverse)
+    head, tail = head_and_tail(right_side)
+    return jnp.dot(
+        jnp.concatenate([inverse_head, inverse_head, inverse_tail, inverse_tail], axis=1),
+        jnp.concatenate([head, tail, head, tail], axis=0),
+        preferred_element_type=F32,
     )
 
 
@@ -71,9 +88,8 @@
     )
     for part in parts:
         part[:, width:] = packed
-    for t in range(tiles):
+    def weights_of(t):
         dest_at = pl.multiple_of(dests_s[0, 0, t] * tile_size, tile_size)
-        anchor_at = pl.multiple_of(anchors_s[0, 0, t] * tile_size, tile_size)
         dest_rows = dest_buf[:, pl.ds(dest_at, tile_size)].T
         weights = []
         for s in range(slots):
@@ -81,10 +97,20 @@
             scale = jnp.where(s < live_s[0, 0, t], scale, 0.0)
             scale_rows[t, s : s + 1, :] = scale
             weights.append((dest_rows * scale).astype(BF16))
-        copies[t].wait()
+        return jnp.concatenate(weights, axis=0)
+
+    starts = [0, tiles // 4, tiles * 7 // 12, tiles]
+    weights = weights_of(0)
+    for t in range(tiles):
+        if t in starts:
+            for arriving in range(t, starts[starts.index(t) + 1]):
+                copies[arriving].wait()
+        anchor_at = pl.multiple_of(anchors_s[0, 0, t] * tile_size, tile_size)
         tile = jnp.concatenate([values_buf[t, s] for s in range(slots)], axis=1)
-        term = jnp.dot(tile, jnp.concatenate(weights, axis=0), preferred_element_type=F32)
+        term = jnp.dot(tile, weights, preferred_element_type=F32)
         sums[:, pl.ds(anchor_at, tile_size)] += term.T
+        if t + 1 < tiles:
+            weights = weights_of(t + 1)
     me = lax.axis_index(axis)
     for k, part in enumerate(parts):
         at = pl.multiple_of(jnp.bitwise_xor(me, k) * part_rows, part_rows)
@@ -115,8 +141,8 @@
 
 
 def dest_pass(dest_axis, orig_axis, anchors, dests, values, spread, gram_inverse, *refs):
-    pieces, refs = refs[:-8], refs[-8:]
-    anchor_factor, kept, sent, sums, halves, anchors_s, dests_s, small_sems = refs
+    pieces, refs = refs[:-10], refs[-10:]
+    anchor_factor, kept, sent, sums, halves, factor, anchors_s, dests_s, small_sems, out_sem = refs
     tiles, slots, tile_size, _ = values.shape
     rank, width = sums.shape
     half = halves.shape[2]
@@ -133,8 +159,10 @@
     for k, piece in enumerate(pieces):
         at = pl.multiple_of(jnp.bitwise_xor(me, k) * part_rows, part_rows)
         sums[pl.ds(at, part_rows), :] = piece[...]
-    solved = jnp.dot(gram_inverse[...], sums[...], precision=HIGHEST, preferred_element_type=F32)
-    anchor_factor[...] = solved
+    solved = solve_with(gram_inverse[...], sums[...])
+    factor[...] = solved
+    out_copy = pltpu.make_async_copy(factor, anchor_factor, out_sem)
+    out_copy.start()
     gram = gram_of(solved)
     kept[:, half:] = gram
     sent[:, half:] = gram
@@ -144,7 +172,7 @@
     for t in range(tiles):
         anchor_at = pl.multiple_of(anchors_s[0, 0, t] * tile_size, tile_size)
         dest = dests_s[0, 0, t]
-        tile_factor = anchor_factor[:, pl.ds(anchor_at, tile_size)]
+        tile_factor = factor[:, pl.ds(anchor_at, tile_size)]
         weights = jnp.concatenate([(tile_factor * spread[t, s]).astype(BF16) for s in range(slots)], axis=1)
         tile = values[t].reshape(slots * tile_size, tile_size)
         term = jnp.dot(weights, tile, preferred_element_type=F32)
@@ -152,6 +180,7 @@
         halves[dest // half_tiles, :, pl.ds(dest_at, tile_size)] += term
     kept[:, :half] = halves[core]
     sent[:, :half] = halves[1 - core]
+    out_copy.wait()
 
 
 def anchor_gram_inverse(gram, hour_gram, inverse):
@@ -164,13 +193,17 @@
     inverse[...] = spd_inverse((total * row_scale * col_scale) * hour_gram[...]) * col_scale
 
 
-def dest_solve(axis, gram_inverse, mine, other, dest_factor):
+def dest_solve(axis, gram_inverse, mine, other, dest_factor, solved, sems):
     half = mine.shape[1]
     core = lax.rem(lax.axis_index(axis), 2)
-    for at, piece in ((core, mine), (1 - core, other)):
-        dest_factor[:, pl.ds(pl.multiple_of(at * half, half), half)] = jnp.dot(
-            gram_inverse[...], piece[...], precision=HIGHEST, preferred_element_type=F32
-        )
+    copies = []
+    for i, (at, piece) in enumerate(((core, mine), (1 - core, other))):
+        solved[i] = solve_with(gram_inverse[...], piece[...])
+        columns = pl.ds(pl.multiple_of(at * half, half), half)
+        copies.append(pltpu.make_async_copy(solved.at[i], dest_factor.at[:, columns], sems.at[i]))
+        copies[i].start()
+    for copy in copies:
+        copy.wait()
 
 
 def swap(array, axis, count, distance):
@@ -191,12 +224,12 @@
     return pltpu.with_memory_space_constraint(array, pltpu.VMEM)
 
 
-def call(body, out_shape, in_specs, scratch_shapes=()):
+def call(body, out_shape, in_specs, scratch_shapes=(), out_specs=None):
     return pl.pallas_call(
         body,
         out_shape=out_shape,
         in_specs=in_specs,
-        out_specs=jax.tree.map(lambda _: VMEM, out_shape),
+        out_specs=jax.tree.map(lambda _: VMEM, out_shape) if out_specs is None else out_specs,
         scratch_shapes=list(scratch_shapes),
         compiler_params=pltpu.CompilerParams(vmem_limit_bytes=VMEM_BYTES),
     )
@@ -263,9 +296,12 @@
             [
                 pltpu.VMEM((rank, width), F32),
                 pltpu.VMEM((2, rank, half), F32),
+                pltpu.VMEM((rank, width), F32),
                 *index_scratch,
                 pltpu.SemaphoreType.DMA((2,)),
+                pltpu.SemaphoreType.DMA,
             ],
+            (HBM, VMEM, VMEM),
         )(anchors, dests, in_vmem(values), in_vmem(spread), dest_inverse, *pieces)
 
         mine = kept + swap(sent, "orig", orig_count, 1)
@@ -280,6 +316,8 @@
             functools.partial(dest_solve, "orig"),
             jax.ShapeDtypeStruct((rank, dest_width), F32),
             [VMEM] * 3,
+            [pltpu.VMEM((2, rank, half), F32), pltpu.SemaphoreType.DMA((2,))],
+            HBM,
         )(anchor_inverse, sums, other)
         return anchor_factor, dest_factor
 

time: 46.8 us -> 43.1 us (0.921)
  Pallas kernels: 18.9 us -> 15.1 us
    pallas_call x1, Pallas kernels: 7.86 us -> 5.29 us  [shards(): call(functools.partial(anchor_pass, 'dest'), (square, pltpu.VMEM(values.s...]
    pallas_call x1, Pallas kernels: 3.49 us -> 2.58 us  [shards(): call(functools.partial(dest_pass, 'dest', 'orig'), (jax.ShapeDtypeStruct(...]
  transfers between devices with their start and end apart: 9 -> 9, of which waited for: 5 -> 5; matrix products, arithmetic and copies ran while one was open for 0% -> 0% of each run, Pallas kernels for 13% -> 14%
where the time goes in v4:
time: 43.1 us; the launch traced here: 42.9 us
  Pallas kernels  15.1 us (35%)
  waiting for transfers between devices  15.1 us (35%)
  starting transfers between devices  11.8 us (27%)
  between operations  0.73 us (2%)
    ppermute x9, waiting for transfers between devices, swap(): return lax.ppermute(array, axis, [(i, i ^ distance) for i in range(count)])  15.1 us
    ppermute x9, starting transfers between devices, swap(): return lax.ppermute(array, axis, [(i, i ^ distance) for i in range(count)])  11.8 us
    pallas_call x1, Pallas kernels, shards(): call(functools.partial(anchor_pass, 'dest'), (square, pltpu.VMEM(values.s...  5.29 us
    pallas_call x1, Pallas kernels, shards(): call(spread_scales, pltpu.VMEM((tiles, slots, rank, tile_size), F32), [VM...  3.07 us
    pallas_call x1, Pallas kernels, shards(): call(functools.partial(dest_pass, 'dest', 'orig'), (jax.ShapeDtypeStruct(...  2.58 us
    pallas_call x1, Pallas kernels, shards(): call(anchor_gram_inverse, square, [VMEM] * 2)(gram, hour_gram)  1.62 us
    pallas_call x1, Pallas kernels, shards(): call(dest_gram_inverse, square, [VMEM] * 2)(packed, hour_gram)  1.5 us
    pallas_call x1, Pallas kernels, shards(): call(functools.partial(dest_solve, 'orig'), jax.ShapeDtypeStruct((rank, d...  1.06 us
  transfers between devices with their start and end apart: 9, of which 5 were waited for; matrix products, arithmetic and copies ran while one was open for 0% of the time, Pallas kernels for 14%

profile of v4, /device:TPU:0, one launch (start us, length us, event | category | flops | bytes accessed | tf_op | source)
XLA Modules:
  0.0 42.9 jit_solution(8767706971658487706)
XLA Ops:
  0.6 5.3 %shard_map.86 = (f32[64,64]{1,0:T(8,128)S(1)}, bf16[12,24,128,128]{3,2,1,0:T(8,128)(2,1)S(1)}, f32[12,24,64]{2,1,0:T(8,128)S(1)}, f32[16,1280]{1,0:T(8,128)S(1)}...) custom-call(s32[12,1,24]{2,1,0:T(1,128)} %bitcast.3, s32[1,1,12]{2,1,0:T(1,128)} %live.1, ...), custom_call_target="tpu_custom_call" | custom-call | tf_op jit(solution)/shard_map/pallas_call | solution.py:254
  5.9 3.1 %collective-permute-start = (f32[16,1280]{1,0:T(8,128)S(1)}, f32[16,1280]{1,0:T(8,128)S(1)}, u32[]{:S(2)}, u32[]{:S(2)}) collective-permute-start(f32[16,1280]{1,0:T(8,128)S(1)} %get-tuple-element.21), channel_id=1, source_target_pairs={{0,1},{1,0},{2,3},{3,2},{4,5},{5,4},{6,7},{7,6},{8,9},{9,8},{10,11... | collective-permute-start | bytes 245768 | tf_op jit(solution)/shard_map/ppermute | solution.py:210
  9.0 2.6 %collective-permute-start.1 = (f32[16,1280]{1,0:T(8,128)S(1)}, f32[16,1280]{1,0:T(8,128)S(1)}, u32[]{:S(2)}, u32[]{:S(2)}) collective-permute-start(f32[16,1280]{1,0:T(8,128)S(1)} %get-tuple-element.22), channel_id=1, source_target_pairs={{0,2},{1,3},{2,0},{3,1},{4,6},{5,7},{6,4},{7,5},{8,10},{9,11},{10,... | collective-permute-start | bytes 245768 | tf_op jit(solution)/shard_map/ppermute | solution.py:210
  11.6 0.0 collective-permute-start.2
  11.6 3.1 %shard_map.87.spread = f32[12,24,64,128]{3,2,1,0:T(8,128)S(1)} custom-call(f32[12,24,64]{2,1,0:T(8,128)S(1)} %get-tuple-element.24.scale_rows), custom_call_target="tpu_custom_call" | custom-call | tf_op jit(solution)/shard_map/pallas_call | solution.py:275
  14.7 0.0 collective-permute-done.refs_1_
  14.7 3.5 %collective-permute-done.1.refs_2_ = f32[16,1280]{1,0:T(8,128)S(1)} collective-permute-done((f32[16,1280]{1,0:T(8,128)S(1)}, f32[16,1280]{1,0:T(8,128)S(1)}, u32[]{:S(2)}, u32[]{:S(2)}) %collective-permute-start.1) | collective-permute-done | bytes 81952 | tf_op jit(solution)/shard_map/ppermute | solution.py:210
  18.2 0.0 collective-permute-done.2.refs_3_
  18.2 2.5 %collective-permute-start.5 = (f32[16,1024]{1,0:T(8,128)S(1)}, f32[16,1024]{1,0:T(8,128)S(1)}, u32[]{:S(2)}, u32[]{:S(2)}) collective-permute-start(f32[16,1024]{1,0:T(8,128)S(1)} %get-tuple-element.32.refs_0_), channel_id=1, source_target_pairs={{0,3},{1,2},{2,1},{3,0},{4,7},{5,6},{6,5},{7,4},{8,11},{9,10},{10,... | collective-permute-start | bytes 196616 | tf_op jit(solution)/shard_map/ppermute | solution.py:210
  20.8 0.4 collective-permute-start.4
  21.2 1.5 %collective-permute-start.3 = (f32[16,1024]{1,0:T(8,128)S(1)}, f32[16,1024]{1,0:T(8,128)S(1)}, u32[]{:S(2)}, u32[]{:S(2)}) collective-permute-start(f32[16,1024]{1,0:T(8,128)S(1)} %get-tuple-element.32.refs_0_), channel_id=1, source_target_pairs={{0,1},{1,0},{2,3},{3,2},{4,5},{5,4},{6,7},{7,6},{8,9},{9,8},{10,11... | collective-permute-start | bytes 196616 | tf_op jit(solution)/shard_map/ppermute | solution.py:210
  22.7 1.5 %shard_map.89.gram_inverse = f32[64,64]{1,0:T(8,128)S(1)} custom-call(f32[16,256]{1,0:T(8,128)S(1)} %get-tuple-element.30.packed, f32[64,64]{1,0:T(8,128)S(1)} %get-tuple-element.31.hour_gram), custom_call_target="tpu_custom_call" | custom-call | tf_op jit(solution)/shard_map/pallas_call | solution.py:287
  24.2 0.6 %collective-permute-done.5.refs_3_ = f32[16,1024]{1,0:T(8,128)S(1)} collective-permute-done((f32[16,1024]{1,0:T(8,128)S(1)}, f32[16,1024]{1,0:T(8,128)S(1)}, u32[]{:S(2)}, u32[]{:S(2)}) %collective-permute-start.5) | collective-permute-done | bytes 65568 | tf_op jit(solution)/shard_map/ppermute | solution.py:210
  24.8 1.9 %collective-permute-done.4.refs_2_ = f32[16,1024]{1,0:T(8,128)S(1)} collective-permute-done((f32[16,1024]{1,0:T(8,128)S(1)}, f32[16,1024]{1,0:T(8,128)S(1)}, u32[]{:S(2)}, u32[]{:S(2)}) %collective-permute-start.4) | collective-permute-done | bytes 65568 | tf_op jit(solution)/shard_map/ppermute | solution.py:210
  26.6 0.0 collective-permute-done.3.refs_1_
  26.6 2.6 %shard_map.90 = (f32[64,1024]{1,0:T(8,128)}, f32[64,1088]{1,0:T(8,128)S(1)}, f32[64,1088]{1,0:T(8,128)S(1)}) custom-call(s32[1,1,12]{2,1,0:T(1,128)} %anchors.3, s32[1,1,12]{2,1,0:T(1,128)} %dests.3, bf16[12,24,128,128]{3,2,1,0:T(8,128)(2,1)S(1)} %get-tuple-element.19.values, f32[12,24,64,128]{3,2,1,0:T(8,128)S(1)} %shard_map.87.spread, ...), custom_call_target="tpu_custom_call" | custom-call | tf_op jit(solution)/shard_map/pallas_call | solution.py:289
  29.2 0.1 collective-permute-start.6
  29.3 1.6 %collective-permute-done.6 = f32[64,1088]{1,0:T(8,128)S(1)} collective-permute-done((f32[64,1088]{1,0:T(8,128)S(1)}, f32[64,1088]{1,0:T(8,128)S(1)}, u32[]{:S(2)}, u32[]{:S(2)}) %collective-permute-start.6) | collective-permute-done | bytes 278560 | tf_op jit(solution)/shard_map/ppermute | solution.py:210
  30.9 1.6 %collective-permute-start.7 = (f32[64,1088]{1,0:T(8,128)S(1)}, f32[64,1088]{1,0:T(8,128)S(1)}, u32[]{:S(2)}, u32[]{:S(2)}) collective-permute-start(f32[64,1088]{1,0:T(8,128)S(1)} %add.6), channel_id=1, source_target_pairs={{0,8},{4,12},{8,0},{12,4},{1,9},{5,13},{9,1},{13,5},{2,10},{6,14},... | collective-permute-start | bytes 835592 | tf_op jit(solution)/shard_map/ppermute | solution.py:210
  32.5 7.6 %collective-permute-done.7 = f32[64,1088]{1,0:T(8,128)S(1)} collective-permute-done((f32[64,1088]{1,0:T(8,128)S(1)}, f32[64,1088]{1,0:T(8,128)S(1)}, u32[]{:S(2)}, u32[]{:S(2)}) %collective-permute-start.7) | collective-permute-done | bytes 278560 | tf_op jit(solution)/shard_map/ppermute | solution.py:210
  40.1 0.1 collective-permute-start.8
  40.2 1.6 %shard_map.91.gram_inverse = f32[64,64]{1,0:T(8,128)S(1)} custom-call(f32[64,64]{1,0:T(8,128)S(1)} %slice.8.gram, f32[64,64]{1,0:T(8,128)S(1)} %get-tuple-element.31.hour_gram), custom_call_target="tpu_custom_call" | custom-call | tf_op jit(solution)/shard_map/pallas_call | solution.py:313
  41.8 0.0 collective-permute-done.8.other
  41.8 1.1 %shard_map.92 = f32[64,2048]{1,0:T(8,128)} custom-call(f32[64,64]{1,0:T(8,128)S(1)} %shard_map.91.gram_inverse, f32[64,1024]{1,0:T(8,128)S(1)} %slice.9.mine, f32[64,1024]{1,0:T(8,128)S(1)} %collective-permute-done.8.other), custom_call_target="tpu_custom_call" | custom-call | tf_op jit(solution)/shard_map/pallas_call | solution.py:315
  (5 shorter events, 0.1 us)
Async XLA Ops:
  5.9 8.8 %collective-permute-start = (f32[16,1280]{1,0:T(8,128)S(1)}, f32[16,1280]{1,0:T(8,128)S(1)}, u32[]{:S(2)}, u32[]{:S(2)}) collective-permute-start(f32[16,1280]{1,0:T(8,128)S(1)} %get-tuple-element.21), channel_id=1, source_target_pairs={{0,1},{1,0},{2,3},{3,2},{4,5},{5,4},{6,7},{7,6},{8,9},{9,8},{10,11... | collective-permute-start | bytes 245768 | tf_op jit(solution)/shard_map/ppermute | solution.py:210
  9.0 9.2 %collective-permute-start.1 = (f32[16,1280]{1,0:T(8,128)S(1)}, f32[16,1280]{1,0:T(8,128)S(1)}, u32[]{:S(2)}, u32[]{:S(2)}) collective-permute-start(f32[16,1280]{1,0:T(8,128)S(1)} %get-tuple-element.22), channel_id=1, source_target_pairs={{0,2},{1,3},{2,0},{3,1},{4,6},{5,7},{6,4},{7,5},{8,10},{9,11},{10,... | collective-permute-start | bytes 245768 | tf_op jit(solution)/shard_map/ppermute | solution.py:210
  11.6 6.6 %collective-permute-start.2 = (f32[16,1280]{1,0:T(8,128)S(1)}, f32[16,1280]{1,0:T(8,128)S(1)}, u32[]{:S(2)}, u32[]{:S(2)}) collective-permute-start(f32[16,1280]{1,0:T(8,128)S(1)} %get-tuple-element.23), channel_id=1, source_target_pairs={{0,3},{1,2},{2,1},{3,0},{4,7},{5,6},{6,5},{7,4},{8,11},{9,10},{10,... | collective-permute-start | bytes 245768 | tf_op jit(solution)/shard_map/ppermute | solution.py:210
  18.2 6.5 %collective-permute-start.5 = (f32[16,1024]{1,0:T(8,128)S(1)}, f32[16,1024]{1,0:T(8,128)S(1)}, u32[]{:S(2)}, u32[]{:S(2)}) collective-permute-start(f32[16,1024]{1,0:T(8,128)S(1)} %get-tuple-element.32.refs_0_), channel_id=1, source_target_pairs={{0,3},{1,2},{2,1},{3,0},{4,7},{5,6},{6,5},{7,4},{8,11},{9,10},{10,... | collective-permute-start | bytes 196616 | tf_op jit(solution)/shard_map/ppermute | solution.py:210
  20.8 5.8 %collective-permute-start.4 = (f32[16,1024]{1,0:T(8,128)S(1)}, f32[16,1024]{1,0:T(8,128)S(1)}, u32[]{:S(2)}, u32[]{:S(2)}) collective-permute-start(f32[16,1024]{1,0:T(8,128)S(1)} %get-tuple-element.32.refs_0_), channel_id=1, source_target_pairs={{0,2},{1,3},{2,0},{3,1},{4,6},{5,7},{6,4},{7,5},{8,10},{9,11},{10,... | collective-permute-start | bytes 196616 | tf_op jit(solution)/shard_map/ppermute | solution.py:210
  21.2 5.4 %collective-permute-start.3 = (f32[16,1024]{1,0:T(8,128)S(1)}, f32[16,1024]{1,0:T(8,128)S(1)}, u32[]{:S(2)}, u32[]{:S(2)}) collective-permute-start(f32[16,1024]{1,0:T(8,128)S(1)} %get-tuple-element.32.refs_0_), channel_id=1, source_target_pairs={{0,1},{1,0},{2,3},{3,2},{4,5},{5,4},{6,7},{7,6},{8,9},{9,8},{10,11... | collective-permute-start | bytes 196616 | tf_op jit(solution)/shard_map/ppermute | solution.py:210
  29.2 1.6 %collective-permute-start.6 = (f32[64,1088]{1,0:T(8,128)S(1)}, f32[64,1088]{1,0:T(8,128)S(1)}, u32[]{:S(2)}, u32[]{:S(2)}) collective-permute-start(f32[64,1088]{1,0:T(8,128)S(1)} %get-tuple-element.35), channel_id=1, source_target_pairs={{0,4},{4,0},{8,12},{12,8},{1,5},{5,1},{9,13},{13,9},{2,6},{6,2},{1... | collective-permute-start | bytes 835592 | tf_op jit(solution)/shard_map/ppermute | solution.py:210
  30.9 9.1 %collective-permute-start.7 = (f32[64,1088]{1,0:T(8,128)S(1)}, f32[64,1088]{1,0:T(8,128)S(1)}, u32[]{:S(2)}, u32[]{:S(2)}) collective-permute-start(f32[64,1088]{1,0:T(8,128)S(1)} %add.6), channel_id=1, source_target_pairs={{0,8},{4,12},{8,0},{12,4},{1,9},{5,13},{9,1},{13,5},{2,10},{6,14},... | collective-permute-start | bytes 835592 | tf_op jit(solution)/shard_map/ppermute | solution.py:210
  40.1 1.7 %collective-permute-start.8 = (f32[64,1024]{1,0:T(8,128)S(1)}, f32[64,1024]{1,0:T(8,128)S(1)}, u32[]{:S(2)}, u32[]{:S(2)}) collective-permute-start(f32[64,1024]{1,0:T(8,128)S(1)} %slice.9.mine), channel_id=1, source_target_pairs={{0,4},{4,0},{8,12},{12,8},{1,5},{5,1},{9,13},{13,9},{2,6},{6,2},{1... | collective-permute-start | bytes 786440 | tf_op jit(solution)/shard_map/ppermute | solution.py:210

commit v5 on v4

--- a/solution.py
+++ b/solution.py
@@ -12,6 +12,7 @@
 BF16 = jnp.bfloat16
 VMEM = pl.BlockSpec(memory_space=pltpu.VMEM)
 HBM = pl.BlockSpec(memory_space=pltpu.HBM)
+SMEM = pl.BlockSpec(memory_space=pltpu.SMEM)
 VMEM_BYTES = 16 << 20
 
 
@@ -60,10 +61,10 @@
 
 
 def anchor_pass(
-    axis, hours, live, anchors, dests, dest_factor, hour_factor, values, hour_gram, values_buf, scale_rows, *refs,
+    dest_axis, orig_axis, hours, live, anchors, dests, dest_factor, hour_factor, values, anchors_s, dests_s, hour_gram, values_buf,
+    scale_rows, *refs,
 ):
-    parts, refs = refs[:-10], refs[-10:]
-    (sums, dest_buf, hour_buf, hour_rows, hours_s, live_s, anchors_s, dests_s, sems, small_sems) = refs
+    *parts, sums, gram, dest_buf, hour_buf, hour_rows, hours_s, live_s, sems, small_sems = refs
     tiles, slots, tile_size, _ = values_buf.shape
     part_rows = parts[0].shape[0]
     rank, width = sums.shape
@@ -82,9 +83,11 @@
         copy.wait()
     hour_rows[...] = hour_buf[...].T
     hour_gram[...] = gram_of(hour_buf[...])
-    gram = gram_of(dest_buf[...])
+    gram[...] = gram_of(dest_buf[...])
+    core = lax.rem(lax.axis_index(orig_axis), 2)
+    first_row = pl.multiple_of(core * (rank // 2), part_rows)
     packed = jnp.concatenate(
-        [gram[c * part_rows : (c + 1) * part_rows] for c in range(rank // part_rows)], axis=1
+        [gram[pl.ds(first_row + at, part_rows), :] for at in range(0, rank // 2, part_rows)], axis=1
     )
     for part in parts:
         part[:, width:] = packed
@@ -111,7 +114,7 @@
         sums[:, pl.ds(anchor_at, tile_size)] += term.T
         if t + 1 < tiles:
             weights = weights_of(t + 1)
-    me = lax.axis_index(axis)
+    me = lax.axis_index(dest_axis)
     for k, part in enumerate(parts):
         at = pl.multiple_of(jnp.bitwise_xor(me, k) * part_rows, part_rows)
         part[:, :width] = sums[pl.ds(at, part_rows), :]
@@ -133,26 +136,23 @@
             spread[t, s] = jnp.broadcast_to(columns[:, s : s + 1], (rank, tile_size))
 
 
-def dest_gram_inverse(packed, hour_gram, inverse):
-    part_rows, width = packed.shape
+def dest_gram_inverse(axis, mine, other, hour_gram, inverse, gram):
+    part_rows, width = mine.shape
     rank = hour_gram.shape[0]
-    gram = jnp.concatenate([packed[:, c * rank : (c + 1) * rank] for c in range(width // rank)], axis=0)
-    inverse[...] = spd_inverse(gram * hour_gram[...])
-
-
-def dest_pass(dest_axis, orig_axis, anchors, dests, values, spread, gram_inverse, *refs):
-    pieces, refs = refs[:-10], refs[-10:]
-    anchor_factor, kept, sent, sums, halves, factor, anchors_s, dests_s, small_sems, out_sem = refs
+    core = lax.rem(lax.axis_index(axis), 2)
+    for at, packed in ((core, mine), (1 - core, other)):
+        for c in range(width // rank):
+            row = pl.multiple_of(at * (rank // 2) + c * part_rows, part_rows)
+            gram[pl.ds(row, part_rows), :] = packed[:, c * rank : (c + 1) * rank]
+    inverse[...] = spd_inverse(gram[...] * hour_gram[...])
+
+
+def dest_pass(dest_axis, orig_axis, anchors_s, dests_s, values, spread, gram_inverse, *refs):
+    *pieces, anchor_factor, kept, sent, sums, halves, factor, out_sem = refs
     tiles, slots, tile_size, _ = values.shape
     rank, width = sums.shape
     half = halves.shape[2]
     half_tiles = half // tile_size
-    small_copies = [
-        pltpu.make_async_copy(anchors, anchors_s, small_sems.at[0]),
-        pltpu.make_async_copy(dests, dests_s, small_sems.at[1]),
-    ]
-    for copy in small_copies:
-        copy.start()
     me = lax.axis_index(dest_axis)
     core = lax.rem(lax.axis_index(orig_axis), 2)
     part_rows = pieces[0].shape[0]
@@ -167,8 +167,6 @@
     kept[:, half:] = gram
     sent[:, half:] = gram
     halves[...] = jnp.zeros_like(halves)
-    for copy in small_copies:
-        copy.wait()
     for t in range(tiles):
         anchor_at = pl.multiple_of(anchors_s[0, 0, t] * tile_size, tile_size)
         dest = dests_s[0, 0, t]
@@ -220,6 +218,10 @@
     return pltpu.with_memory_space_constraint(array, pltpu.HBM)
 
 
+def in_smem(array):
+    return pltpu.with_memory_space_constraint(array, pltpu.SMEM)
+
+
 def in_vmem(array):
     return pltpu.with_memory_space_constraint(array, pltpu.VMEM)
 
@@ -246,31 +248,34 @@
         hour_count = hour_factor.shape[1]
         width = OB * tile_size
         part_rows = rank // dest_count
+        packed_width = dest_count // 2 * rank
         half = dest_width // 2
         square = jax.ShapeDtypeStruct((rank, rank), F32)
-        index_scratch = [pltpu.SMEM((1, 1, tiles), jnp.int32)] * 2
         hours = in_hbm(tile_hours.reshape(tiles, 1, slots))
         live, anchors, dests = (in_hbm(index) for index in (tile_live, tile_anchor, tile_dest))
-        hour_gram, values, scale_rows, *parts = call(
-            functools.partial(anchor_pass, "dest"),
+        anchors, dests, hour_gram, values, scale_rows, *parts = call(
+            functools.partial(anchor_pass, "dest", "orig"),
             (
+                pltpu.SMEM(anchors.shape, jnp.int32),
+                pltpu.SMEM(dests.shape, jnp.int32),
                 square,
                 pltpu.VMEM(values.shape, BF16),
                 jax.ShapeDtypeStruct((tiles, slots, rank), F32),
-                *[jax.ShapeDtypeStruct((part_rows, width + dest_count * rank), F32)] * dest_count,
+                *[jax.ShapeDtypeStruct((part_rows, width + packed_width), F32)] * dest_count,
             ),
             [HBM] * 7,
             [
                 pltpu.VMEM((rank, width), F32),
+                pltpu.VMEM((rank, rank), F32),
                 pltpu.VMEM((rank, dest_width), F32),
                 pltpu.VMEM((rank, hour_count), F32),
                 pltpu.VMEM((hour_count, rank), F32),
                 pltpu.SMEM((tiles, 1, slots), jnp.int32),
-                *index_scratch,
-                *index_scratch[:1],
+                pltpu.SMEM(live.shape, jnp.int32),
                 pltpu.SemaphoreType.DMA((tiles,)),
                 pltpu.SemaphoreType.DMA((6,)),
             ],
+            (SMEM, SMEM, *[VMEM] * (3 + dest_count)),
         )(hours, live, anchors, dests, in_hbm(dest_factor_in), in_hbm(hour_factor), in_hbm(values))
         spread = call(spread_scales, pltpu.VMEM((tiles, slots, rank, tile_size), F32), [VMEM])(scale_rows)
         parts = parts[:1] + [swap(parts[k], "dest", dest_count, k) for k in range(1, dest_count)]
@@ -279,12 +284,14 @@
             add_parts,
             (
                 jax.ShapeDtypeStruct((part_rows, width), F32),
-                jax.ShapeDtypeStruct((part_rows, dest_count * rank), F32),
+                jax.ShapeDtypeStruct((part_rows, packed_width), F32),
             ),
             [VMEM] * dest_count,
         )(*parts)
         pieces = [piece] + [swap(piece, "dest", dest_count, k) for k in range(1, dest_count)]
-        dest_inverse = call(dest_gram_inverse, square, [VMEM] * 2)(packed, hour_gram)
+        dest_inverse = call(
+            functools.partial(dest_gram_inverse, "orig"), square, [VMEM] * 3, [pltpu.VMEM((rank, rank), F32)]
+        )(packed, swap(packed, "orig", orig_count, 1), hour_gram)
 
         anchor_factor, kept, sent = call(
             functools.partial(dest_pass, "dest", "orig"),
@@ -292,17 +299,15 @@
                 jax.ShapeDtypeStruct((rank, width), F32),
                 *[jax.ShapeDtypeStruct((rank, half + rank), F32)] * 2,
             ),
-            [HBM] * 2 + [VMEM] * (3 + dest_count),
+            [SMEM] * 2 + [VMEM] * (3 + dest_count),
             [
                 pltpu.VMEM((rank, width), F32),
                 pltpu.VMEM((2, rank, half), F32),
                 pltpu.VMEM((rank, width), F32),
-                *index_scratch,
-                pltpu.SemaphoreType.DMA((2,)),
                 pltpu.SemaphoreType.DMA,
             ],
             (HBM, VMEM, VMEM),
-        )(anchors, dests, in_vmem(values), in_vmem(spread), dest_inverse, *pieces)
+        )(in_smem(anchors), in_smem(dests), in_vmem(values), in_vmem(spread), dest_inverse, *pieces)
 
         mine = kept + swap(sent, "orig", orig_count, 1)
         distance = 2

time: 43.1 us -> 42.2 us (0.979)
  waiting for transfers between devices: 15.1 us -> 14.3 us
    ppermute x9 -> x10, waiting for transfers between devices: 15.1 us -> 14.3 us  [swap(): return lax.ppermute(array, axis, [(i, i ^ distance) for i in range(count)])]
    ppermute x9 -> x10, starting transfers between devices: 11.8 us -> 11.9 us  [swap(): return lax.ppermute(array, axis, [(i, i ^ distance) for i in range(count)])]
  transfers between devices with their start and end apart: 9 -> 10, of which waited for: 5 -> 6; matrix products, arithmetic and copies ran while one was open for 0% -> 0% of each run, Pallas kernels for 14% -> 15%
where the time goes in v5:
time: 42.2 us; the launch traced here: 42 us
  Pallas kernels  15 us (36%)
  waiting for transfers between devices  14.3 us (34%)
  starting transfers between devices  11.9 us (28%)
  between operations  0.73 us (2%)
    ppermute x10, waiting for transfers between devices, swap(): return lax.ppermute(array, axis, [(i, i ^ distance) for i in range(count)])  14.3 us
    ppermute x10, starting transfers between devices, swap(): return lax.ppermute(array, axis, [(i, i ^ distance) for i in range(count)])  11.9 us
    pallas_call x1, Pallas kernels, shards(): call(functools.partial(anchor_pass, 'dest', 'orig'), (pltpu.SMEM(anchors....  5.3 us
    pallas_call x1, Pallas kernels, shards(): call(spread_scales, pltpu.VMEM((tiles, slots, rank, tile_size), F32), [VM...  3.07 us
    pallas_call x1, Pallas kernels, shards(): call(functools.partial(dest_pass, 'dest', 'orig'), (jax.ShapeDtypeStruct(...  2.43 us
    pallas_call x1, Pallas kernels, shards(): call(anchor_gram_inverse, square, [VMEM] * 2)(gram, hour_gram)  1.62 us
    pallas_call x1, Pallas kernels, shards(): call(functools.partial(dest_gram_inverse, 'orig'), square, [VMEM] * 3, [p...  1.52 us
    pallas_call x1, Pallas kernels, shards(): call(functools.partial(dest_solve, 'orig'), jax.ShapeDtypeStruct((rank, d...  1.06 us
  transfers between devices with their start and end apart: 10, of which 6 were waited for; matrix products, arithmetic and copies ran while one was open for 0% of the time, Pallas kernels for 15%

profile of v5, /device:TPU:0, one launch (start us, length us, event | category | flops | bytes accessed | tf_op | source)
XLA Modules:
  0.0 42.0 jit_solution(16500287254857144900)
XLA Ops:
  0.6 5.3 %shard_map.86 = (s32[1,1,12]{2,1,0:T(1,128)S(4)}, s32[1,1,12]{2,1,0:T(1,128)S(4)}, f32[64,64]{1,0:T(8,128)S(1)}, bf16[12,24,128,128]{3,2,1,0:T(8,128)(2,1)S(1)},...) custom-call(s32[12,1,24]{2,1,0:T(1,128)} %bitcast.3, ...), custom_call_target="tpu_custom_call" | custom-call | tf_op jit(solution)/shard_map/pallas_call | solution.py:256
  5.9 3.1 %collective-permute-start = (f32[16,1152]{1,0:T(8,128)S(1)}, f32[16,1152]{1,0:T(8,128)S(1)}, u32[]{:S(2)}, u32[]{:S(2)}) collective-permute-start(f32[16,1152]{1,0:T(8,128)S(1)} %get-tuple-element.25), channel_id=1, source_target_pairs={{0,1},{1,0},{2,3},{3,2},{4,5},{5,4},{6,7},{7,6},{8,9},{9,8},{10,11... | collective-permute-start | bytes 221192 | tf_op jit(solution)/shard_map/ppermute | solution.py:208
  9.0 2.6 %collective-permute-start.1 = (f32[16,1152]{1,0:T(8,128)S(1)}, f32[16,1152]{1,0:T(8,128)S(1)}, u32[]{:S(2)}, u32[]{:S(2)}) collective-permute-start(f32[16,1152]{1,0:T(8,128)S(1)} %get-tuple-element.26), channel_id=1, source_target_pairs={{0,2},{1,3},{2,0},{3,1},{4,6},{5,7},{6,4},{7,5},{8,10},{9,11},{10,... | collective-permute-start | bytes 221192 | tf_op jit(solution)/shard_map/ppermute | solution.py:208
  11.6 0.0 collective-permute-start.2
  11.6 3.1 %shard_map.87.spread = f32[12,24,64,128]{3,2,1,0:T(8,128)S(1)} custom-call(f32[12,24,64]{2,1,0:T(8,128)S(1)} %get-tuple-element.28.scale_rows), custom_call_target="tpu_custom_call" | custom-call | tf_op jit(solution)/shard_map/pallas_call | solution.py:280
  14.7 0.0 collective-permute-done.refs_1_
  14.7 2.1 %collective-permute-done.1.refs_2_ = f32[16,1152]{1,0:T(8,128)S(1)} collective-permute-done((f32[16,1152]{1,0:T(8,128)S(1)}, f32[16,1152]{1,0:T(8,128)S(1)}, u32[]{:S(2)}, u32[]{:S(2)}) %collective-permute-start.1) | collective-permute-done | bytes 73760 | tf_op jit(solution)/shard_map/ppermute | solution.py:208
  16.8 1.1 %collective-permute-done.2.refs_3_ = f32[16,1152]{1,0:T(8,128)S(1)} collective-permute-done((f32[16,1152]{1,0:T(8,128)S(1)}, f32[16,1152]{1,0:T(8,128)S(1)}, u32[]{:S(2)}, u32[]{:S(2)}) %collective-permute-start.2) | collective-permute-done | bytes 73760 | tf_op jit(solution)/shard_map/ppermute | solution.py:208
  17.9 2.3 %collective-permute-start.6 = (f32[16,1024]{1,0:T(8,128)S(1)}, f32[16,1024]{1,0:T(8,128)S(1)}, u32[]{:S(2)}, u32[]{:S(2)}) collective-permute-start(f32[16,1024]{1,0:T(8,128)S(1)} %get-tuple-element.36.refs_0_), channel_id=1, source_target_pairs={{0,3},{1,2},{2,1},{3,0},{4,7},{5,6},{6,5},{7,4},{8,11},{9,10},{10,... | collective-permute-start | bytes 196616 | tf_op jit(solution)/shard_map/ppermute | solution.py:208
  20.2 0.3 collective-permute-start.5
  20.5 1.8 %collective-permute-start.4 = (f32[16,1024]{1,0:T(8,128)S(1)}, f32[16,1024]{1,0:T(8,128)S(1)}, u32[]{:S(2)}, u32[]{:S(2)}) collective-permute-start(f32[16,1024]{1,0:T(8,128)S(1)} %get-tuple-element.36.refs_0_), channel_id=1, source_target_pairs={{0,1},{1,0},{2,3},{3,2},{4,5},{5,4},{6,7},{7,6},{8,9},{9,8},{10,11... | collective-permute-start | bytes 196616 | tf_op jit(solution)/shard_map/ppermute | solution.py:208
  22.4 0.0 collective-permute-start.3
  22.4 1.2 %collective-permute-done.3.other = f32[16,128]{1,0:T(8,128)S(1)} collective-permute-done((f32[16,128]{1,0:T(8,128)S(1)}, f32[16,128]{1,0:T(8,128)S(1)}, u32[]{:S(2)}, u32[]{:S(2)}) %collective-permute-start.3) | collective-permute-done | bytes 8224 | tf_op jit(solution)/shard_map/ppermute | solution.py:208
  23.5 1.5 %shard_map.89.gram_inverse = f32[64,64]{1,0:T(8,128)S(1)} custom-call(f32[16,128]{1,0:T(8,128)S(1)} %get-tuple-element.34.mine, f32[16,128]{1,0:T(8,128)S(1)} %collective-permute-done.3.other, f32[64,64]{1,0:T(8,128)S(1)} %get-tuple-element.35.hour_gram), custom_call_target="tpu_custom_call" | custom-call | tf_op jit(solution)/shard_map/pallas_call | solution.py:292
  25.1 0.0 collective-permute-done.6.refs_3_
  25.1 0.9 %collective-permute-done.5.refs_2_ = f32[16,1024]{1,0:T(8,128)S(1)} collective-permute-done((f32[16,1024]{1,0:T(8,128)S(1)}, f32[16,1024]{1,0:T(8,128)S(1)}, u32[]{:S(2)}, u32[]{:S(2)}) %collective-permute-start.5) | collective-permute-done | bytes 65568 | tf_op jit(solution)/shard_map/ppermute | solution.py:208
  25.9 0.0 collective-permute-done.4.refs_1_
  25.9 2.4 %shard_map.90 = (f32[64,1024]{1,0:T(8,128)}, f32[64,1088]{1,0:T(8,128)S(1)}, f32[64,1088]{1,0:T(8,128)S(1)}) custom-call(s32[1,1,12]{2,1,0:T(1,128)S(4)} %get-tuple-element.21.anchors_s, s32[1,1,12]{2,1,0:T(1,128)S(4)} %get-tuple-element.22.dests_s, bf16[12,24,128,128]{3,2,1,0:T(8,128)(2,1)S(1)} %get-tuple-element.23.values, ...), custom_call_target="tpu_custom_call" | custom-call | tf_op jit(solution)/shard_map/pallas_call | solution.py:296
  28.4 0.1 collective-permute-start.7
  28.4 1.6 %collective-permute-done.7 = f32[64,1088]{1,0:T(8,128)S(1)} collective-permute-done((f32[64,1088]{1,0:T(8,128)S(1)}, f32[64,1088]{1,0:T(8,128)S(1)}, u32[]{:S(2)}, u32[]{:S(2)}) %collective-permute-start.7) | collective-permute-done | bytes 278560 | tf_op jit(solution)/shard_map/ppermute | solution.py:208
  30.1 1.6 %collective-permute-start.8 = (f32[64,1088]{1,0:T(8,128)S(1)}, f32[64,1088]{1,0:T(8,128)S(1)}, u32[]{:S(2)}, u32[]{:S(2)}) collective-permute-start(f32[64,1088]{1,0:T(8,128)S(1)} %add.6), channel_id=1, source_target_pairs={{0,8},{4,12},{8,0},{12,4},{1,9},{5,13},{9,1},{13,5},{2,10},{6,14},... | collective-permute-start | bytes 835592 | tf_op jit(solution)/shard_map/ppermute | solution.py:208
  31.6 7.5 %collective-permute-done.8 = f32[64,1088]{1,0:T(8,128)S(1)} collective-permute-done((f32[64,1088]{1,0:T(8,128)S(1)}, f32[64,1088]{1,0:T(8,128)S(1)}, u32[]{:S(2)}, u32[]{:S(2)}) %collective-permute-start.8) | collective-permute-done | bytes 278560 | tf_op jit(solution)/shard_map/ppermute | solution.py:208
  39.2 0.1 collective-permute-start.9
  39.3 1.6 %shard_map.91.gram_inverse = f32[64,64]{1,0:T(8,128)S(1)} custom-call(f32[64,64]{1,0:T(8,128)S(1)} %slice.8.gram, f32[64,64]{1,0:T(8,128)S(1)} %get-tuple-element.35.hour_gram), custom_call_target="tpu_custom_call" | custom-call | tf_op jit(solution)/shard_map/pallas_call | solution.py:318
  40.9 0.0 collective-permute-done.9.other
  41.0 1.1 %shard_map.92 = f32[64,2048]{1,0:T(8,128)} custom-call(f32[64,64]{1,0:T(8,128)S(1)} %shard_map.91.gram_inverse, f32[64,1024]{1,0:T(8,128)S(1)} %slice.9.mine, f32[64,1024]{1,0:T(8,128)S(1)} %collective-permute-done.9.other), custom_call_target="tpu_custom_call" | custom-call | tf_op jit(solution)/shard_map/pallas_call | solution.py:320
  (5 shorter events, 0.1 us)
Async XLA Ops:
  5.9 8.8 %collective-permute-start = (f32[16,1152]{1,0:T(8,128)S(1)}, f32[16,1152]{1,0:T(8,128)S(1)}, u32[]{:S(2)}, u32[]{:S(2)}) collective-permute-start(f32[16,1152]{1,0:T(8,128)S(1)} %get-tuple-element.25), channel_id=1, source_target_pairs={{0,1},{1,0},{2,3},{3,2},{4,5},{5,4},{6,7},{7,6},{8,9},{9,8},{10,11... | collective-permute-start | bytes 221192 | tf_op jit(solution)/shard_map/ppermute | solution.py:208
  9.0 7.8 %collective-permute-start.1 = (f32[16,1152]{1,0:T(8,128)S(1)}, f32[16,1152]{1,0:T(8,128)S(1)}, u32[]{:S(2)}, u32[]{:S(2)}) collective-permute-start(f32[16,1152]{1,0:T(8,128)S(1)} %get-tuple-element.26), channel_id=1, source_target_pairs={{0,2},{1,3},{2,0},{3,1},{4,6},{5,7},{6,4},{7,5},{8,10},{9,11},{10,... | collective-permute-start | bytes 221192 | tf_op jit(solution)/shard_map/ppermute | solution.py:208
  11.6 6.3 %collective-permute-start.2 = (f32[16,1152]{1,0:T(8,128)S(1)}, f32[16,1152]{1,0:T(8,128)S(1)}, u32[]{:S(2)}, u32[]{:S(2)}) collective-permute-start(f32[16,1152]{1,0:T(8,128)S(1)} %get-tuple-element.27), channel_id=1, source_target_pairs={{0,3},{1,2},{2,1},{3,0},{4,7},{5,6},{6,5},{7,4},{8,11},{9,10},{10,... | collective-permute-start | bytes 221192 | tf_op jit(solution)/shard_map/ppermute | solution.py:208
  17.9 7.2 %collective-permute-start.6 = (f32[16,1024]{1,0:T(8,128)S(1)}, f32[16,1024]{1,0:T(8,128)S(1)}, u32[]{:S(2)}, u32[]{:S(2)}) collective-permute-start(f32[16,1024]{1,0:T(8,128)S(1)} %get-tuple-element.36.refs_0_), channel_id=1, source_target_pairs={{0,3},{1,2},{2,1},{3,0},{4,7},{5,6},{6,5},{7,4},{8,11},{9,10},{10,... | collective-permute-start | bytes 196616 | tf_op jit(solution)/shard_map/ppermute | solution.py:208
  20.2 5.8 %collective-permute-start.5 = (f32[16,1024]{1,0:T(8,128)S(1)}, f32[16,1024]{1,0:T(8,128)S(1)}, u32[]{:S(2)}, u32[]{:S(2)}) collective-permute-start(f32[16,1024]{1,0:T(8,128)S(1)} %get-tuple-element.36.refs_0_), channel_id=1, source_target_pairs={{0,2},{1,3},{2,0},{3,1},{4,6},{5,7},{6,4},{7,5},{8,10},{9,11},{10,... | collective-permute-start | bytes 196616 | tf_op jit(solution)/shard_map/ppermute | solution.py:208
  20.5 5.4 %collective-permute-start.4 = (f32[16,1024]{1,0:T(8,128)S(1)}, f32[16,1024]{1,0:T(8,128)S(1)}, u32[]{:S(2)}, u32[]{:S(2)}) collective-permute-start(f32[16,1024]{1,0:T(8,128)S(1)} %get-tuple-element.36.refs_0_), channel_id=1, source_target_pairs={{0,1},{1,0},{2,3},{3,2},{4,5},{5,4},{6,7},{7,6},{8,9},{9,8},{10,11... | collective-permute-start | bytes 196616 | tf_op jit(solution)/shard_map/ppermute | solution.py:208
  22.4 1.2 %collective-permute-start.3 = (f32[16,128]{1,0:T(8,128)S(1)}, f32[16,128]{1,0:T(8,128)S(1)}, u32[]{:S(2)}, u32[]{:S(2)}) collective-permute-start(f32[16,128]{1,0:T(8,128)S(1)} %get-tuple-element.34.mine), channel_id=1, source_target_pairs={{0,4},{4,0},{8,12},{12,8},{1,5},{5,1},{9,13},{13,9},{2,6},{6,2},{1... | collective-permute-start | bytes 24584 | tf_op jit(solution)/shard_map/ppermute | solution.py:208
  28.4 1.6 %collective-permute-start.7 = (f32[64,1088]{1,0:T(8,128)S(1)}, f32[64,1088]{1,0:T(8,128)S(1)}, u32[]{:S(2)}, u32[]{:S(2)}) collective-permute-start(f32[64,1088]{1,0:T(8,128)S(1)} %get-tuple-element.39), channel_id=1, source_target_pairs={{0,4},{4,0},{8,12},{12,8},{1,5},{5,1},{9,13},{13,9},{2,6},{6,2},{1... | collective-permute-start | bytes 835592 | tf_op jit(solution)/shard_map/ppermute | solution.py:208
  30.1 9.1 %collective-permute-start.8 = (f32[64,1088]{1,0:T(8,128)S(1)}, f32[64,1088]{1,0:T(8,128)S(1)}, u32[]{:S(2)}, u32[]{:S(2)}) collective-permute-start(f32[64,1088]{1,0:T(8,128)S(1)} %add.6), channel_id=1, source_target_pairs={{0,8},{4,12},{8,0},{12,4},{1,9},{5,13},{9,1},{13,5},{2,10},{6,14},... | collective-permute-start | bytes 835592 | tf_op jit(solution)/shard_map/ppermute | solution.py:208
  39.2 1.7 %collective-permute-start.9 = (f32[64,1024]{1,0:T(8,128)S(1)}, f32[64,1024]{1,0:T(8,128)S(1)}, u32[]{:S(2)}, u32[]{:S(2)}) collective-permute-start(f32[64,1024]{1,0:T(8,128)S(1)} %slice.9.mine), channel_id=1, source_target_pairs={{0,4},{4,0},{8,12},{12,8},{1,5},{5,1},{9,13},{13,9},{2,6},{6,2},{1... | collective-permute-start | bytes 786440 | tf_op jit(solution)/shard_map/ppermute | solution.py:208

commit v6 on v5

--- a/solution.py
+++ b/solution.py
@@ -164,8 +164,9 @@
     out_copy = pltpu.make_async_copy(factor, anchor_factor, out_sem)
     out_copy.start()
     gram = gram_of(solved)
-    kept[:, half:] = gram
-    sent[:, half:] = gram
+    packed = jnp.concatenate([gram[: rank // 2], gram[rank // 2 :]], axis=1)
+    kept[:, 2 * half :] = packed
+    sent[:, 2 * half :] = packed
     halves[...] = jnp.zeros_like(halves)
     for t in range(tiles):
         anchor_at = pl.multiple_of(anchors_s[0, 0, t] * tile_size, tile_size)
@@ -176,13 +177,15 @@
         term = jnp.dot(weights, tile, preferred_element_type=F32)
         dest_at = pl.multiple_of(lax.rem(dest, half_tiles) * tile_size, tile_size)
         halves[dest // half_tiles, :, pl.ds(dest_at, tile_size)] += term
-    kept[:, :half] = halves[core]
-    sent[:, :half] = halves[1 - core]
+    for block, at in ((kept, core), (sent, 1 - core)):
+        block[:, :half] = halves[at, : rank // 2]
+        block[:, half : 2 * half] = halves[at, rank // 2 :]
     out_copy.wait()
 
 
 def anchor_gram_inverse(gram, hour_gram, inverse):
-    total = gram[...]
+    rank = hour_gram.shape[0]
+    total = jnp.concatenate([gram[:, :rank], gram[:, rank:]], axis=0)
     rows = lax.broadcasted_iota(jnp.int32, total.shape, 0)
     cols = lax.broadcasted_iota(jnp.int32, total.shape, 1)
     diagonal = jnp.where(rows == cols, total, 0.0)
@@ -192,11 +195,12 @@
 
 
 def dest_solve(axis, gram_inverse, mine, other, dest_factor, solved, sems):
-    half = mine.shape[1]
+    half = mine.shape[1] // 2
     core = lax.rem(lax.axis_index(axis), 2)
     copies = []
     for i, (at, piece) in enumerate(((core, mine), (1 - core, other))):
-        solved[i] = solve_with(gram_inverse[...], piece[...])
+        right_side = jnp.concatenate([piece[:, :half], piece[:, half:]], axis=0)
+        solved[i] = solve_with(gram_inverse[...], right_side)
         columns = pl.ds(pl.multiple_of(at * half, half), half)
         copies.append(pltpu.make_async_copy(solved.at[i], dest_factor.at[:, columns], sems.at[i]))
         copies[i].start()
@@ -297,7 +301,7 @@
             functools.partial(dest_pass, "dest", "orig"),
             (
                 jax.ShapeDtypeStruct((rank, width), F32),
-                *[jax.ShapeDtypeStruct((rank, half + rank), F32)] * 2,
+                *[jax.ShapeDtypeStruct((rank // 2, 2 * half + 2 * rank), F32)] * 2,
             ),
             [SMEM] * 2 + [VMEM] * (3 + dest_count),
             [
@@ -314,7 +318,7 @@
         while distance < orig_count:
             mine = mine + swap(mine, "orig", orig_count, distance)
             distance *= 2
-        sums, gram = mine[:, :half], mine[:, half:]
+        sums, gram = mine[:, : 2 * half], mine[:, 2 * half :]
         anchor_inverse = call(anchor_gram_inverse, square, [VMEM] * 2)(gram, hour_gram)
         other = swap(sums, "orig", orig_count, 1)
         dest_factor = call(

time: 42.2 us -> 41.8 us (level)
  no operation moved by 1% of the time
where the time goes in v6:
time: 41.8 us; the launch traced here: 41.6 us
  Pallas kernels  15 us (36%)
  waiting for transfers between devices  14 us (33%)
  starting transfers between devices  11.8 us (28%)
  between operations  0.73 us (2%)
    ppermute x10, waiting for transfers between devices, swap(): return lax.ppermute(array, axis, [(i, i ^ distance) for i in range(count)])  14 us
    ppermute x10, starting transfers between devices, swap(): return lax.ppermute(array, axis, [(i, i ^ distance) for i in range(count)])  11.8 us
    pallas_call x1, Pallas kernels, shards(): call(functools.partial(anchor_pass, 'dest', 'orig'), (pltpu.SMEM(anchors....  5.3 us
    pallas_call x1, Pallas kernels, shards(): call(spread_scales, pltpu.VMEM((tiles, slots, rank, tile_size), F32), [VM...  3.07 us
    pallas_call x1, Pallas kernels, shards(): call(functools.partial(dest_pass, 'dest', 'orig'), (jax.ShapeDtypeStruct(...  2.43 us
    pallas_call x1, Pallas kernels, shards(): call(anchor_gram_inverse, square, [VMEM] * 2)(gram, hour_gram)  1.61 us
    pallas_call x1, Pallas kernels, shards(): call(functools.partial(dest_gram_inverse, 'orig'), square, [VMEM] * 3, [p...  1.52 us
    pallas_call x1, Pallas kernels, shards(): call(functools.partial(dest_solve, 'orig'), jax.ShapeDtypeStruct((rank, d...  1.06 us
  transfers between devices with their start and end apart: 10, of which 6 were waited for; matrix products, arithmetic and copies ran while one was open for 0% of the time, Pallas kernels for 15%

profile of v6, /device:TPU:0, one launch (start us, length us, event | category | flops | bytes accessed | tf_op | source)
XLA Modules:
  0.0 41.6 jit_solution(3373359392870897556)
XLA Ops:
  0.6 5.3 %shard_map.86 = (s32[1,1,12]{2,1,0:T(1,128)S(4)}, s32[1,1,12]{2,1,0:T(1,128)S(4)}, f32[64,64]{1,0:T(8,128)S(1)}, bf16[12,24,128,128]{3,2,1,0:T(8,128)(2,1)S(1)},...) custom-call(s32[12,1,24]{2,1,0:T(1,128)} %bitcast.3, ...), custom_call_target="tpu_custom_call" | custom-call | tf_op jit(solution)/shard_map/pallas_call | solution.py:260
  5.9 3.1 %collective-permute-start = (f32[16,1152]{1,0:T(8,128)S(1)}, f32[16,1152]{1,0:T(8,128)S(1)}, u32[]{:S(2)}, u32[]{:S(2)}) collective-permute-start(f32[16,1152]{1,0:T(8,128)S(1)} %get-tuple-element.25), channel_id=1, source_target_pairs={{0,1},{1,0},{2,3},{3,2},{4,5},{5,4},{6,7},{7,6},{8,9},{9,8},{10,11... | collective-permute-start | bytes 221192 | tf_op jit(solution)/shard_map/ppermute | solution.py:212
  9.0 2.6 %collective-permute-start.1 = (f32[16,1152]{1,0:T(8,128)S(1)}, f32[16,1152]{1,0:T(8,128)S(1)}, u32[]{:S(2)}, u32[]{:S(2)}) collective-permute-start(f32[16,1152]{1,0:T(8,128)S(1)} %get-tuple-element.26), channel_id=1, source_target_pairs={{0,2},{1,3},{2,0},{3,1},{4,6},{5,7},{6,4},{7,5},{8,10},{9,11},{10,... | collective-permute-start | bytes 221192 | tf_op jit(solution)/shard_map/ppermute | solution.py:212
  11.6 0.0 collective-permute-start.2
  11.6 3.1 %shard_map.87.spread = f32[12,24,64,128]{3,2,1,0:T(8,128)S(1)} custom-call(f32[12,24,64]{2,1,0:T(8,128)S(1)} %get-tuple-element.28.scale_rows), custom_call_target="tpu_custom_call" | custom-call | tf_op jit(solution)/shard_map/pallas_call | solution.py:284
  14.7 0.0 collective-permute-done.refs_1_
  14.7 2.1 %collective-permute-done.1.refs_2_ = f32[16,1152]{1,0:T(8,128)S(1)} collective-permute-done((f32[16,1152]{1,0:T(8,128)S(1)}, f32[16,1152]{1,0:T(8,128)S(1)}, u32[]{:S(2)}, u32[]{:S(2)}) %collective-permute-start.1) | collective-permute-done | bytes 73760 | tf_op jit(solution)/shard_map/ppermute | solution.py:212
  16.8 1.1 %collective-permute-done.2.refs_3_ = f32[16,1152]{1,0:T(8,128)S(1)} collective-permute-done((f32[16,1152]{1,0:T(8,128)S(1)}, f32[16,1152]{1,0:T(8,128)S(1)}, u32[]{:S(2)}, u32[]{:S(2)}) %collective-permute-start.2) | collective-permute-done | bytes 73760 | tf_op jit(solution)/shard_map/ppermute | solution.py:212
  17.9 2.3 %collective-permute-start.6 = (f32[16,1024]{1,0:T(8,128)S(1)}, f32[16,1024]{1,0:T(8,128)S(1)}, u32[]{:S(2)}, u32[]{:S(2)}) collective-permute-start(f32[16,1024]{1,0:T(8,128)S(1)} %get-tuple-element.36.refs_0_), channel_id=1, source_target_pairs={{0,3},{1,2},{2,1},{3,0},{4,7},{5,6},{6,5},{7,4},{8,11},{9,10},{10,... | collective-permute-start | bytes 196616 | tf_op jit(solution)/shard_map/ppermute | solution.py:212
  20.2 0.3 collective-permute-start.5
  20.5 1.8 %collective-permute-start.4 = (f32[16,1024]{1,0:T(8,128)S(1)}, f32[16,1024]{1,0:T(8,128)S(1)}, u32[]{:S(2)}, u32[]{:S(2)}) collective-permute-start(f32[16,1024]{1,0:T(8,128)S(1)} %get-tuple-element.36.refs_0_), channel_id=1, source_target_pairs={{0,1},{1,0},{2,3},{3,2},{4,5},{5,4},{6,7},{7,6},{8,9},{9,8},{10,11... | collective-permute-start | bytes 196616 | tf_op jit(solution)/shard_map/ppermute | solution.py:212
  22.4 0.0 collective-permute-start.3
  22.4 1.2 %collective-permute-done.3.other = f32[16,128]{1,0:T(8,128)S(1)} collective-permute-done((f32[16,128]{1,0:T(8,128)S(1)}, f32[16,128]{1,0:T(8,128)S(1)}, u32[]{:S(2)}, u32[]{:S(2)}) %collective-permute-start.3) | collective-permute-done | bytes 8224 | tf_op jit(solution)/shard_map/ppermute | solution.py:212
  23.5 1.5 %shard_map.89.gram_inverse = f32[64,64]{1,0:T(8,128)S(1)} custom-call(f32[16,128]{1,0:T(8,128)S(1)} %get-tuple-element.34.mine, f32[16,128]{1,0:T(8,128)S(1)} %collective-permute-done.3.other, f32[64,64]{1,0:T(8,128)S(1)} %get-tuple-element.35.hour_gram), custom_call_target="tpu_custom_call" | custom-call | tf_op jit(solution)/shard_map/pallas_call | solution.py:296
  25.1 0.0 collective-permute-done.6.refs_3_
  25.1 0.9 %collective-permute-done.5.refs_2_ = f32[16,1024]{1,0:T(8,128)S(1)} collective-permute-done((f32[16,1024]{1,0:T(8,128)S(1)}, f32[16,1024]{1,0:T(8,128)S(1)}, u32[]{:S(2)}, u32[]{:S(2)}) %collective-permute-start.5) | collective-permute-done | bytes 65568 | tf_op jit(solution)/shard_map/ppermute | solution.py:212
  25.9 0.0 collective-permute-done.4.refs_1_
  25.9 2.4 %shard_map.90 = (f32[64,1024]{1,0:T(8,128)}, f32[32,2176]{1,0:T(8,128)S(1)}, f32[32,2176]{1,0:T(8,128)S(1)}) custom-call(s32[1,1,12]{2,1,0:T(1,128)S(4)} %get-tuple-element.21.anchors_s, s32[1,1,12]{2,1,0:T(1,128)S(4)} %get-tuple-element.22.dests_s, bf16[12,24,128,128]{3,2,1,0:T(8,128)(2,1)S(1)} %get-tuple-element.23.values, ...), custom_call_target="tpu_custom_call" | custom-call | tf_op jit(solution)/shard_map/pallas_call | solution.py:300
  28.4 0.1 collective-permute-start.7
  28.4 1.5 %collective-permute-done.7 = f32[32,2176]{1,0:T(8,128)S(1)} collective-permute-done((f32[32,2176]{1,0:T(8,128)S(1)}, f32[32,2176]{1,0:T(8,128)S(1)}, u32[]{:S(2)}, u32[]{:S(2)}) %collective-permute-start.7) | collective-permute-done | bytes 278560 | tf_op jit(solution)/shard_map/ppermute | solution.py:212
  30.0 1.5 %collective-permute-start.8 = (f32[32,2176]{1,0:T(8,128)S(1)}, f32[32,2176]{1,0:T(8,128)S(1)}, u32[]{:S(2)}, u32[]{:S(2)}) collective-permute-start(f32[32,2176]{1,0:T(8,128)S(1)} %add.6), channel_id=1, source_target_pairs={{0,8},{4,12},{8,0},{12,4},{1,9},{5,13},{9,1},{13,5},{2,10},{6,14},... | collective-permute-start | bytes 835592 | tf_op jit(solution)/shard_map/ppermute | solution.py:212
  31.6 7.2 %collective-permute-done.8 = f32[32,2176]{1,0:T(8,128)S(1)} collective-permute-done((f32[32,2176]{1,0:T(8,128)S(1)}, f32[32,2176]{1,0:T(8,128)S(1)}, u32[]{:S(2)}, u32[]{:S(2)}) %collective-permute-start.8) | collective-permute-done | bytes 278560 | tf_op jit(solution)/shard_map/ppermute | solution.py:212
  38.9 0.1 collective-permute-start.9
  38.9 1.6 %shard_map.91.gram_inverse = f32[64,64]{1,0:T(8,128)S(1)} custom-call(f32[32,128]{1,0:T(8,128)S(1)} %slice.8.gram, f32[64,64]{1,0:T(8,128)S(1)} %get-tuple-element.35.hour_gram), custom_call_target="tpu_custom_call" | custom-call | tf_op jit(solution)/shard_map/pallas_call | solution.py:322
  40.6 0.0 collective-permute-done.9.other
  40.6 1.1 %shard_map.92 = f32[64,2048]{1,0:T(8,128)} custom-call(f32[64,64]{1,0:T(8,128)S(1)} %shard_map.91.gram_inverse, f32[32,2048]{1,0:T(8,128)S(1)} %slice.9.mine, f32[32,2048]{1,0:T(8,128)S(1)} %collective-permute-done.9.other), custom_call_target="tpu_custom_call" | custom-call | tf_op jit(solution)/shard_map/pallas_call | solution.py:324
  (5 shorter events, 0.1 us)
Async XLA Ops:
  5.9 8.8 %collective-permute-start = (f32[16,1152]{1,0:T(8,128)S(1)}, f32[16,1152]{1,0:T(8,128)S(1)}, u32[]{:S(2)}, u32[]{:S(2)}) collective-permute-start(f32[16,1152]{1,0:T(8,128)S(1)} %get-tuple-element.25), channel_id=1, source_target_pairs={{0,1},{1,0},{2,3},{3,2},{4,5},{5,4},{6,7},{7,6},{8,9},{9,8},{10,11... | collective-permute-start | bytes 221192 | tf_op jit(solution)/shard_map/ppermute | solution.py:212
  9.0 7.8 %collective-permute-start.1 = (f32[16,1152]{1,0:T(8,128)S(1)}, f32[16,1152]{1,0:T(8,128)S(1)}, u32[]{:S(2)}, u32[]{:S(2)}) collective-permute-start(f32[16,1152]{1,0:T(8,128)S(1)} %get-tuple-element.26), channel_id=1, source_target_pairs={{0,2},{1,3},{2,0},{3,1},{4,6},{5,7},{6,4},{7,5},{8,10},{9,11},{10,... | collective-permute-start | bytes 221192 | tf_op jit(solution)/shard_map/ppermute | solution.py:212
  11.6 6.3 %collective-permute-start.2 = (f32[16,1152]{1,0:T(8,128)S(1)}, f32[16,1152]{1,0:T(8,128)S(1)}, u32[]{:S(2)}, u32[]{:S(2)}) collective-permute-start(f32[16,1152]{1,0:T(8,128)S(1)} %get-tuple-element.27), channel_id=1, source_target_pairs={{0,3},{1,2},{2,1},{3,0},{4,7},{5,6},{6,5},{7,4},{8,11},{9,10},{10,... | collective-permute-start | bytes 221192 | tf_op jit(solution)/shard_map/ppermute | solution.py:212
  17.9 7.2 %collective-permute-start.6 = (f32[16,1024]{1,0:T(8,128)S(1)}, f32[16,1024]{1,0:T(8,128)S(1)}, u32[]{:S(2)}, u32[]{:S(2)}) collective-permute-start(f32[16,1024]{1,0:T(8,128)S(1)} %get-tuple-element.36.refs_0_), channel_id=1, source_target_pairs={{0,3},{1,2},{2,1},{3,0},{4,7},{5,6},{6,5},{7,4},{8,11},{9,10},{10,... | collective-permute-start | bytes 196616 | tf_op jit(solution)/shard_map/ppermute | solution.py:212
  20.2 5.8 %collective-permute-start.5 = (f32[16,1024]{1,0:T(8,128)S(1)}, f32[16,1024]{1,0:T(8,128)S(1)}, u32[]{:S(2)}, u32[]{:S(2)}) collective-permute-start(f32[16,1024]{1,0:T(8,128)S(1)} %get-tuple-element.36.refs_0_), channel_id=1, source_target_pairs={{0,2},{1,3},{2,0},{3,1},{4,6},{5,7},{6,4},{7,5},{8,10},{9,11},{10,... | collective-permute-start | bytes 196616 | tf_op jit(solution)/shard_map/ppermute | solution.py:212
  20.5 5.4 %collective-permute-start.4 = (f32[16,1024]{1,0:T(8,128)S(1)}, f32[16,1024]{1,0:T(8,128)S(1)}, u32[]{:S(2)}, u32[]{:S(2)}) collective-permute-start(f32[16,1024]{1,0:T(8,128)S(1)} %get-tuple-element.36.refs_0_), channel_id=1, source_target_pairs={{0,1},{1,0},{2,3},{3,2},{4,5},{5,4},{6,7},{7,6},{8,9},{9,8},{10,11... | collective-permute-start | bytes 196616 | tf_op jit(solution)/shard_map/ppermute | solution.py:212
  22.4 1.2 %collective-permute-start.3 = (f32[16,128]{1,0:T(8,128)S(1)}, f32[16,128]{1,0:T(8,128)S(1)}, u32[]{:S(2)}, u32[]{:S(2)}) collective-permute-start(f32[16,128]{1,0:T(8,128)S(1)} %get-tuple-element.34.mine), channel_id=1, source_target_pairs={{0,4},{4,0},{8,12},{12,8},{1,5},{5,1},{9,13},{13,9},{2,6},{6,2},{1... | collective-permute-start | bytes 24584 | tf_op jit(solution)/shard_map/ppermute | solution.py:212
  28.4 1.6 %collective-permute-start.7 = (f32[32,2176]{1,0:T(8,128)S(1)}, f32[32,2176]{1,0:T(8,128)S(1)}, u32[]{:S(2)}, u32[]{:S(2)}) collective-permute-start(f32[32,2176]{1,0:T(8,128)S(1)} %get-tuple-element.39), channel_id=1, source_target_pairs={{0,4},{4,0},{8,12},{12,8},{1,5},{5,1},{9,13},{13,9},{2,6},{6,2},{1... | collective-permute-start | bytes 835592 | tf_op jit(solution)/shard_map/ppermute | solution.py:212
  30.0 8.8 %collective-permute-start.8 = (f32[32,2176]{1,0:T(8,128)S(1)}, f32[32,2176]{1,0:T(8,128)S(1)}, u32[]{:S(2)}, u32[]{:S(2)}) collective-permute-start(f32[32,2176]{1,0:T(8,128)S(1)} %add.6), channel_id=1, source_target_pairs={{0,8},{4,12},{8,0},{12,4},{1,9},{5,13},{9,1},{13,5},{2,10},{6,14},... | collective-permute-start | bytes 835592 | tf_op jit(solution)/shard_map/ppermute | solution.py:212
  38.9 1.7 %collective-permute-start.9 = (f32[32,2048]{1,0:T(8,128)S(1)}, f32[32,2048]{1,0:T(8,128)S(1)}, u32[]{:S(2)}, u32[]{:S(2)}) collective-permute-start(f32[32,2048]{1,0:T(8,128)S(1)} %slice.9.mine), channel_id=1, source_target_pairs={{0,4},{4,0},{8,12},{12,8},{1,5},{5,1},{9,13},{13,9},{2,6},{6,2},{1... | collective-permute-start | bytes 786440 | tf_op jit(solution)/shard_map/ppermute | solution.py:212

commit v7 on v6

--- a/solution.py
+++ b/solution.py
@@ -8,6 +8,7 @@
 from jax.sharding import PartitionSpec as P
 
 OB = 8
+STEP = 128
 F32 = jnp.float32
 BF16 = jnp.bfloat16
 VMEM = pl.BlockSpec(memory_space=pltpu.VMEM)
@@ -148,11 +149,13 @@
 
 
 def dest_pass(dest_axis, orig_axis, anchors_s, dests_s, values, spread, gram_inverse, *refs):
-    *pieces, anchor_factor, kept, sent, sums, halves, factor, out_sem = refs
+    *pieces, anchor_factor, kept, late_kept, sent, late_sent, sums, halves, factor, out_sem = refs
     tiles, slots, tile_size, _ = values.shape
     rank, width = sums.shape
     half = halves.shape[2]
     half_tiles = half // tile_size
+    late = late_kept.shape[1] // 2
+    early = half - late
     me = lax.axis_index(dest_axis)
     core = lax.rem(lax.axis_index(orig_axis), 2)
     part_rows = pieces[0].shape[0]
@@ -165,8 +168,8 @@
     out_copy.start()
     gram = gram_of(solved)
     packed = jnp.concatenate([gram[: rank // 2], gram[rank // 2 :]], axis=1)
-    kept[:, 2 * half :] = packed
-    sent[:, 2 * half :] = packed
+    kept[:, 2 * early :] = packed
+    sent[:, 2 * early :] = packed
     halves[...] = jnp.zeros_like(halves)
     for t in range(tiles):
         anchor_at = pl.multiple_of(anchors_s[0, 0, t] * tile_size, tile_size)
@@ -177,9 +180,11 @@
         term = jnp.dot(weights, tile, preferred_element_type=F32)
         dest_at = pl.multiple_of(lax.rem(dest, half_tiles) * tile_size, tile_size)
         halves[dest // half_tiles, :, pl.ds(dest_at, tile_size)] += term
-    for block, at in ((kept, core), (sent, 1 - core)):
-        block[:, :half] = halves[at, : rank // 2]
-        block[:, half : 2 * half] = halves[at, rank // 2 :]
+    for block, late_block, at in ((kept, late_kept, core), (sent, late_sent, 1 - core)):
+        for i in range(2):
+            rows = pl.ds(i * (rank // 2), rank // 2)
+            block[:, i * early : (i + 1) * early] = halves[at, rows, :early]
+            late_block[:, i * late : (i + 1) * late] = halves[at, rows, early:]
     out_copy.wait()
 
 
@@ -194,16 +199,34 @@
     inverse[...] = spd_inverse((total * row_scale * col_scale) * hour_gram[...]) * col_scale
 
 
-def dest_solve(axis, gram_inverse, mine, other, dest_factor, solved, sems):
-    half = mine.shape[1] // 2
+def finish_early(mine, other, hour_gram, sums, inverse):
+    total = mine[...] + other[...]
+    width = sums.shape[1]
+    sums[...] = total[:, :width]
+    anchor_gram_inverse(total[:, width:], hour_gram, inverse)
+
+
+def solve_part(gram_inverse, mine, other, solved):
+    width = mine.shape[1] // 2
+    for i, piece in enumerate((mine, other)):
+        right_side = jnp.concatenate([piece[:, :width], piece[:, width:]], axis=0)
+        solved[i] = solve_with(gram_inverse[...], right_side)
+
+
+def dest_solve(axis, gram_inverse, mine, other, ready, dest_factor, solved, sems):
+    half = dest_factor.shape[1] // 2
     core = lax.rem(lax.axis_index(axis), 2)
     copies = []
-    for i, (at, piece) in enumerate(((core, mine), (1 - core, other))):
-        right_side = jnp.concatenate([piece[:, :half], piece[:, half:]], axis=0)
-        solved[i] = solve_with(gram_inverse[...], right_side)
-        columns = pl.ds(pl.multiple_of(at * half, half), half)
-        copies.append(pltpu.make_async_copy(solved.at[i], dest_factor.at[:, columns], sems.at[i]))
-        copies[i].start()
+    start = 0
+    for source in (ready, solved):
+        if source is solved:
+            solve_part(gram_inverse, mine, other, solved)
+        width = source.shape[2]
+        for i, at in enumerate((core, 1 - core)):
+            columns = pl.ds(pl.multiple_of(at * half + start, STEP), width)
+            copies.append(pltpu.make_async_copy(source.at[i], dest_factor.at[:, columns], sems.at[len(copies)]))
+            copies[-1].start()
+        start += width
     for copy in copies:
         copy.wait()
 
@@ -297,12 +320,14 @@
             functools.partial(dest_gram_inverse, "orig"), square, [VMEM] * 3, [pltpu.VMEM((rank, rank), F32)]
         )(packed, swap(packed, "orig", orig_count, 1), hour_gram)
 
-        anchor_factor, kept, sent = call(
+        early_half = max(half // 2 // STEP, 1) * STEP
+        blocks = [
+            jax.ShapeDtypeStruct((rank // 2, 2 * early_half + 2 * rank), F32),
+            jax.ShapeDtypeStruct((rank // 2, 2 * (half - early_half)), F32),
+        ]
+        anchor_factor, *blocks = call(
             functools.partial(dest_pass, "dest", "orig"),
-            (
-                jax.ShapeDtypeStruct((rank, width), F32),
-                *[jax.ShapeDtypeStruct((rank // 2, 2 * half + 2 * rank), F32)] * 2,
-            ),
+            (jax.ShapeDtypeStruct((rank, width), F32), *blocks, *blocks),
             [SMEM] * 2 + [VMEM] * (3 + dest_count),
             [
                 pltpu.VMEM((rank, width), F32),
@@ -310,24 +335,35 @@
                 pltpu.VMEM((rank, width), F32),
                 pltpu.SemaphoreType.DMA,
             ],
-            (HBM, VMEM, VMEM),
+            (HBM, VMEM, VMEM, VMEM, VMEM),
         )(in_smem(anchors), in_smem(dests), in_vmem(values), in_vmem(spread), dest_inverse, *pieces)
 
-        mine = kept + swap(sent, "orig", orig_count, 1)
-        distance = 2
-        while distance < orig_count:
-            mine = mine + swap(mine, "orig", orig_count, distance)
-            distance *= 2
-        sums, gram = mine[:, : 2 * half], mine[:, 2 * half :]
-        anchor_inverse = call(anchor_gram_inverse, square, [VMEM] * 2)(gram, hour_gram)
-        other = swap(sums, "orig", orig_count, 1)
+        def arrived(kept, sent):
+            mine = kept + swap(sent, "orig", orig_count, 1)
+            distance = 2
+            while distance < orig_count // 2:
+                mine = mine + swap(mine, "orig", orig_count, distance)
+                distance *= 2
+            return mine, swap(mine, "orig", orig_count, distance)
+
+        early_sums, early_other = arrived(blocks[0], blocks[2])
+        sums, anchor_inverse = call(
+            finish_early,
+            (jax.ShapeDtypeStruct((rank // 2, 2 * early_half), F32), square),
+            [VMEM] * 3,
+        )(early_sums, early_other, hour_gram)
+        ready = call(solve_part, jax.ShapeDtypeStruct((2, rank, early_half), F32), [VMEM] * 3)(
+            anchor_inverse, sums, swap(sums, "orig", orig_count, 1)
+        )
+        late_mine, late_other = arrived(blocks[1], blocks[3])
+        late_sums = late_mine + late_other
         dest_factor = call(
             functools.partial(dest_solve, "orig"),
             jax.ShapeDtypeStruct((rank, dest_width), F32),
-            [VMEM] * 3,
-            [pltpu.VMEM((2, rank, half), F32), pltpu.SemaphoreType.DMA((2,))],
+            [VMEM] * 4,
+            [pltpu.VMEM((2, rank, half - early_half), F32), pltpu.SemaphoreType.DMA((4,))],
             HBM,
-        )(anchor_inverse, sums, other)
+        )(anchor_inverse, late_sums, swap(late_sums, "orig", orig_count, 1), ready)
         return anchor_factor, dest_factor
 
     placed = (

time: 41.8 us -> 41.4 us (level)
  waiting for transfers between devices: 14 us -> 11.9 us
  starting transfers between devices: 11.8 us -> 13.2 us
    ppermute x10 -> x13, waiting for transfers between devices: 14 us -> 11.9 us  [swap(): return lax.ppermute(array, axis, [(i, i ^ distance) for i in range(count)])]
    ppermute x10 -> x13, starting transfers between devices: 11.8 us -> 13.2 us  [swap(): return lax.ppermute(array, axis, [(i, i ^ distance) for i in range(count)])]
    pallas_call x1 -> x2, Pallas kernels: 1.61 us -> 1.86 us  [the longest x1 1.62 us: shards(): call(finish_early, (jax.ShapeDtypeStruct((rank // 2, 2 * early_half), F32...]
  transfers between devices with their start and end apart: 10 -> 13, of which waited for: 6 -> 9; matrix products, arithmetic and copies ran while one was open for 0% -> 0% of each run, Pallas kernels for 15% -> 16%
where the time goes in v7:
time: 41.4 us; the launch traced here: 41.2 us
  Pallas kernels  15.4 us (37%)
  starting transfers between devices  13.2 us (32%)
  waiting for transfers between devices  11.9 us (29%)
  between operations  0.73 us (2%)
    ppermute x13, starting transfers between devices, swap(): return lax.ppermute(array, axis, [(i, i ^ distance) for i in range(count)])  13.2 us
    ppermute x13, waiting for transfers between devices, swap(): return lax.ppermute(array, axis, [(i, i ^ distance) for i in range(count)])  11.9 us
    pallas_call x1, Pallas kernels, shards(): call(functools.partial(anchor_pass, 'dest', 'orig'), (pltpu.SMEM(anchors....  5.3 us
    pallas_call x1, Pallas kernels, shards(): call(spread_scales, pltpu.VMEM((tiles, slots, rank, tile_size), F32), [VM...  3.07 us
    pallas_call x1, Pallas kernels, shards(): call(functools.partial(dest_pass, 'dest', 'orig'), (jax.ShapeDtypeStruct(...  2.64 us
    pallas_call x1, Pallas kernels, shards(): call(finish_early, (jax.ShapeDtypeStruct((rank // 2, 2 * early_half), F32...  1.62 us
    pallas_call x1, Pallas kernels, shards(): call(functools.partial(dest_gram_inverse, 'orig'), square, [VMEM] * 3, [p...  1.52 us
    pallas_call x1, Pallas kernels, shards(): call(functools.partial(dest_solve, 'orig'), jax.ShapeDtypeStruct((rank, d...  0.98 us
  transfers between devices with their start and end apart: 13, of which 9 were waited for; matrix products, arithmetic and copies ran while one was open for 0% of the time, Pallas kernels for 16%

profile of v7, /device:TPU:0, one launch (start us, length us, event | category | flops | bytes accessed | tf_op | source)
XLA Modules:
  0.0 41.2 jit_solution(12787344560956397663)
XLA Ops:
  0.6 5.3 %shard_map.86 = (s32[1,1,12]{2,1,0:T(1,128)S(4)}, s32[1,1,12]{2,1,0:T(1,128)S(4)}, f32[64,64]{1,0:T(8,128)S(1)}, bf16[12,24,128,128]{3,2,1,0:T(8,128)(2,1)S(1)},...) custom-call(s32[12,1,24]{2,1,0:T(1,128)} %bitcast.3, ...), custom_call_target="tpu_custom_call" | custom-call | tf_op jit(solution)/shard_map/pallas_call | solution.py:283
  5.9 3.1 %collective-permute-start = (f32[16,1152]{1,0:T(8,128)S(1)}, f32[16,1152]{1,0:T(8,128)S(1)}, u32[]{:S(2)}, u32[]{:S(2)}) collective-permute-start(f32[16,1152]{1,0:T(8,128)S(1)} %get-tuple-element.29), channel_id=1, source_target_pairs={{0,1},{1,0},{2,3},{3,2},{4,5},{5,4},{6,7},{7,6},{8,9},{9,8},{10,11... | collective-permute-start | bytes 221192 | tf_op jit(solution)/shard_map/ppermute | solution.py:235
  9.0 2.6 %collective-permute-start.1 = (f32[16,1152]{1,0:T(8,128)S(1)}, f32[16,1152]{1,0:T(8,128)S(1)}, u32[]{:S(2)}, u32[]{:S(2)}) collective-permute-start(f32[16,1152]{1,0:T(8,128)S(1)} %get-tuple-element.30), channel_id=1, source_target_pairs={{0,2},{1,3},{2,0},{3,1},{4,6},{5,7},{6,4},{7,5},{8,10},{9,11},{10,... | collective-permute-start | bytes 221192 | tf_op jit(solution)/shard_map/ppermute | solution.py:235
  11.6 0.0 collective-permute-start.2
  11.6 3.1 %shard_map.87.spread = f32[12,24,64,128]{3,2,1,0:T(8,128)S(1)} custom-call(f32[12,24,64]{2,1,0:T(8,128)S(1)} %get-tuple-element.32.scale_rows), custom_call_target="tpu_custom_call" | custom-call | tf_op jit(solution)/shard_map/pallas_call | solution.py:307
  14.7 0.0 collective-permute-done.refs_1_
  14.7 2.1 %collective-permute-done.1.refs_2_ = f32[16,1152]{1,0:T(8,128)S(1)} collective-permute-done((f32[16,1152]{1,0:T(8,128)S(1)}, f32[16,1152]{1,0:T(8,128)S(1)}, u32[]{:S(2)}, u32[]{:S(2)}) %collective-permute-start.1) | collective-permute-done | bytes 73760 | tf_op jit(solution)/shard_map/ppermute | solution.py:235
  16.8 1.1 %collective-permute-done.2.refs_3_ = f32[16,1152]{1,0:T(8,128)S(1)} collective-permute-done((f32[16,1152]{1,0:T(8,128)S(1)}, f32[16,1152]{1,0:T(8,128)S(1)}, u32[]{:S(2)}, u32[]{:S(2)}) %collective-permute-start.2) | collective-permute-done | bytes 73760 | tf_op jit(solution)/shard_map/ppermute | solution.py:235
  17.9 2.3 %collective-permute-start.6 = (f32[16,1024]{1,0:T(8,128)S(1)}, f32[16,1024]{1,0:T(8,128)S(1)}, u32[]{:S(2)}, u32[]{:S(2)}) collective-permute-start(f32[16,1024]{1,0:T(8,128)S(1)} %get-tuple-element.40.refs_0_), channel_id=1, source_target_pairs={{0,3},{1,2},{2,1},{3,0},{4,7},{5,6},{6,5},{7,4},{8,11},{9,10},{10,... | collective-permute-start | bytes 196616 | tf_op jit(solution)/shard_map/ppermute | solution.py:235
  20.2 0.3 collective-permute-start.5
  20.5 1.8 %collective-permute-start.4 = (f32[16,1024]{1,0:T(8,128)S(1)}, f32[16,1024]{1,0:T(8,128)S(1)}, u32[]{:S(2)}, u32[]{:S(2)}) collective-permute-start(f32[16,1024]{1,0:T(8,128)S(1)} %get-tuple-element.40.refs_0_), channel_id=1, source_target_pairs={{0,1},{1,0},{2,3},{3,2},{4,5},{5,4},{6,7},{7,6},{8,9},{9,8},{10,11... | collective-permute-start | bytes 196616 | tf_op jit(solution)/shard_map/ppermute | solution.py:235
  22.4 0.0 collective-permute-start.3
  22.4 1.2 %collective-permute-done.3.other = f32[16,128]{1,0:T(8,128)S(1)} collective-permute-done((f32[16,128]{1,0:T(8,128)S(1)}, f32[16,128]{1,0:T(8,128)S(1)}, u32[]{:S(2)}, u32[]{:S(2)}) %collective-permute-start.3) | collective-permute-done | bytes 8224 | tf_op jit(solution)/shard_map/ppermute | solution.py:235
  23.5 1.5 %shard_map.89.gram_inverse = f32[64,64]{1,0:T(8,128)S(1)} custom-call(f32[16,128]{1,0:T(8,128)S(1)} %get-tuple-element.38.mine, f32[16,128]{1,0:T(8,128)S(1)} %collective-permute-done.3.other, f32[64,64]{1,0:T(8,128)S(1)} %get-tuple-element.39.hour_gram), custom_call_target="tpu_custom_call" | custom-call | tf_op jit(solution)/shard_map/pallas_call | solution.py:319
  25.0 0.0 collective-permute-done.6.refs_3_
  25.1 0.9 %collective-permute-done.5.refs_2_ = f32[16,1024]{1,0:T(8,128)S(1)} collective-permute-done((f32[16,1024]{1,0:T(8,128)S(1)}, f32[16,1024]{1,0:T(8,128)S(1)}, u32[]{:S(2)}, u32[]{:S(2)}) %collective-permute-start.5) | collective-permute-done | bytes 65568 | tf_op jit(solution)/shard_map/ppermute | solution.py:235
  25.9 0.0 collective-permute-done.4.refs_1_
  25.9 2.6 %shard_map.90 = (f32[64,1024]{1,0:T(8,128)}, f32[32,1152]{1,0:T(8,128)S(1)}, f32[32,1024]{1,0:T(8,128)S(1)}, f32[32,1152]{1,0:T(8,128)S(1)}, f32[32,1024]{1,0:T(8,128)S(1)}) custom-call(s32[1,1,12]{2,1,0:T(1,128)S(4)} %get-tuple-element.25.anchors_s, s32[1,1,12]{2,1,0:T(1,128)S(4)} %get-tuple-element.26.dests_s, ...), custom_call_target="tpu_custom_call" | custom-call | tf_op jit(solution)/shard_map/pallas_call | solution.py:328
  28.6 0.1 collective-permute-start.7
  28.7 0.5 %collective-permute-start.9 = (f32[32,1024]{1,0:T(8,128)S(1)}, f32[32,1024]{1,0:T(8,128)S(1)}, u32[]{:S(2)}, u32[]{:S(2)}) collective-permute-start(f32[32,1024]{1,0:T(8,128)S(1)} %get-tuple-element.46), channel_id=1, source_target_pairs={{0,4},{4,0},{8,12},{12,8},{1,5},{5,1},{9,13},{13,9},{2,6},{6,2},{1... | collective-permute-start | bytes 393224 | tf_op jit(solution)/shard_map/ppermute | solution.py:235
  29.2 0.9 %collective-permute-done.7 = f32[32,1152]{1,0:T(8,128)S(1)} collective-permute-done((f32[32,1152]{1,0:T(8,128)S(1)}, f32[32,1152]{1,0:T(8,128)S(1)}, u32[]{:S(2)}, u32[]{:S(2)}) %collective-permute-start.7) | collective-permute-done | bytes 147488 | tf_op jit(solution)/shard_map/ppermute | solution.py:235
  30.0 1.6 %collective-permute-start.8 = (f32[32,1152]{1,0:T(8,128)S(1)}, f32[32,1152]{1,0:T(8,128)S(1)}, u32[]{:S(2)}, u32[]{:S(2)}) collective-permute-start(f32[32,1152]{1,0:T(8,128)S(1)} %add.9.mine), channel_id=1, source_target_pairs={{0,8},{4,12},{8,0},{12,4},{1,9},{5,13},{9,1},{13,5},{2,10},{6,14},... | collective-permute-start | bytes 442376 | tf_op jit(solution)/shard_map/ppermute | solution.py:235
  31.6 0.0 collective-permute-done.9
  31.6 0.6 %collective-permute-start.10 = (f32[32,1024]{1,0:T(8,128)S(1)}, f32[32,1024]{1,0:T(8,128)S(1)}, u32[]{:S(2)}, u32[]{:S(2)}) collective-permute-start(f32[32,1024]{1,0:T(8,128)S(1)} %add.10), channel_id=1, source_target_pairs={{0,8},{4,12},{8,0},{12,4},{1,9},{5,13},{9,1},{13,5},{2,10},{6,14},... | collective-permute-start | bytes 393224 | tf_op jit(solution)/shard_map/ppermute | solution.py:235
  32.2 4.6 %collective-permute-done.8.other = f32[32,1152]{1,0:T(8,128)S(1)} collective-permute-done((f32[32,1152]{1,0:T(8,128)S(1)}, f32[32,1152]{1,0:T(8,128)S(1)}, u32[]{:S(2)}, u32[]{:S(2)}) %collective-permute-start.8) | collective-permute-done | bytes 147488 | tf_op jit(solution)/shard_map/ppermute | solution.py:235
  36.8 1.6 %shard_map.91 = (f32[32,1024]{1,0:T(8,128)S(1)}, f32[64,64]{1,0:T(8,128)S(1)}) custom-call(f32[32,1152]{1,0:T(8,128)S(1)} %add.9.mine, f32[32,1152]{1,0:T(8,128)S(1)} %collective-permute-done.8.other, f32[64,64]{1,0:T(8,128)S(1)} %get-tuple-element.39.hour_gram), custom_call_target="tpu_custom_call" | custom-call | tf_op jit(solution)/shard_map/pallas_call | solution.py:350
  38.4 0.1 collective-permute-start.12
  38.5 0.3 collective-permute-done.10
  38.8 0.3 collective-permute-start.11
  39.1 0.7 %collective-permute-done.12.other = f32[32,1024]{1,0:T(8,128)S(1)} collective-permute-done((f32[32,1024]{1,0:T(8,128)S(1)}, f32[32,1024]{1,0:T(8,128)S(1)}, u32[]{:S(2)}, u32[]{:S(2)}) %collective-permute-start.12) | collective-permute-done | bytes 131104 | tf_op jit(solution)/shard_map/ppermute | solution.py:235
  39.8 0.2 shard_map.92.ready
  40.1 0.2 collective-permute-done.11.other
  40.2 1.0 %shard_map.93 = f32[64,2048]{1,0:T(8,128)} custom-call(f32[64,64]{1,0:T(8,128)S(1)} %get-tuple-element.44.gram_inverse, f32[32,1024]{1,0:T(8,128)S(1)} %add.11.mine, f32[32,1024]{1,0:T(8,128)S(1)} %collective-permute-done.11.other, f32[2,64,512]{2,1,0:T(8,128)S(1)} %shard_map.92.ready), custom_call_target="tpu_custom_call" | custom-call | tf_op jit(solution)/shard_map/pallas_call | solution.py:360
  (4 shorter events, 0.1 us)
Async XLA Ops:
  5.9 8.8 %collective-permute-start = (f32[16,1152]{1,0:T(8,128)S(1)}, f32[16,1152]{1,0:T(8,128)S(1)}, u32[]{:S(2)}, u32[]{:S(2)}) collective-permute-start(f32[16,1152]{1,0:T(8,128)S(1)} %get-tuple-element.29), channel_id=1, source_target_pairs={{0,1},{1,0},{2,3},{3,2},{4,5},{5,4},{6,7},{7,6},{8,9},{9,8},{10,11... | collective-permute-start | bytes 221192 | tf_op jit(solution)/shard_map/ppermute | solution.py:235
  9.0 7.8 %collective-permute-start.1 = (f32[16,1152]{1,0:T(8,128)S(1)}, f32[16,1152]{1,0:T(8,128)S(1)}, u32[]{:S(2)}, u32[]{:S(2)}) collective-permute-start(f32[16,1152]{1,0:T(8,128)S(1)} %get-tuple-element.30), channel_id=1, source_target_pairs={{0,2},{1,3},{2,0},{3,1},{4,6},{5,7},{6,4},{7,5},{8,10},{9,11},{10,... | collective-permute-start | bytes 221192 | tf_op jit(solution)/shard_map/ppermute | solution.py:235
  11.6 6.3 %collective-permute-start.2 = (f32[16,1152]{1,0:T(8,128)S(1)}, f32[16,1152]{1,0:T(8,128)S(1)}, u32[]{:S(2)}, u32[]{:S(2)}) collective-permute-start(f32[16,1152]{1,0:T(8,128)S(1)} %get-tuple-element.31), channel_id=1, source_target_pairs={{0,3},{1,2},{2,1},{3,0},{4,7},{5,6},{6,5},{7,4},{8,11},{9,10},{10,... | collective-permute-start | bytes 221192 | tf_op jit(solution)/shard_map/ppermute | solution.py:235
  17.9 7.2 %collective-permute-start.6 = (f32[16,1024]{1,0:T(8,128)S(1)}, f32[16,1024]{1,0:T(8,128)S(1)}, u32[]{:S(2)}, u32[]{:S(2)}) collective-permute-start(f32[16,1024]{1,0:T(8,128)S(1)} %get-tuple-element.40.refs_0_), channel_id=1, source_target_pairs={{0,3},{1,2},{2,1},{3,0},{4,7},{5,6},{6,5},{7,4},{8,11},{9,10},{10,... | collective-permute-start | bytes 196616 | tf_op jit(solution)/shard_map/ppermute | solution.py:235
  20.2 5.8 %collective-permute-start.5 = (f32[16,1024]{1,0:T(8,128)S(1)}, f32[16,1024]{1,0:T(8,128)S(1)}, u32[]{:S(2)}, u32[]{:S(2)}) collective-permute-start(f32[16,1024]{1,0:T(8,128)S(1)} %get-tuple-element.40.refs_0_), channel_id=1, source_target_pairs={{0,2},{1,3},{2,0},{3,1},{4,6},{5,7},{6,4},{7,5},{8,10},{9,11},{10,... | collective-permute-start | bytes 196616 | tf_op jit(solution)/shard_map/ppermute | solution.py:235
  20.5 5.4 %collective-permute-start.4 = (f32[16,1024]{1,0:T(8,128)S(1)}, f32[16,1024]{1,0:T(8,128)S(1)}, u32[]{:S(2)}, u32[]{:S(2)}) collective-permute-start(f32[16,1024]{1,0:T(8,128)S(1)} %get-tuple-element.40.refs_0_), channel_id=1, source_target_pairs={{0,1},{1,0},{2,3},{3,2},{4,5},{5,4},{6,7},{7,6},{8,9},{9,8},{10,11... | collective-permute-start | bytes 196616 | tf_op jit(solution)/shard_map/ppermute | solution.py:235
  22.4 1.2 %collective-permute-start.3 = (f32[16,128]{1,0:T(8,128)S(1)}, f32[16,128]{1,0:T(8,128)S(1)}, u32[]{:S(2)}, u32[]{:S(2)}) collective-permute-start(f32[16,128]{1,0:T(8,128)S(1)} %get-tuple-element.38.mine), channel_id=1, source_target_pairs={{0,4},{4,0},{8,12},{12,8},{1,5},{5,1},{9,13},{13,9},{2,6},{6,2},{1... | collective-permute-start | bytes 24584 | tf_op jit(solution)/shard_map/ppermute | solution.py:235
  28.6 1.4 %collective-permute-start.7 = (f32[32,1152]{1,0:T(8,128)S(1)}, f32[32,1152]{1,0:T(8,128)S(1)}, u32[]{:S(2)}, u32[]{:S(2)}) collective-permute-start(f32[32,1152]{1,0:T(8,128)S(1)} %get-tuple-element.43), channel_id=1, source_target_pairs={{0,4},{4,0},{8,12},{12,8},{1,5},{5,1},{9,13},{13,9},{2,6},{6,2},{1... | collective-permute-start | bytes 442376 | tf_op jit(solution)/shard_map/ppermute | solution.py:235
  28.7 3.0 %collective-permute-start.9 = (f32[32,1024]{1,0:T(8,128)S(1)}, f32[32,1024]{1,0:T(8,128)S(1)}, u32[]{:S(2)}, u32[]{:S(2)}) collective-permute-start(f32[32,1024]{1,0:T(8,128)S(1)} %get-tuple-element.46), channel_id=1, source_target_pairs={{0,4},{4,0},{8,12},{12,8},{1,5},{5,1},{9,13},{13,9},{2,6},{6,2},{1... | collective-permute-start | bytes 393224 | tf_op jit(solution)/shard_map/ppermute | solution.py:235
  30.0 6.8 %collective-permute-start.8 = (f32[32,1152]{1,0:T(8,128)S(1)}, f32[32,1152]{1,0:T(8,128)S(1)}, u32[]{:S(2)}, u32[]{:S(2)}) collective-permute-start(f32[32,1152]{1,0:T(8,128)S(1)} %add.9.mine), channel_id=1, source_target_pairs={{0,8},{4,12},{8,0},{12,4},{1,9},{5,13},{9,1},{13,5},{2,10},{6,14},... | collective-permute-start | bytes 442376 | tf_op jit(solution)/shard_map/ppermute | solution.py:235
  31.6 7.2 %collective-permute-start.10 = (f32[32,1024]{1,0:T(8,128)S(1)}, f32[32,1024]{1,0:T(8,128)S(1)}, u32[]{:S(2)}, u32[]{:S(2)}) collective-permute-start(f32[32,1024]{1,0:T(8,128)S(1)} %add.10), channel_id=1, source_target_pairs={{0,8},{4,12},{8,0},{12,4},{1,9},{5,13},{9,1},{13,5},{2,10},{6,14},... | collective-permute-start | bytes 393224 | tf_op jit(solution)/shard_map/ppermute | solution.py:235
  38.4 1.4 %collective-permute-start.12 = (f32[32,1024]{1,0:T(8,128)S(1)}, f32[32,1024]{1,0:T(8,128)S(1)}, u32[]{:S(2)}, u32[]{:S(2)}) collective-permute-start(f32[32,1024]{1,0:T(8,128)S(1)} %get-tuple-element.47.mine), channel_id=1, source_target_pairs={{0,4},{4,0},{8,12},{12,8},{1,5},{5,1},{9,13},{13,9},{2,6},{6,2},{1... | collective-permute-start | bytes 393224 | tf_op jit(solution)/shard_map/ppermute | solution.py:235
  38.8 1.4 %collective-permute-start.11 = (f32[32,1024]{1,0:T(8,128)S(1)}, f32[32,1024]{1,0:T(8,128)S(1)}, u32[]{:S(2)}, u32[]{:S(2)}) collective-permute-start(f32[32,1024]{1,0:T(8,128)S(1)} %add.11.mine), channel_id=1, source_target_pairs={{0,4},{4,0},{8,12},{12,8},{1,5},{5,1},{9,13},{13,9},{2,6},{6,2},{1... | collective-permute-start | bytes 393224 | tf_op jit(solution)/shard_map/ppermute | solution.py:235

commit v8 on v7

--- a/solution.py
+++ b/solution.py
@@ -61,8 +61,12 @@
     return matrix
 
 
+def partners(orders, core):
+    return [0] + [jnp.where(core == 0, first, second) for first, second in zip(*orders)]
+
+
 def anchor_pass(
-    dest_axis, orig_axis, hours, live, anchors, dests, dest_factor, hour_factor, values, anchors_s, dests_s, hour_gram, values_buf,
+    dest_axis, orig_axis, reduce_orders, hours, live, anchors, dests, dest_factor, hour_factor, values, anchors_s, dests_s, hour_gram, values_buf,
     scale_rows, *refs,
 ):
     *parts, sums, gram, dest_buf, hour_buf, hour_rows, hours_s, live_s, sems, small_sems = refs
@@ -116,15 +120,20 @@
         if t + 1 < tiles:
             weights = weights_of(t + 1)
     me = lax.axis_index(dest_axis)
-    for k, part in enumerate(parts):
+    for k, part in zip(partners(reduce_orders, core), parts):
         at = pl.multiple_of(jnp.bitwise_xor(me, k) * part_rows, part_rows)
         part[:, :width] = sums[pl.ds(at, part_rows), :]
 
 
-def add_parts(*refs):
-    parts, (piece, packed) = refs[:-2], refs[-2:]
+def add_parts(axis, orders, *refs):
+    (mine, *parts), (piece, packed) = refs[:-2], refs[-2:]
     width = piece.shape[1]
-    total = tree_sum([part[...] for part in parts])
+    core = lax.rem(lax.axis_index(axis), 2)
+    terms = [mine[...]]
+    for k in range(1, len(parts) + 1):
+        first, second = (parts[order.index(k)] for order in orders)
+        terms.append(jnp.where(core == 0, first[...], second[...]))
+    total = tree_sum(terms)
     piece[...] = total[:, :width]
     packed[...] = total[:, width:]
 
@@ -166,10 +175,6 @@
     factor[...] = solved
     out_copy = pltpu.make_async_copy(factor, anchor_factor, out_sem)
     out_copy.start()
-    gram = gram_of(solved)
-    packed = jnp.concatenate([gram[: rank // 2], gram[rank // 2 :]], axis=1)
-    kept[:, 2 * early :] = packed
-    sent[:, 2 * early :] = packed
     halves[...] = jnp.zeros_like(halves)
     for t in range(tiles):
         anchor_at = pl.multiple_of(anchors_s[0, 0, t] * tile_size, tile_size)
@@ -178,6 +183,11 @@
         weights = jnp.concatenate([(tile_factor * spread[t, s]).astype(BF16) for s in range(slots)], axis=1)
         tile = values[t].reshape(slots * tile_size, tile_size)
         term = jnp.dot(weights, tile, preferred_element_type=F32)
+        if t == 3:
+            gram = gram_of(factor[...])
+            packed = jnp.concatenate([gram[: rank // 2], gram[rank // 2 :]], axis=1)
+            kept[:, 2 * early :] = packed
+            sent[:, 2 * early :] = packed
         dest_at = pl.multiple_of(lax.rem(dest, half_tiles) * tile_size, tile_size)
         halves[dest // half_tiles, :, pl.ds(dest_at, tile_size)] += term
     for block, late_block, at in ((kept, late_kept, core), (sent, late_sent, 1 - core)):
@@ -268,6 +278,17 @@
     dest_count = mesh.shape["dest"]
     orig_count = mesh.shape["orig"]
 
+    distances = list(range(1, dest_count))
+    reduce_orders = (distances, distances[1:] + distances[:1])
+
+    def staggered_swap(array, j):
+        pairs = [
+            (o * dest_count + z, o * dest_count + (z ^ reduce_orders[o % 2][j]))
+            for o in range(orig_count)
+            for z in range(dest_count)
+        ]
+        return lax.ppermute(array, ("orig", "dest"), pairs)
+
     def shards(hours_of_values, tile_hours, tile_anchor, tile_dest, tile_live, dest_factor_in, hour_factor):
         values = hours_of_values[0, 0]
         tiles, slots, tile_size, _ = values.shape
@@ -281,7 +302,7 @@
         hours = in_hbm(tile_hours.reshape(tiles, 1, slots))
         live, anchors, dests = (in_hbm(index) for index in (tile_live, tile_anchor, tile_dest))
         anchors, dests, hour_gram, values, scale_rows, *parts = call(
-            functools.partial(anchor_pass, "dest", "orig"),
+            functools.partial(anchor_pass, "dest", "orig", reduce_orders),
             (
                 pltpu.SMEM(anchors.shape, jnp.int32),
                 pltpu.SMEM(dests.shape, jnp.int32),
@@ -305,10 +326,10 @@
             (SMEM, SMEM, *[VMEM] * (3 + dest_count)),
         )(hours, live, anchors, dests, in_hbm(dest_factor_in), in_hbm(hour_factor), in_hbm(values))
         spread = call(spread_scales, pltpu.VMEM((tiles, slots, rank, tile_size), F32), [VMEM])(scale_rows)
-        parts = parts[:1] + [swap(parts[k], "dest", dest_count, k) for k in range(1, dest_count)]
+        parts = parts[:1] + [staggered_swap(part, j) for j, part in enumerate(parts[1:])]
         parts, spread = lax.optimization_barrier((parts, spread))
         piece, packed = call(
-            add_parts,
+            functools.partial(add_parts, "orig", reduce_orders),
             (
                 jax.ShapeDtypeStruct((part_rows, width), F32),
                 jax.ShapeDtypeStruct((part_rows, packed_width), F32),

time: 41.4 us -> 41 us (level)
    ppermute x0 -> x3, starting transfers between devices: none -> 5.68 us  [staggered_swap(): return lax.ppermute(array, ('orig', 'dest'), pairs)]
    ppermute x13 -> x10, starting transfers between devices: 13.2 us -> 7.51 us  [swap(): return lax.ppermute(array, axis, [(i, i ^ distance) for i in range(count)])]
    ppermute x13 -> x10, waiting for transfers between devices: 11.9 us -> 8.42 us  [swap(): return lax.ppermute(array, axis, [(i, i ^ distance) for i in range(count)])]
    ppermute x0 -> x3, waiting for transfers between devices: none -> 3.17 us  [staggered_swap(): return lax.ppermute(array, ('orig', 'dest'), pairs)]
where the time goes in v8:
time: 41 us; the launch traced here: 40.8 us
  Pallas kernels  15.2 us (37%)
  starting transfers between devices  13.2 us (32%)
  waiting for transfers between devices  11.6 us (28%)
  between operations  0.73 us (2%)
    ppermute x10, waiting for transfers between devices, swap(): return lax.ppermute(array, axis, [(i, i ^ distance) for i in range(count)])  8.42 us
    ppermute x10, starting transfers between devices, swap(): return lax.ppermute(array, axis, [(i, i ^ distance) for i in range(count)])  7.51 us
    ppermute x3, starting transfers between devices, staggered_swap(): return lax.ppermute(array, ('orig', 'dest'), pairs)  5.68 us
    pallas_call x1, Pallas kernels, shards(): call(functools.partial(anchor_pass, 'dest', 'orig', reduce_orders), (pltp...  5.29 us
    ppermute x3, waiting for transfers between devices, staggered_swap(): return lax.ppermute(array, ('orig', 'dest'), pairs)  3.17 us
    pallas_call x1, Pallas kernels, shards(): call(spread_scales, pltpu.VMEM((tiles, slots, rank, tile_size), F32), [VM...  3.07 us
    pallas_call x1, Pallas kernels, shards(): call(functools.partial(dest_pass, 'dest', 'orig'), (jax.ShapeDtypeStruct(...  2.49 us
    pallas_call x1, Pallas kernels, shards(): call(finish_early, (jax.ShapeDtypeStruct((rank // 2, 2 * early_half), F32...  1.62 us
  transfers between devices with their start and end apart: 13, of which 9 were waited for; matrix products, arithmetic and copies ran while one was open for 0% of the time, Pallas kernels for 16%

profile of v8, /device:TPU:0, one launch (start us, length us, event | category | flops | bytes accessed | tf_op | source)
XLA Modules:
  0.0 40.8 jit_solution(5274398601648739940)
XLA Ops:
  0.6 5.3 %shard_map.86 = (s32[1,1,12]{2,1,0:T(1,128)S(4)}, s32[1,1,12]{2,1,0:T(1,128)S(4)}, f32[64,64]{1,0:T(8,128)S(1)}, bf16[12,24,128,128]{3,2,1,0:T(8,128)(2,1)S(1)},...) custom-call(s32[12,1,24]{2,1,0:T(1,128)} %bitcast.3, ...), custom_call_target="tpu_custom_call" | custom-call | tf_op jit(solution)/shard_map/pallas_call | solution.py:304
  5.9 3.1 %collective-permute-start = (f32[16,1152]{1,0:T(8,128)S(1)}, f32[16,1152]{1,0:T(8,128)S(1)}, u32[]{:S(2)}, u32[]{:S(2)}) collective-permute-start(f32[16,1152]{1,0:T(8,128)S(1)} %get-tuple-element.29), channel_id=1, source_target_pairs={{0,1},{1,0},{2,3},{3,2},{4,6},{5,7},{6,4},{7,5},{8,9},{9,8},{10,11... | collective-permute-start | bytes 221192 | tf_op jit(solution)/shard_map/ppermute | solution.py:290
  9.0 2.6 %collective-permute-start.1 = (f32[16,1152]{1,0:T(8,128)S(1)}, f32[16,1152]{1,0:T(8,128)S(1)}, u32[]{:S(2)}, u32[]{:S(2)}) collective-permute-start(f32[16,1152]{1,0:T(8,128)S(1)} %get-tuple-element.30), channel_id=1, source_target_pairs={{0,2},{1,3},{2,0},{3,1},{4,7},{5,6},{6,5},{7,4},{8,10},{9,11},{10,... | collective-permute-start | bytes 221192 | tf_op jit(solution)/shard_map/ppermute | solution.py:290
  11.6 0.0 collective-permute-start.2
  11.6 3.1 %shard_map.87.spread = f32[12,24,64,128]{3,2,1,0:T(8,128)S(1)} custom-call(f32[12,24,64]{2,1,0:T(8,128)S(1)} %get-tuple-element.32.scale_rows), custom_call_target="tpu_custom_call" | custom-call | tf_op jit(solution)/shard_map/pallas_call | solution.py:328
  14.7 0.0 collective-permute-done.refs_1_
  14.7 1.7 %collective-permute-done.1.refs_2_ = f32[16,1152]{1,0:T(8,128)S(1)} collective-permute-done((f32[16,1152]{1,0:T(8,128)S(1)}, f32[16,1152]{1,0:T(8,128)S(1)}, u32[]{:S(2)}, u32[]{:S(2)}) %collective-permute-start.1) | collective-permute-done | bytes 73760 | tf_op jit(solution)/shard_map/ppermute | solution.py:290
  16.4 1.5 %collective-permute-done.2.refs_3_ = f32[16,1152]{1,0:T(8,128)S(1)} collective-permute-done((f32[16,1152]{1,0:T(8,128)S(1)}, f32[16,1152]{1,0:T(8,128)S(1)}, u32[]{:S(2)}, u32[]{:S(2)}) %collective-permute-start.2) | collective-permute-done | bytes 73760 | tf_op jit(solution)/shard_map/ppermute | solution.py:290
  17.9 2.0 %collective-permute-start.6 = (f32[16,1024]{1,0:T(8,128)S(1)}, f32[16,1024]{1,0:T(8,128)S(1)}, u32[]{:S(2)}, u32[]{:S(2)}) collective-permute-start(f32[16,1024]{1,0:T(8,128)S(1)} %get-tuple-element.40.refs_0_), channel_id=1, source_target_pairs={{0,3},{1,2},{2,1},{3,0},{4,7},{5,6},{6,5},{7,4},{8,11},{9,10},{10,... | collective-permute-start | bytes 196616 | tf_op jit(solution)/shard_map/ppermute | solution.py:245
  19.9 0.2 collective-permute-start.5
  20.1 2.3 %collective-permute-start.4 = (f32[16,1024]{1,0:T(8,128)S(1)}, f32[16,1024]{1,0:T(8,128)S(1)}, u32[]{:S(2)}, u32[]{:S(2)}) collective-permute-start(f32[16,1024]{1,0:T(8,128)S(1)} %get-tuple-element.40.refs_0_), channel_id=1, source_target_pairs={{0,1},{1,0},{2,3},{3,2},{4,5},{5,4},{6,7},{7,6},{8,9},{9,8},{10,11... | collective-permute-start | bytes 196616 | tf_op jit(solution)/shard_map/ppermute | solution.py:245
  22.4 0.0 collective-permute-start.3
  22.4 1.2 %collective-permute-done.3.other = f32[16,128]{1,0:T(8,128)S(1)} collective-permute-done((f32[16,128]{1,0:T(8,128)S(1)}, f32[16,128]{1,0:T(8,128)S(1)}, u32[]{:S(2)}, u32[]{:S(2)}) %collective-permute-start.3) | collective-permute-done | bytes 8224 | tf_op jit(solution)/shard_map/ppermute | solution.py:245
  23.5 1.5 %shard_map.89.gram_inverse = f32[64,64]{1,0:T(8,128)S(1)} custom-call(f32[16,128]{1,0:T(8,128)S(1)} %get-tuple-element.38.mine, f32[16,128]{1,0:T(8,128)S(1)} %collective-permute-done.3.other, f32[64,64]{1,0:T(8,128)S(1)} %get-tuple-element.39.hour_gram), custom_call_target="tpu_custom_call" | custom-call | tf_op jit(solution)/shard_map/pallas_call | solution.py:340
  25.1 0.0 collective-permute-done.6.refs_3_
  25.1 0.6 %collective-permute-done.5.refs_2_ = f32[16,1024]{1,0:T(8,128)S(1)} collective-permute-done((f32[16,1024]{1,0:T(8,128)S(1)}, f32[16,1024]{1,0:T(8,128)S(1)}, u32[]{:S(2)}, u32[]{:S(2)}) %collective-permute-start.5) | collective-permute-done | bytes 65568 | tf_op jit(solution)/shard_map/ppermute | solution.py:245
  25.7 0.0 collective-permute-done.4.refs_1_
  25.7 2.5 %shard_map.90 = (f32[64,1024]{1,0:T(8,128)}, f32[32,1152]{1,0:T(8,128)S(1)}, f32[32,1024]{1,0:T(8,128)S(1)}, f32[32,1152]{1,0:T(8,128)S(1)}, f32[32,1024]{1,0:T(8,128)S(1)}) custom-call(s32[1,1,12]{2,1,0:T(1,128)S(4)} %get-tuple-element.25.anchors_s, s32[1,1,12]{2,1,0:T(1,128)S(4)} %get-tuple-element.26.dests_s, ...), custom_call_target="tpu_custom_call" | custom-call | tf_op jit(solution)/shard_map/pallas_call | solution.py:349
  28.2 0.1 collective-permute-start.7
  28.2 0.5 %collective-permute-start.9 = (f32[32,1024]{1,0:T(8,128)S(1)}, f32[32,1024]{1,0:T(8,128)S(1)}, u32[]{:S(2)}, u32[]{:S(2)}) collective-permute-start(f32[32,1024]{1,0:T(8,128)S(1)} %get-tuple-element.46), channel_id=1, source_target_pairs={{0,4},{4,0},{8,12},{12,8},{1,5},{5,1},{9,13},{13,9},{2,6},{6,2},{1... | collective-permute-start | bytes 393224 | tf_op jit(solution)/shard_map/ppermute | solution.py:245
  28.7 0.9 %collective-permute-done.7 = f32[32,1152]{1,0:T(8,128)S(1)} collective-permute-done((f32[32,1152]{1,0:T(8,128)S(1)}, f32[32,1152]{1,0:T(8,128)S(1)}, u32[]{:S(2)}, u32[]{:S(2)}) %collective-permute-start.7) | collective-permute-done | bytes 147488 | tf_op jit(solution)/shard_map/ppermute | solution.py:245
  29.6 1.6 %collective-permute-start.8 = (f32[32,1152]{1,0:T(8,128)S(1)}, f32[32,1152]{1,0:T(8,128)S(1)}, u32[]{:S(2)}, u32[]{:S(2)}) collective-permute-start(f32[32,1152]{1,0:T(8,128)S(1)} %add.9.mine), channel_id=1, source_target_pairs={{0,8},{4,12},{8,0},{12,4},{1,9},{5,13},{9,1},{13,5},{2,10},{6,14},... | collective-permute-start | bytes 442376 | tf_op jit(solution)/shard_map/ppermute | solution.py:245
  31.2 0.0 collective-permute-done.9
  31.2 0.6 %collective-permute-start.10 = (f32[32,1024]{1,0:T(8,128)S(1)}, f32[32,1024]{1,0:T(8,128)S(1)}, u32[]{:S(2)}, u32[]{:S(2)}) collective-permute-start(f32[32,1024]{1,0:T(8,128)S(1)} %add.10), channel_id=1, source_target_pairs={{0,8},{4,12},{8,0},{12,4},{1,9},{5,13},{9,1},{13,5},{2,10},{6,14},... | collective-permute-start | bytes 393224 | tf_op jit(solution)/shard_map/ppermute | solution.py:245
  31.8 4.6 %collective-permute-done.8.other = f32[32,1152]{1,0:T(8,128)S(1)} collective-permute-done((f32[32,1152]{1,0:T(8,128)S(1)}, f32[32,1152]{1,0:T(8,128)S(1)}, u32[]{:S(2)}, u32[]{:S(2)}) %collective-permute-start.8) | collective-permute-done | bytes 147488 | tf_op jit(solution)/shard_map/ppermute | solution.py:245
  36.4 1.6 %shard_map.91 = (f32[32,1024]{1,0:T(8,128)S(1)}, f32[64,64]{1,0:T(8,128)S(1)}) custom-call(f32[32,1152]{1,0:T(8,128)S(1)} %add.9.mine, f32[32,1152]{1,0:T(8,128)S(1)} %collective-permute-done.8.other, f32[64,64]{1,0:T(8,128)S(1)} %get-tuple-element.39.hour_gram), custom_call_target="tpu_custom_call" | custom-call | tf_op jit(solution)/shard_map/pallas_call | solution.py:371
  38.0 0.1 collective-permute-start.12
  38.1 0.3 collective-permute-done.10
  38.4 0.3 collective-permute-start.11
  38.7 0.7 %collective-permute-done.12.other = f32[32,1024]{1,0:T(8,128)S(1)} collective-permute-done((f32[32,1024]{1,0:T(8,128)S(1)}, f32[32,1024]{1,0:T(8,128)S(1)}, u32[]{:S(2)}, u32[]{:S(2)}) %collective-permute-start.12) | collective-permute-done | bytes 131104 | tf_op jit(solution)/shard_map/ppermute | solution.py:245
  39.4 0.2 shard_map.92.ready
  39.7 0.2 collective-permute-done.11.other
  39.8 1.0 %shard_map.93 = f32[64,2048]{1,0:T(8,128)} custom-call(f32[64,64]{1,0:T(8,128)S(1)} %get-tuple-element.44.gram_inverse, f32[32,1024]{1,0:T(8,128)S(1)} %add.11.mine, f32[32,1024]{1,0:T(8,128)S(1)} %collective-permute-done.11.other, f32[2,64,512]{2,1,0:T(8,128)S(1)} %shard_map.92.ready), custom_call_target="tpu_custom_call" | custom-call | tf_op jit(solution)/shard_map/pallas_call | solution.py:381
  (4 shorter events, 0.1 us)
Async XLA Ops:
  5.9 8.8 %collective-permute-start = (f32[16,1152]{1,0:T(8,128)S(1)}, f32[16,1152]{1,0:T(8,128)S(1)}, u32[]{:S(2)}, u32[]{:S(2)}) collective-permute-start(f32[16,1152]{1,0:T(8,128)S(1)} %get-tuple-element.29), channel_id=1, source_target_pairs={{0,1},{1,0},{2,3},{3,2},{4,6},{5,7},{6,4},{7,5},{8,9},{9,8},{10,11... | collective-permute-start | bytes 221192 | tf_op jit(solution)/shard_map/ppermute | solution.py:290
  9.0 7.3 %collective-permute-start.1 = (f32[16,1152]{1,0:T(8,128)S(1)}, f32[16,1152]{1,0:T(8,128)S(1)}, u32[]{:S(2)}, u32[]{:S(2)}) collective-permute-start(f32[16,1152]{1,0:T(8,128)S(1)} %get-tuple-element.30), channel_id=1, source_target_pairs={{0,2},{1,3},{2,0},{3,1},{4,7},{5,6},{6,5},{7,4},{8,10},{9,11},{10,... | collective-permute-start | bytes 221192 | tf_op jit(solution)/shard_map/ppermute | solution.py:290
  11.6 6.3 %collective-permute-start.2 = (f32[16,1152]{1,0:T(8,128)S(1)}, f32[16,1152]{1,0:T(8,128)S(1)}, u32[]{:S(2)}, u32[]{:S(2)}) collective-permute-start(f32[16,1152]{1,0:T(8,128)S(1)} %get-tuple-element.31), channel_id=1, source_target_pairs={{0,3},{1,2},{2,1},{3,0},{4,5},{5,4},{6,7},{7,6},{8,11},{9,10},{10,... | collective-permute-start | bytes 221192 | tf_op jit(solution)/shard_map/ppermute | solution.py:290
  17.9 7.2 %collective-permute-start.6 = (f32[16,1024]{1,0:T(8,128)S(1)}, f32[16,1024]{1,0:T(8,128)S(1)}, u32[]{:S(2)}, u32[]{:S(2)}) collective-permute-start(f32[16,1024]{1,0:T(8,128)S(1)} %get-tuple-element.40.refs_0_), channel_id=1, source_target_pairs={{0,3},{1,2},{2,1},{3,0},{4,7},{5,6},{6,5},{7,4},{8,11},{9,10},{10,... | collective-permute-start | bytes 196616 | tf_op jit(solution)/shard_map/ppermute | solution.py:245
  19.9 5.8 %collective-permute-start.5 = (f32[16,1024]{1,0:T(8,128)S(1)}, f32[16,1024]{1,0:T(8,128)S(1)}, u32[]{:S(2)}, u32[]{:S(2)}) collective-permute-start(f32[16,1024]{1,0:T(8,128)S(1)} %get-tuple-element.40.refs_0_), channel_id=1, source_target_pairs={{0,2},{1,3},{2,0},{3,1},{4,6},{5,7},{6,4},{7,5},{8,10},{9,11},{10,... | collective-permute-start | bytes 196616 | tf_op jit(solution)/shard_map/ppermute | solution.py:245
  20.1 5.6 %collective-permute-start.4 = (f32[16,1024]{1,0:T(8,128)S(1)}, f32[16,1024]{1,0:T(8,128)S(1)}, u32[]{:S(2)}, u32[]{:S(2)}) collective-permute-start(f32[16,1024]{1,0:T(8,128)S(1)} %get-tuple-element.40.refs_0_), channel_id=1, source_target_pairs={{0,1},{1,0},{2,3},{3,2},{4,5},{5,4},{6,7},{7,6},{8,9},{9,8},{10,11... | collective-permute-start | bytes 196616 | tf_op jit(solution)/shard_map/ppermute | solution.py:245
  22.4 1.2 %collective-permute-start.3 = (f32[16,128]{1,0:T(8,128)S(1)}, f32[16,128]{1,0:T(8,128)S(1)}, u32[]{:S(2)}, u32[]{:S(2)}) collective-permute-start(f32[16,128]{1,0:T(8,128)S(1)} %get-tuple-element.38.mine), channel_id=1, source_target_pairs={{0,4},{4,0},{8,12},{12,8},{1,5},{5,1},{9,13},{13,9},{2,6},{6,2},{1... | collective-permute-start | bytes 24584 | tf_op jit(solution)/shard_map/ppermute | solution.py:245
  28.2 1.4 %collective-permute-start.7 = (f32[32,1152]{1,0:T(8,128)S(1)}, f32[32,1152]{1,0:T(8,128)S(1)}, u32[]{:S(2)}, u32[]{:S(2)}) collective-permute-start(f32[32,1152]{1,0:T(8,128)S(1)} %get-tuple-element.43), channel_id=1, source_target_pairs={{0,4},{4,0},{8,12},{12,8},{1,5},{5,1},{9,13},{13,9},{2,6},{6,2},{1... | collective-permute-start | bytes 442376 | tf_op jit(solution)/shard_map/ppermute | solution.py:245
  28.2 3.0 %collective-permute-start.9 = (f32[32,1024]{1,0:T(8,128)S(1)}, f32[32,1024]{1,0:T(8,128)S(1)}, u32[]{:S(2)}, u32[]{:S(2)}) collective-permute-start(f32[32,1024]{1,0:T(8,128)S(1)} %get-tuple-element.46), channel_id=1, source_target_pairs={{0,4},{4,0},{8,12},{12,8},{1,5},{5,1},{9,13},{13,9},{2,6},{6,2},{1... | collective-permute-start | bytes 393224 | tf_op jit(solution)/shard_map/ppermute | solution.py:245
  29.6 6.8 %collective-permute-start.8 = (f32[32,1152]{1,0:T(8,128)S(1)}, f32[32,1152]{1,0:T(8,128)S(1)}, u32[]{:S(2)}, u32[]{:S(2)}) collective-permute-start(f32[32,1152]{1,0:T(8,128)S(1)} %add.9.mine), channel_id=1, source_target_pairs={{0,8},{4,12},{8,0},{12,4},{1,9},{5,13},{9,1},{13,5},{2,10},{6,14},... | collective-permute-start | bytes 442376 | tf_op jit(solution)/shard_map/ppermute | solution.py:245
  31.2 7.2 %collective-permute-start.10 = (f32[32,1024]{1,0:T(8,128)S(1)}, f32[32,1024]{1,0:T(8,128)S(1)}, u32[]{:S(2)}, u32[]{:S(2)}) collective-permute-start(f32[32,1024]{1,0:T(8,128)S(1)} %add.10), channel_id=1, source_target_pairs={{0,8},{4,12},{8,0},{12,4},{1,9},{5,13},{9,1},{13,5},{2,10},{6,14},... | collective-permute-start | bytes 393224 | tf_op jit(solution)/shard_map/ppermute | solution.py:245
  38.0 1.4 %collective-permute-start.12 = (f32[32,1024]{1,0:T(8,128)S(1)}, f32[32,1024]{1,0:T(8,128)S(1)}, u32[]{:S(2)}, u32[]{:S(2)}) collective-permute-start(f32[32,1024]{1,0:T(8,128)S(1)} %get-tuple-element.47.mine), channel_id=1, source_target_pairs={{0,4},{4,0},{8,12},{12,8},{1,5},{5,1},{9,13},{13,9},{2,6},{6,2},{1... | collective-permute-start | bytes 393224 | tf_op jit(solution)/shard_map/ppermute | solution.py:245
  38.4 1.4 %collective-permute-start.11 = (f32[32,1024]{1,0:T(8,128)S(1)}, f32[32,1024]{1,0:T(8,128)S(1)}, u32[]{:S(2)}, u32[]{:S(2)}) collective-permute-start(f32[32,1024]{1,0:T(8,128)S(1)} %add.11.mine), channel_id=1, source_target_pairs={{0,4},{4,0},{8,12},{12,8},{1,5},{5,1},{9,13},{13,9},{2,6},{6,2},{1... | collective-permute-start | bytes 393224 | tf_op jit(solution)/shard_map/ppermute | solution.py:245

commit v9 on v8

--- a/solution.py
+++ b/solution.py
@@ -279,7 +279,7 @@
     orig_count = mesh.shape["orig"]
 
     distances = list(range(1, dest_count))
-    reduce_orders = (distances, distances[1:] + distances[:1])
+    reduce_orders = (distances, distances[1::-1] + distances[2:])
 
     def staggered_swap(array, j):
         pairs = [

time: 41 us -> 40.9 us (level)
  no operation moved by 1% of the time
where the time goes in v9:
time: 40.9 us; the launch traced here: 40.8 us
  Pallas kernels  15.2 us (37%)
  starting transfers between devices  13.2 us (32%)
  waiting for transfers between devices  11.6 us (28%)
  between operations  0.73 us (2%)
    ppermute x10, waiting for transfers between devices, swap(): return lax.ppermute(array, axis, [(i, i ^ distance) for i in range(count)])  8.42 us
    ppermute x10, starting transfers between devices, swap(): return lax.ppermute(array, axis, [(i, i ^ distance) for i in range(count)])  7.51 us
    ppermute x3, starting transfers between devices, staggered_swap(): return lax.ppermute(array, ('orig', 'dest'), pairs)  5.68 us
    pallas_call x1, Pallas kernels, shards(): call(functools.partial(anchor_pass, 'dest', 'orig', reduce_orders), (pltp...  5.3 us
    ppermute x3, waiting for transfers between devices, staggered_swap(): return lax.ppermute(array, ('orig', 'dest'), pairs)  3.17 us
    pallas_call x1, Pallas kernels, shards(): call(spread_scales, pltpu.VMEM((tiles, slots, rank, tile_size), F32), [VM...  3.07 us
    pallas_call x1, Pallas kernels, shards(): call(functools.partial(dest_pass, 'dest', 'orig'), (jax.ShapeDtypeStruct(...  2.49 us
    pallas_call x1, Pallas kernels, shards(): call(finish_early, (jax.ShapeDtypeStruct((rank // 2, 2 * early_half), F32...  1.62 us
  transfers between devices with their start and end apart: 13, of which 9 were waited for; matrix products, arithmetic and copies ran while one was open for 0% of the time, Pallas kernels for 16%

profile of v9, /device:TPU:0, one launch (start us, length us, event | category | flops | bytes accessed | tf_op | source)
XLA Modules:
  0.0 40.8 jit_solution(6719047910466912184)
XLA Ops:
  0.6 5.3 %shard_map.86 = (s32[1,1,12]{2,1,0:T(1,128)S(4)}, s32[1,1,12]{2,1,0:T(1,128)S(4)}, f32[64,64]{1,0:T(8,128)S(1)}, bf16[12,24,128,128]{3,2,1,0:T(8,128)(2,1)S(1)},...) custom-call(s32[12,1,24]{2,1,0:T(1,128)} %bitcast.3, ...), custom_call_target="tpu_custom_call" | custom-call | tf_op jit(solution)/shard_map/pallas_call | solution.py:304
  5.9 3.1 %collective-permute-start = (f32[16,1152]{1,0:T(8,128)S(1)}, f32[16,1152]{1,0:T(8,128)S(1)}, u32[]{:S(2)}, u32[]{:S(2)}) collective-permute-start(f32[16,1152]{1,0:T(8,128)S(1)} %get-tuple-element.29), channel_id=1, source_target_pairs={{0,1},{1,0},{2,3},{3,2},{4,6},{5,7},{6,4},{7,5},{8,9},{9,8},{10,11... | collective-permute-start | bytes 221192 | tf_op jit(solution)/shard_map/ppermute | solution.py:290
  9.0 2.6 %collective-permute-start.1 = (f32[16,1152]{1,0:T(8,128)S(1)}, f32[16,1152]{1,0:T(8,128)S(1)}, u32[]{:S(2)}, u32[]{:S(2)}) collective-permute-start(f32[16,1152]{1,0:T(8,128)S(1)} %get-tuple-element.30), channel_id=1, source_target_pairs={{0,2},{1,3},{2,0},{3,1},{4,5},{5,4},{6,7},{7,6},{8,10},{9,11},{10,... | collective-permute-start | bytes 221192 | tf_op jit(solution)/shard_map/ppermute | solution.py:290
  11.6 0.0 collective-permute-start.2
  11.6 3.1 %shard_map.87.spread = f32[12,24,64,128]{3,2,1,0:T(8,128)S(1)} custom-call(f32[12,24,64]{2,1,0:T(8,128)S(1)} %get-tuple-element.32.scale_rows), custom_call_target="tpu_custom_call" | custom-call | tf_op jit(solution)/shard_map/pallas_call | solution.py:328
  14.7 0.0 collective-permute-done.refs_1_
  14.7 1.8 %collective-permute-done.1.refs_2_ = f32[16,1152]{1,0:T(8,128)S(1)} collective-permute-done((f32[16,1152]{1,0:T(8,128)S(1)}, f32[16,1152]{1,0:T(8,128)S(1)}, u32[]{:S(2)}, u32[]{:S(2)}) %collective-permute-start.1) | collective-permute-done | bytes 73760 | tf_op jit(solution)/shard_map/ppermute | solution.py:290
  16.5 1.3 %collective-permute-done.2.refs_3_ = f32[16,1152]{1,0:T(8,128)S(1)} collective-permute-done((f32[16,1152]{1,0:T(8,128)S(1)}, f32[16,1152]{1,0:T(8,128)S(1)}, u32[]{:S(2)}, u32[]{:S(2)}) %collective-permute-start.2) | collective-permute-done | bytes 73760 | tf_op jit(solution)/shard_map/ppermute | solution.py:290
  17.9 2.0 %collective-permute-start.6 = (f32[16,1024]{1,0:T(8,128)S(1)}, f32[16,1024]{1,0:T(8,128)S(1)}, u32[]{:S(2)}, u32[]{:S(2)}) collective-permute-start(f32[16,1024]{1,0:T(8,128)S(1)} %get-tuple-element.40.refs_0_), channel_id=1, source_target_pairs={{0,3},{1,2},{2,1},{3,0},{4,7},{5,6},{6,5},{7,4},{8,11},{9,10},{10,... | collective-permute-start | bytes 196616 | tf_op jit(solution)/shard_map/ppermute | solution.py:245
  19.9 0.3 collective-permute-start.5
  20.2 2.1 %collective-permute-start.4 = (f32[16,1024]{1,0:T(8,128)S(1)}, f32[16,1024]{1,0:T(8,128)S(1)}, u32[]{:S(2)}, u32[]{:S(2)}) collective-permute-start(f32[16,1024]{1,0:T(8,128)S(1)} %get-tuple-element.40.refs_0_), channel_id=1, source_target_pairs={{0,1},{1,0},{2,3},{3,2},{4,5},{5,4},{6,7},{7,6},{8,9},{9,8},{10,11... | collective-permute-start | bytes 196616 | tf_op jit(solution)/shard_map/ppermute | solution.py:245
  22.4 0.0 collective-permute-start.3
  22.4 1.2 %collective-permute-done.3.other = f32[16,128]{1,0:T(8,128)S(1)} collective-permute-done((f32[16,128]{1,0:T(8,128)S(1)}, f32[16,128]{1,0:T(8,128)S(1)}, u32[]{:S(2)}, u32[]{:S(2)}) %collective-permute-start.3) | collective-permute-done | bytes 8224 | tf_op jit(solution)/shard_map/ppermute | solution.py:245
  23.5 1.5 %shard_map.89.gram_inverse = f32[64,64]{1,0:T(8,128)S(1)} custom-call(f32[16,128]{1,0:T(8,128)S(1)} %get-tuple-element.38.mine, f32[16,128]{1,0:T(8,128)S(1)} %collective-permute-done.3.other, f32[64,64]{1,0:T(8,128)S(1)} %get-tuple-element.39.hour_gram), custom_call_target="tpu_custom_call" | custom-call | tf_op jit(solution)/shard_map/pallas_call | solution.py:340
  25.1 0.0 collective-permute-done.6.refs_3_
  25.1 0.6 %collective-permute-done.5.refs_2_ = f32[16,1024]{1,0:T(8,128)S(1)} collective-permute-done((f32[16,1024]{1,0:T(8,128)S(1)}, f32[16,1024]{1,0:T(8,128)S(1)}, u32[]{:S(2)}, u32[]{:S(2)}) %collective-permute-start.5) | collective-permute-done | bytes 65568 | tf_op jit(solution)/shard_map/ppermute | solution.py:245
  25.6 0.0 collective-permute-done.4.refs_1_
  25.7 2.5 %shard_map.90 = (f32[64,1024]{1,0:T(8,128)}, f32[32,1152]{1,0:T(8,128)S(1)}, f32[32,1024]{1,0:T(8,128)S(1)}, f32[32,1152]{1,0:T(8,128)S(1)}, f32[32,1024]{1,0:T(8,128)S(1)}) custom-call(s32[1,1,12]{2,1,0:T(1,128)S(4)} %get-tuple-element.25.anchors_s, s32[1,1,12]{2,1,0:T(1,128)S(4)} %get-tuple-element.26.dests_s, ...), custom_call_target="tpu_custom_call" | custom-call | tf_op jit(solution)/shard_map/pallas_call | solution.py:349
  28.2 0.1 collective-permute-start.7
  28.2 0.5 %collective-permute-start.9 = (f32[32,1024]{1,0:T(8,128)S(1)}, f32[32,1024]{1,0:T(8,128)S(1)}, u32[]{:S(2)}, u32[]{:S(2)}) collective-permute-start(f32[32,1024]{1,0:T(8,128)S(1)} %get-tuple-element.46), channel_id=1, source_target_pairs={{0,4},{4,0},{8,12},{12,8},{1,5},{5,1},{9,13},{13,9},{2,6},{6,2},{1... | collective-permute-start | bytes 393224 | tf_op jit(solution)/shard_map/ppermute | solution.py:245
  28.7 0.9 %collective-permute-done.7 = f32[32,1152]{1,0:T(8,128)S(1)} collective-permute-done((f32[32,1152]{1,0:T(8,128)S(1)}, f32[32,1152]{1,0:T(8,128)S(1)}, u32[]{:S(2)}, u32[]{:S(2)}) %collective-permute-start.7) | collective-permute-done | bytes 147488 | tf_op jit(solution)/shard_map/ppermute | solution.py:245
  29.6 1.5 %collective-permute-start.8 = (f32[32,1152]{1,0:T(8,128)S(1)}, f32[32,1152]{1,0:T(8,128)S(1)}, u32[]{:S(2)}, u32[]{:S(2)}) collective-permute-start(f32[32,1152]{1,0:T(8,128)S(1)} %add.9.mine), channel_id=1, source_target_pairs={{0,8},{4,12},{8,0},{12,4},{1,9},{5,13},{9,1},{13,5},{2,10},{6,14},... | collective-permute-start | bytes 442376 | tf_op jit(solution)/shard_map/ppermute | solution.py:245
  31.2 0.0 collective-permute-done.9
  31.2 0.6 %collective-permute-start.10 = (f32[32,1024]{1,0:T(8,128)S(1)}, f32[32,1024]{1,0:T(8,128)S(1)}, u32[]{:S(2)}, u32[]{:S(2)}) collective-permute-start(f32[32,1024]{1,0:T(8,128)S(1)} %add.10), channel_id=1, source_target_pairs={{0,8},{4,12},{8,0},{12,4},{1,9},{5,13},{9,1},{13,5},{2,10},{6,14},... | collective-permute-start | bytes 393224 | tf_op jit(solution)/shard_map/ppermute | solution.py:245
  31.8 4.6 %collective-permute-done.8.other = f32[32,1152]{1,0:T(8,128)S(1)} collective-permute-done((f32[32,1152]{1,0:T(8,128)S(1)}, f32[32,1152]{1,0:T(8,128)S(1)}, u32[]{:S(2)}, u32[]{:S(2)}) %collective-permute-start.8) | collective-permute-done | bytes 147488 | tf_op jit(solution)/shard_map/ppermute | solution.py:245
  36.4 1.6 %shard_map.91 = (f32[32,1024]{1,0:T(8,128)S(1)}, f32[64,64]{1,0:T(8,128)S(1)}) custom-call(f32[32,1152]{1,0:T(8,128)S(1)} %add.9.mine, f32[32,1152]{1,0:T(8,128)S(1)} %collective-permute-done.8.other, f32[64,64]{1,0:T(8,128)S(1)} %get-tuple-element.39.hour_gram), custom_call_target="tpu_custom_call" | custom-call | tf_op jit(solution)/shard_map/pallas_call | solution.py:371
  38.0 0.1 collective-permute-start.12
  38.1 0.3 collective-permute-done.10
  38.4 0.3 collective-permute-start.11
  38.7 0.7 %collective-permute-done.12.other = f32[32,1024]{1,0:T(8,128)S(1)} collective-permute-done((f32[32,1024]{1,0:T(8,128)S(1)}, f32[32,1024]{1,0:T(8,128)S(1)}, u32[]{:S(2)}, u32[]{:S(2)}) %collective-permute-start.12) | collective-permute-done | bytes 131104 | tf_op jit(solution)/shard_map/ppermute | solution.py:245
  39.4 0.2 shard_map.92.ready
  39.7 0.2 collective-permute-done.11.other
  39.8 1.0 %shard_map.93 = f32[64,2048]{1,0:T(8,128)} custom-call(f32[64,64]{1,0:T(8,128)S(1)} %get-tuple-element.44.gram_inverse, f32[32,1024]{1,0:T(8,128)S(1)} %add.11.mine, f32[32,1024]{1,0:T(8,128)S(1)} %collective-permute-done.11.other, f32[2,64,512]{2,1,0:T(8,128)S(1)} %shard_map.92.ready), custom_call_target="tpu_custom_call" | custom-call | tf_op jit(solution)/shard_map/pallas_call | solution.py:381
  (4 shorter events, 0.1 us)
Async XLA Ops:
  5.9 8.8 %collective-permute-start = (f32[16,1152]{1,0:T(8,128)S(1)}, f32[16,1152]{1,0:T(8,128)S(1)}, u32[]{:S(2)}, u32[]{:S(2)}) collective-permute-start(f32[16,1152]{1,0:T(8,128)S(1)} %get-tuple-element.29), channel_id=1, source_target_pairs={{0,1},{1,0},{2,3},{3,2},{4,6},{5,7},{6,4},{7,5},{8,9},{9,8},{10,11... | collective-permute-start | bytes 221192 | tf_op jit(solution)/shard_map/ppermute | solution.py:290
  9.0 7.5 %collective-permute-start.1 = (f32[16,1152]{1,0:T(8,128)S(1)}, f32[16,1152]{1,0:T(8,128)S(1)}, u32[]{:S(2)}, u32[]{:S(2)}) collective-permute-start(f32[16,1152]{1,0:T(8,128)S(1)} %get-tuple-element.30), channel_id=1, source_target_pairs={{0,2},{1,3},{2,0},{3,1},{4,5},{5,4},{6,7},{7,6},{8,10},{9,11},{10,... | collective-permute-start | bytes 221192 | tf_op jit(solution)/shard_map/ppermute | solution.py:290
  11.6 6.3 %collective-permute-start.2 = (f32[16,1152]{1,0:T(8,128)S(1)}, f32[16,1152]{1,0:T(8,128)S(1)}, u32[]{:S(2)}, u32[]{:S(2)}) collective-permute-start(f32[16,1152]{1,0:T(8,128)S(1)} %get-tuple-element.31), channel_id=1, source_target_pairs={{0,3},{1,2},{2,1},{3,0},{4,7},{5,6},{6,5},{7,4},{8,11},{9,10},{10,... | collective-permute-start | bytes 221192 | tf_op jit(solution)/shard_map/ppermute | solution.py:290
  17.9 7.2 %collective-permute-start.6 = (f32[16,1024]{1,0:T(8,128)S(1)}, f32[16,1024]{1,0:T(8,128)S(1)}, u32[]{:S(2)}, u32[]{:S(2)}) collective-permute-start(f32[16,1024]{1,0:T(8,128)S(1)} %get-tuple-element.40.refs_0_), channel_id=1, source_target_pairs={{0,3},{1,2},{2,1},{3,0},{4,7},{5,6},{6,5},{7,4},{8,11},{9,10},{10,... | collective-permute-start | bytes 196616 | tf_op jit(solution)/shard_map/ppermute | solution.py:245
  19.9 5.7 %collective-permute-start.5 = (f32[16,1024]{1,0:T(8,128)S(1)}, f32[16,1024]{1,0:T(8,128)S(1)}, u32[]{:S(2)}, u32[]{:S(2)}) collective-permute-start(f32[16,1024]{1,0:T(8,128)S(1)} %get-tuple-element.40.refs_0_), channel_id=1, source_target_pairs={{0,2},{1,3},{2,0},{3,1},{4,6},{5,7},{6,4},{7,5},{8,10},{9,11},{10,... | collective-permute-start | bytes 196616 | tf_op jit(solution)/shard_map/ppermute | solution.py:245
  20.2 5.4 %collective-permute-start.4 = (f32[16,1024]{1,0:T(8,128)S(1)}, f32[16,1024]{1,0:T(8,128)S(1)}, u32[]{:S(2)}, u32[]{:S(2)}) collective-permute-start(f32[16,1024]{1,0:T(8,128)S(1)} %get-tuple-element.40.refs_0_), channel_id=1, source_target_pairs={{0,1},{1,0},{2,3},{3,2},{4,5},{5,4},{6,7},{7,6},{8,9},{9,8},{10,11... | collective-permute-start | bytes 196616 | tf_op jit(solution)/shard_map/ppermute | solution.py:245
  22.4 1.2 %collective-permute-start.3 = (f32[16,128]{1,0:T(8,128)S(1)}, f32[16,128]{1,0:T(8,128)S(1)}, u32[]{:S(2)}, u32[]{:S(2)}) collective-permute-start(f32[16,128]{1,0:T(8,128)S(1)} %get-tuple-element.38.mine), channel_id=1, source_target_pairs={{0,4},{4,0},{8,12},{12,8},{1,5},{5,1},{9,13},{13,9},{2,6},{6,2},{1... | collective-permute-start | bytes 24584 | tf_op jit(solution)/shard_map/ppermute | solution.py:245
  28.2 1.4 %collective-permute-start.7 = (f32[32,1152]{1,0:T(8,128)S(1)}, f32[32,1152]{1,0:T(8,128)S(1)}, u32[]{:S(2)}, u32[]{:S(2)}) collective-permute-start(f32[32,1152]{1,0:T(8,128)S(1)} %get-tuple-element.43), channel_id=1, source_target_pairs={{0,4},{4,0},{8,12},{12,8},{1,5},{5,1},{9,13},{13,9},{2,6},{6,2},{1... | collective-permute-start | bytes 442376 | tf_op jit(solution)/shard_map/ppermute | solution.py:245
  28.2 2.9 %collective-permute-start.9 = (f32[32,1024]{1,0:T(8,128)S(1)}, f32[32,1024]{1,0:T(8,128)S(1)}, u32[]{:S(2)}, u32[]{:S(2)}) collective-permute-start(f32[32,1024]{1,0:T(8,128)S(1)} %get-tuple-element.46), channel_id=1, source_target_pairs={{0,4},{4,0},{8,12},{12,8},{1,5},{5,1},{9,13},{13,9},{2,6},{6,2},{1... | collective-permute-start | bytes 393224 | tf_op jit(solution)/shard_map/ppermute | solution.py:245
  29.6 6.8 %collective-permute-start.8 = (f32[32,1152]{1,0:T(8,128)S(1)}, f32[32,1152]{1,0:T(8,128)S(1)}, u32[]{:S(2)}, u32[]{:S(2)}) collective-permute-start(f32[32,1152]{1,0:T(8,128)S(1)} %add.9.mine), channel_id=1, source_target_pairs={{0,8},{4,12},{8,0},{12,4},{1,9},{5,13},{9,1},{13,5},{2,10},{6,14},... | collective-permute-start | bytes 442376 | tf_op jit(solution)/shard_map/ppermute | solution.py:245
  31.2 7.2 %collective-permute-start.10 = (f32[32,1024]{1,0:T(8,128)S(1)}, f32[32,1024]{1,0:T(8,128)S(1)}, u32[]{:S(2)}, u32[]{:S(2)}) collective-permute-start(f32[32,1024]{1,0:T(8,128)S(1)} %add.10), channel_id=1, source_target_pairs={{0,8},{4,12},{8,0},{12,4},{1,9},{5,13},{9,1},{13,5},{2,10},{6,14},... | collective-permute-start | bytes 393224 | tf_op jit(solution)/shard_map/ppermute | solution.py:245
  38.0 1.4 %collective-permute-start.12 = (f32[32,1024]{1,0:T(8,128)S(1)}, f32[32,1024]{1,0:T(8,128)S(1)}, u32[]{:S(2)}, u32[]{:S(2)}) collective-permute-start(f32[32,1024]{1,0:T(8,128)S(1)} %get-tuple-element.47.mine), channel_id=1, source_target_pairs={{0,4},{4,0},{8,12},{12,8},{1,5},{5,1},{9,13},{13,9},{2,6},{6,2},{1... | collective-permute-start | bytes 393224 | tf_op jit(solution)/shard_map/ppermute | solution.py:245
  38.4 1.4 %collective-permute-start.11 = (f32[32,1024]{1,0:T(8,128)S(1)}, f32[32,1024]{1,0:T(8,128)S(1)}, u32[]{:S(2)}, u32[]{:S(2)}) collective-permute-start(f32[32,1024]{1,0:T(8,128)S(1)} %add.11.mine), channel_id=1, source_target_pairs={{0,4},{4,0},{8,12},{12,8},{1,5},{5,1},{9,13},{13,9},{2,6},{6,2},{1... | collective-permute-start | bytes 393224 | tf_op jit(solution)/shard_map/ppermute | solution.py:245
